TPU v7x, 256 devices: a whole 4x4x8 slice. The times are simulated.
256 devices in a mesh: pipe: 16 (over y, x), dp: 16 (over z, core).
Axes of the slice: x: 4, y: 4, z: 8, core: 2. Of those that a mesh axis runs over, the one named last changes fastest.
Arguments:
- inputs: bfloat16 [16, 128, 8192], P('pipe', 'dp'), may hold values from -6 to 6
- cotangent: bfloat16 [16, 128, 8192], P('pipe', 'dp'), may hold values from -6 to 6
- norm_gain: float32 [16, 8192], P('pipe'), may hold values from 0.1 to 1.9
- w_value: bfloat16 [16, 64, 8192], P('pipe'), may hold values from -0.0625 to 0.0625
- w_out: bfloat16 [16, 64, 8192], P('pipe'), may hold values from -0.75 to 0.75
- value_down: bfloat16 [16, 16, 16, 8192], P('pipe', 'dp'), may hold values from -0.0625 to 0.0625
- value_up_factor: bfloat16 [16, 16, 16, 64], P('pipe', 'dp'), may hold values from -1.5 to 1.5
- out_down: bfloat16 [16, 16, 16, 64], P('pipe', 'dp'), may hold values from -0.75 to 0.75
- output_up_factor: bfloat16 [16, 16, 16, 8192], P('pipe', 'dp'), may hold values from -1.5 to 1.5
- block_tenant: int32 [16], replicated, may hold values from 0 to 15
- valid_tokens: int32 [16], replicated, may hold values from 1 to 128, 1536 in all
- tenant_slot: int32 [16], replicated, may hold values from 0 to 15, each once
Outputs:
- grad_value_down: bfloat16 [16, 16, 16, 8192], P('pipe', 'dp')
- grad_value_up: bfloat16 [16, 16, 16, 64], P('pipe', 'dp')
- grad_out_down: bfloat16 [16, 16, 16, 64], P('pipe', 'dp')
- grad_out_up: bfloat16 [16, 16, 16, 8192], P('pipe', 'dp')
Inputs may be any that keep to these rules, and one draw needn't show every extreme that they name: `block_tenant`: tenant whose adapters serve all 128 tokens of a dp index. The first valid_tokens[i] block positions of dp index i are valid, the rest padding. A permutation: the adapters and gradients of tenant t sit at slot tenant_slot[t], stored on dp index tenant_slot[t].
All inputs are finite; a program needn't handle non-finite values.
Results may differ from a plain program's by a relative error of at most 0.034.
Values may be sent and summed in bfloat16 or wider, within the bound.
No kernel may reach another device: no remote copies, remote signals or barrier semaphores. Data moves between devices by JAX's collectives and lax.ppermute only.
A program may use at most 64 MiB of HBM per device.

v0:
```python
import jax
import jax.numpy as jnp
from jax import lax
from jax.sharding import PartitionSpec as P

adapter_scale = 2.0
norm_eps = 1e-05


def from_behind(value, axis, by):
    peers = lax.axis_size(axis)
    return lax.ppermute(value, axis, [(i, (i + by) % peers) for i in range(peers)])


def normalize(token_rows, gain_row):
    wide_rows = token_rows.astype(jnp.float32)
    inverse = lax.rsqrt(jnp.mean(wide_rows * wide_rows, axis=-1, keepdims=True) + norm_eps)
    return ((wide_rows * inverse * gain_row).astype(jnp.bfloat16), inverse)


def contract_trailing(left, right):
    return lax.dot_general(
        left, right, (((1,), (1,)), ((), ())), preferred_element_type=jnp.float32
    )


def contract_leading(left, right):
    return lax.dot_general(
        left, right, (((0,), (0,)), ((), ())), preferred_element_type=jnp.float32
    )


def section_parts(token_rows, gain_row, value_weight, tenant_adapters):
    value_down, value_up_factor, out_down, output_up_factor = tenant_adapters
    normalized_rows, inverse = normalize(token_rows, gain_row)
    lowrank_product = contract_trailing(normalized_rows, value_down).astype(jnp.bfloat16)
    value_blend = contract_trailing(normalized_rows, value_weight)
    value_blend = value_blend + adapter_scale * jnp.dot(
        lowrank_product, value_up_factor, preferred_element_type=jnp.float32
    )
    value_row_block = value_blend.astype(jnp.bfloat16)
    sidepath_rank = contract_trailing(value_row_block, out_down).astype(jnp.bfloat16)
    return (normalized_rows, inverse, lowrank_product, value_row_block, sidepath_rank)


def section_output(token_rows, layer_pieces, out_weight, tenant_adapters):
    blended_rows = token_rows.astype(jnp.float32) + jnp.dot(
        layer_pieces[3], out_weight, preferred_element_type=jnp.float32
    )
    blended_rows = blended_rows + adapter_scale * jnp.dot(
        layer_pieces[4], tenant_adapters[3], preferred_element_type=jnp.float32
    )
    return blended_rows.astype(jnp.bfloat16)


def section_backward(
    token_rows, input_gradient, layer_pieces, gain_row, value_weight, out_weight, tenant_adapters
):
    value_down, value_up_factor, out_down, output_up_factor = tenant_adapters
    normalized_rows, inverse, lowrank_product, value_row_block, sidepath_rank = layer_pieces
    sidepath_gradient = (
        adapter_scale * contract_trailing(input_gradient, output_up_factor)
    ).astype(jnp.bfloat16)
    value_gradient = contract_trailing(input_gradient, out_weight)
    value_gradient = (
        value_gradient + jnp.dot(sidepath_gradient, out_down, preferred_element_type=jnp.float32)
    ).astype(jnp.bfloat16)
    lowrank_gradient = (adapter_scale * contract_trailing(value_gradient, value_up_factor)).astype(
        jnp.bfloat16
    )
    grad_normed = jnp.dot(
        value_gradient, value_weight, preferred_element_type=jnp.float32
    ) + jnp.dot(lowrank_gradient, value_down, preferred_element_type=jnp.float32)
    scaled = grad_normed * gain_row
    wide_rows = token_rows.astype(jnp.float32)
    correction = jnp.mean(scaled * wide_rows, axis=-1, keepdims=True)
    grad_rows = inverse * scaled - wide_rows * (inverse * inverse * inverse) * correction
    grad_out = (input_gradient.astype(jnp.float32) + grad_rows).astype(jnp.bfloat16)
    gradient_pieces = (
        contract_leading(lowrank_gradient, normalized_rows),
        adapter_scale * contract_leading(lowrank_product, value_gradient),
        contract_leading(sidepath_gradient, value_row_block),
        adapter_scale * contract_leading(sidepath_rank, input_gradient),
    )
    return (grad_out, gradient_pieces)


def pass_section(token_rows, shift_by):
    return from_behind(token_rows, "pipe", shift_by)


def owner_layout(first, second, third, fourth):
    return (
        lax.all_to_all(first, "dp", split_axis=0, concat_axis=2, tiled=True),
        lax.all_to_all(second, "dp", split_axis=0, concat_axis=2, tiled=True),
        lax.all_to_all(third, "dp", split_axis=0, concat_axis=2, tiled=True),
        lax.all_to_all(fourth, "dp", split_axis=0, concat_axis=2, tiled=True),
    )


def pick_rows(picker, sliced_part):
    flat_rows = sliced_part.reshape(sliced_part.shape[0], -1)
    chosen = jnp.dot(picker, flat_rows, preferred_element_type=jnp.float32).astype(jnp.bfloat16)
    return chosen.reshape((picker.shape[0],) + sliced_part.shape[1:])


def sum_by_slot(slot_float, gathered_part):
    flat_rows = gathered_part.reshape(gathered_part.shape[0], -1)
    summed = lax.dot_general(
        slot_float,
        flat_rows,
        (((0,), (0,)), ((), ())),
        precision=lax.Precision.HIGHEST,
        preferred_element_type=jnp.float32,
    )
    return summed.astype(jnp.bfloat16).reshape((slot_float.shape[1],) + gathered_part.shape[1:])


def put_entry(stash, entry, micro_index, active):

    def update(stored_all, new_entry):
        previous = lax.dynamic_index_in_dim(stored_all, micro_index, 0, keepdims=False)
        return lax.dynamic_update_index_in_dim(
            stored_all, jnp.where(active, new_entry, previous), micro_index, 0
        )

    return jax.tree.map(update, stash, entry)


def get_entry(stash, micro_index):
    return jax.tree.map(
        lambda stored_all: lax.dynamic_index_in_dim(stored_all, micro_index, 0, keepdims=False),
        stash,
    )


def body(
    inputs,
    cotangent,
    norm_gain,
    w_value,
    w_out,
    value_down,
    value_up_factor,
    out_down,
    output_up_factor,
    block_tenant,
    valid_tokens,
    tenant_slot,
):
    section_index = lax.axis_index("pipe")
    sections = lax.axis_size("pipe")
    member = lax.axis_index("dp")
    members = lax.axis_size("dp")
    queue_depth = inputs.shape[0]
    row_count = inputs.shape[1]
    micro_count = queue_depth * sections
    ticks = micro_count + sections - 1
    tenant_ids = jnp.arange(tenant_slot.shape[0], dtype=jnp.int32)
    tenant_hot = block_tenant[:, None] == tenant_ids[None, :]
    slot_of = jnp.sum(jnp.where(tenant_hot, tenant_slot[None, :], 0), axis=1)
    slot_hot = slot_of[:, None] == tenant_ids[None, :]
    member_hot = jnp.arange(members, dtype=jnp.int32) == member
    own_tenant = jnp.sum(jnp.where(member_hot, block_tenant, 0))
    own_valid = jnp.sum(jnp.where(member_hot, valid_tokens, 0))
    tenant_tokens = jnp.sum(jnp.where(block_tenant == own_tenant, valid_tokens, 0)).astype(
        jnp.float32
    )
    sliced = (
        lax.all_to_all(value_down[0], "dp", split_axis=2, concat_axis=0, tiled=True),
        lax.all_to_all(value_up_factor[0], "dp", split_axis=2, concat_axis=0, tiled=True),
        lax.all_to_all(out_down[0], "dp", split_axis=2, concat_axis=0, tiled=True),
        lax.all_to_all(output_up_factor[0], "dp", split_axis=2, concat_axis=0, tiled=True),
    )
    picker = slot_hot.astype(jnp.bfloat16)
    picked = [pick_rows(picker, sliced_part) for sliced_part in sliced]
    fetched = owner_layout(picked[0], picked[1], picked[2], picked[3])
    tenant_adapters = tuple((whole_part[0] for whole_part in fetched))
    gain_row = norm_gain[0]
    value_weight = w_value[0]
    out_weight = w_out[0]

    def token_weight(micro_index):
        position = micro_index * row_count + jnp.arange(row_count, dtype=jnp.int32)
        return (
            jnp.where(position < own_valid, 1.0, 0.0).astype(jnp.float32)[:, None] / tenant_tokens
        )

    def keep_entry(current):
        return (current,)

    def parts_of(entry):
        return section_parts(entry[0], gain_row, value_weight, tenant_adapters)

    blank = jnp.zeros((row_count, inputs.shape[2]), jnp.bfloat16)
    sample = keep_entry(blank)
    stash = jax.tree.map(
        lambda leaf_value: jnp.zeros((micro_count,) + leaf_value.shape, leaf_value.dtype), sample
    )
    accum = tuple((jnp.zeros(adapter_part.shape, jnp.float32) for adapter_part in tenant_adapters))

    def forward_tick(tick_index, arriving, feed_rows, stash_now, order):
        position = tick_index - section_index
        active = (position >= 0) & (position < micro_count)
        micro_index = order(jnp.clip(position, 0, micro_count - 1))
        current = jnp.where(section_index == 0, feed_rows, arriving)
        layer_pieces = section_parts(current, gain_row, value_weight, tenant_adapters)
        result = section_output(current, layer_pieces, out_weight, tenant_adapters)
        stash_now = put_entry(stash_now, keep_entry(current), micro_index, active)
        return (result, stash_now)

    def backward_tick(tick_index, arriving, feed_rows, stash_now, accum_now, order):
        position = tick_index - (sections - 1 - section_index)
        active = (position >= 0) & (position < micro_count)
        micro_index = order(jnp.clip(position, 0, micro_count - 1))
        entry = get_entry(stash_now, micro_index)
        seeded = (feed_rows.astype(jnp.float32) * token_weight(micro_index)).astype(jnp.bfloat16)
        input_gradient = jnp.where(section_index == sections - 1, seeded, arriving)
        grad_out, gradient_pieces = section_backward(
            entry[0],
            input_gradient,
            parts_of(entry),
            gain_row,
            value_weight,
            out_weight,
            tenant_adapters,
        )
        accum_now = tuple(
            (
                running + jnp.where(active, addend, 0.0)
                for running, addend in zip(accum_now, gradient_pieces)
            )
        )
        return (grad_out, accum_now)

    all_inputs, all_cotangents = (
        lax.all_gather(inputs, "pipe", axis=0, tiled=True),
        lax.all_gather(cotangent, "pipe", axis=0, tiled=True),
    )

    def plain_order(position):
        return position

    def forward_step(tick_index, carry):
        arriving, stash_now = carry
        feed_rows = lax.dynamic_index_in_dim(
            all_inputs, jnp.minimum(tick_index, micro_count - 1), 0, keepdims=False
        )
        result, stash_now = forward_tick(tick_index, arriving, feed_rows, stash_now, plain_order)
        return (pass_section(result, 1), stash_now)

    arriving, stash = lax.fori_loop(0, ticks, forward_step, (blank, stash))

    def backward_step(tick_index, carry):
        arriving, accum_now = carry
        feed_rows = lax.dynamic_index_in_dim(
            all_cotangents, jnp.minimum(tick_index, micro_count - 1), 0, keepdims=False
        )
        grad_out, accum_now = backward_tick(
            tick_index, arriving, feed_rows, stash, accum_now, plain_order
        )
        return (pass_section(grad_out, sections - 1), accum_now)

    arriving, accum = lax.fori_loop(0, ticks, backward_step, (blank, accum))
    spread = (
        lax.all_to_all(
            accum[0][None].astype(jnp.bfloat16), "dp", split_axis=2, concat_axis=0, tiled=True
        ).astype(jnp.float32),
        lax.all_to_all(
            accum[1][None].astype(jnp.bfloat16), "dp", split_axis=2, concat_axis=0, tiled=True
        ).astype(jnp.float32),
        lax.all_to_all(
            accum[2][None].astype(jnp.bfloat16), "dp", split_axis=2, concat_axis=0, tiled=True
        ).astype(jnp.float32),
        lax.all_to_all(
            accum[3][None].astype(jnp.bfloat16), "dp", split_axis=2, concat_axis=0, tiled=True
        ).astype(jnp.float32),
    )
    slot_float = slot_hot.astype(jnp.float32)
    totals = [sum_by_slot(slot_float, gathered_part) for gathered_part in spread]
    owned = owner_layout(totals[0], totals[1], totals[2], totals[3])
    return (owned[0][None], owned[1][None], owned[2][None], owned[3][None])


def solution(mesh):
    return jax.shard_map(
        body,
        mesh=mesh,
        in_specs=(
            P("pipe", "dp", None),
            P("pipe", "dp", None),
            P("pipe", None),
            P("pipe", None, None),
            P("pipe", None, None),
            P("pipe", "dp", None, None),
            P("pipe", "dp", None, None),
            P("pipe", "dp", None, None),
            P("pipe", "dp", None, None),
            P(),
            P(),
            P(),
        ),
        out_specs=(
            P("pipe", "dp", None, None),
            P("pipe", "dp", None, None),
            P("pipe", "dp", None, None),
            P("pipe", "dp", None, None),
        ),
        check_vma=False,
    )
```

profile of v0, /device:TPU:1, one launch (start us, length us, event | category | flops | bytes accessed | tf_op | source)
XLA Modules:
  0.0 1314.0 jit_solution(12247208075223459638)
XLA Ops:
  9.3 10.0 all-to-all-start.2
  52.6 8.3 copy.184
  61.5 45.2 %reduce.1 = bf16[8192,16]{1,0:T(8,128)(2,1)S(1)} reduce(bf16[8192,1,16]{2,1,0:T(2,128)(2,1)} %bitcast.325, bf16[]{:T(256)} %broadcast.230), dimensions={1}, to_apply=%bitcast.160.reduce_sub_computation | reduce | bytes 524290
  109.6 7.6 all-to-all-start.6
  123.9 45.2 %reduce = bf16[8192,16]{1,0:T(8,128)(2,1)S(1)} reduce(bf16[8192,1,16]{2,1,0:T(2,128)(2,1)} %bitcast.332, bf16[]{:T(256)} %broadcast.230), dimensions={1}, to_apply=%bitcast.158.reduce_sub_computation | reduce | bytes 524290
  186.8 7.9 copy.185
  203.2 7.6 reshape.150
  210.8 7.9 copy.173
  230.8 8.1 all-to-all-done.1
  240.6 362.3 %while.40 = (s32[]{:T(128)}, bf16[8,8192]{1,0:T(8,128)(2,1)S(1)}, bf16[16,8,8192]{2,1,0:T(8,128)(2,1)}, pred[]{:T(512)}, bf16[16,8,8192]{2,1,0:T(8,128)(2,1)}, /...) while((s32[]{:T(128)}, bf16[8,8192]{1,0:T(8,128)(2,1)S(1)}, ...), condition=%wide.region_3.4_spmd, body=%wide.region_1.3_spmd.sunk | while | flops 22185748 | bytes 5320665 | solution.py:252
  246.0 8.7 collective-permute-done
  258.9 8.0 collective-permute-done
  271.0 9.8 collective-permute-done
  375.9 8.8 collective-permute-done
  388.9 8.0 collective-permute-done
  503.1 8.1 collective-permute-done
  515.4 8.1 collective-permute-done
  602.9 425.5 %while.41 = (s32[]{:T(128)}, bf16[8,8192]{1,0:T(8,128)(2,1)S(1)}, f32[16,8192]{1,0:T(8,128)}, f32[16,64]{1,0:T(8,128)S(1)}, f32[16,64]{1,0:T(8,128)S(1)}, /*inde...) while((s32[]{:T(128)}, bf16[8,8192]{1,0:T(8,128)(2,1)S(1)}, ...), condition=%wide.region_10.11_spmd.clone, body=%wide.region_7.10_spmd.clone.sunk | while | flops 38709568 | bytes 13674686 | solution.py:264
  1029.1 57.9 %all-to-all-start.10 = ((bf16[1,16,64]{1,0,2:T(2,128)(2,1)}), bf16[1,16,64]{1,0,2:T(2,128)(2,1)S(1)}, u32[]{:S(2)}, u32[]{:S(2)}) async-start(bf16[1,16,64]{1,0,2:T(2,128)(2,1)} %copy.196), calls=%async_computation.10 | async-start | bytes 65536 | tf_op jit(solution)/shard_map/all_to_all | solution.py:269
  1128.6 45.2 %reduce.3 = bf16[8192,16]{1,0:T(8,128)(2,1)S(1)} reduce(bf16[8192,1,16]{2,1,0:T(2,128)(2,1)} %bitcast.329, bf16[]{:T(256)} %broadcast.230), dimensions={1}, to_apply=%bitcast.164.reduce_sub_computation | reduce | bytes 524290
  1191.0 45.2 %reduce.2 = bf16[8192,16]{1,0:T(8,128)(2,1)S(1)} reduce(bf16[8192,1,16]{2,1,0:T(2,128)(2,1)} %bitcast.326, bf16[]{:T(256)} %broadcast.230), dimensions={1}, to_apply=%bitcast.162.reduce_sub_computation | reduce | bytes 524290
  1253.9 7.9 copy.205
  1277.9 7.9 copy.193
  1296.6 9.4 all-to-all-done.9
  (1139 shorter events, 915.9 us)
Async XLA Ops:
  7.2 231.8 %all-gather.5.cloned.1.call-start = ((), (), s32[]{:S(2)}) async-start(), calls=%async_computation.17 | async-start | bytes 2228224 | tf_op jit(solution)/shard_map/all_gather | solution.py:237
  9.3 17.4 %all-to-all-start.2 = ((bf16[1,16,64]{1,0,2:T(2,128)(2,1)}), bf16[1,16,64]{1,0,2:T(2,128)(2,1)S(1)}, u32[]{:S(2)}, u32[]{:S(2)}) async-start(bf16[1,16,64]{1,0,2:T(2,128)(2,1)} %copy.176), calls=%async_computation.2 | async-start | bytes 65536 | tf_op jit(solution)/shard_map/all_to_all | solution.py:171
  26.7 11.2 all-to-all-start.4
  37.8 11.1 all-to-all-start.3
  48.9 60.6 %all-to-all-start.5 = ((bf16[16,16,4]{1,2,0:T(4,128)(2,1)}), bf16[16,16,4]{1,2,0:T(4,128)(2,1)S(1)}, u32[]{:S(2)}, u32[]{:S(2)}) async-start(bf16[16,16,4]{1,2,0:T(4,128)(2,1)} %copy.183), calls=%async_computation.5 | async-start | bytes 32768 | tf_op jit(solution)/shard_map/all_to_all | solution.py:96
  109.6 62.4 %all-to-all-start.6 = ((bf16[16,2,4096]{2,1,0:T(2,128)(2,1)}), bf16[16,2,4096]{2,1,0:T(2,128)(2,1)S(1)}, u32[]{:S(2)}, u32[]{:S(2)}) async-start(bf16[16,2,4096]{2,1,0:T(2,128)(2,1)} %reshape.151), calls=%async_computation.6 | async-start | bytes 524288 | tf_op jit(solution)/shard_map/all_to_all | solution.py:173
  172.0 23.9 %all-to-all-start = ((bf16[16,2,4096]{2,1,0:T(2,128)(2,1)}), bf16[16,2,4096]{2,1,0:T(2,128)(2,1)S(1)}, u32[]{:S(2)}, u32[]{:S(2)}) async-start(bf16[16,2,4096]{2,1,0:T(2,128)(2,1)} %reshape.149), calls=%async_computation | async-start | bytes 524288 | tf_op jit(solution)/shard_map/all_to_all | solution.py:170
  195.9 24.0 %all-to-all-start.7 = ((bf16[16,16,512]{2,1,0:T(8,128)(2,1)}), bf16[16,16,512]{2,1,0:T(8,128)(2,1)S(1)}, u32[]{:S(2)}, u32[]{:S(2)}) async-start(bf16[16,16,512]{2,1,0:T(8,128)(2,1)} %bitcast.97), calls=%async_computation.7 | async-start | bytes 524288 | tf_op jit(solution)/shard_map/all_to_all | solution.py:97
  219.9 19.1 %all-to-all-start.1 = ((bf16[16,16,512]{2,1,0:T(8,128)(2,1)}), bf16[16,16,512]{2,1,0:T(8,128)(2,1)S(1)}, u32[]{:S(2)}, u32[]{:S(2)}) async-start(bf16[16,16,512]{2,1,0:T(8,128)(2,1)} %bitcast.84), calls=%async_computation.1 | async-start | bytes 524288 | tf_op jit(solution)/shard_map/all_to_all | solution.py:94
  227.2 375.6 %all-gather.3.cloned.1.call-start = ((), (), s32[]{:S(2)}) async-start(), calls=%async_computation.16 | async-start | bytes 2228224 | tf_op jit(solution)/shard_map/all_gather | solution.py:238
  244.7 10.0 collective-permute-start
  271.0 9.9 collective-permute-start
  375.8 8.9 collective-permute-start
  794.4 11.3 collective-permute-start.1
  812.0 11.3 collective-permute-start.1
  1016.5 11.3 collective-permute-start.1
  1029.1 65.4 %all-to-all-start.10 = ((bf16[1,16,64]{1,0,2:T(2,128)(2,1)}), bf16[1,16,64]{1,0,2:T(2,128)(2,1)S(1)}, u32[]{:S(2)}, u32[]{:S(2)}) async-start(bf16[1,16,64]{1,0,2:T(2,128)(2,1)} %copy.196), calls=%async_computation.10 | async-start | bytes 65536 | tf_op jit(solution)/shard_map/all_to_all | solution.py:269
  1094.5 11.2 all-to-all-start.12
  1105.6 11.1 all-to-all-start.11
  1116.7 60.0 %all-to-all-start.13 = ((bf16[16,16,4]{1,2,0:T(4,128)(2,1)}), bf16[16,16,4]{1,2,0:T(4,128)(2,1)S(1)}, u32[]{:S(2)}, u32[]{:S(2)}) async-start(bf16[16,16,4]{1,2,0:T(4,128)(2,1)} %copy.203), calls=%async_computation.13 | async-start | bytes 32768 | tf_op jit(solution)/shard_map/all_to_all | solution.py:96
  1176.7 62.4 %all-to-all-start.14 = ((bf16[16,2,4096]{2,1,0:T(2,128)(2,1)}), bf16[16,2,4096]{2,1,0:T(2,128)(2,1)S(1)}, u32[]{:S(2)}, u32[]{:S(2)}) async-start(bf16[16,2,4096]{2,1,0:T(2,128)(2,1)} %reshape.155), calls=%async_computation.14 | async-start | bytes 524288 | tf_op jit(solution)/shard_map/all_to_all | solution.py:275
  1239.0 24.0 %all-to-all-start.8 = ((bf16[16,2,4096]{2,1,0:T(2,128)(2,1)}), bf16[16,2,4096]{2,1,0:T(2,128)(2,1)S(1)}, u32[]{:S(2)}, u32[]{:S(2)}) async-start(bf16[16,2,4096]{2,1,0:T(2,128)(2,1)} %reshape.153), calls=%async_computation.8 | async-start | bytes 524288 | tf_op jit(solution)/shard_map/all_to_all | solution.py:266
  1263.1 24.0 %all-to-all-start.15 = ((bf16[16,16,512]{2,1,0:T(8,128)(2,1)}), bf16[16,16,512]{2,1,0:T(8,128)(2,1)S(1)}, u32[]{:S(2)}, u32[]{:S(2)}) async-start(bf16[16,16,512]{2,1,0:T(8,128)(2,1)} %bitcast.121), calls=%async_computation.15 | async-start | bytes 524288 | tf_op jit(solution)/shard_map/all_to_all | solution.py:97
  1287.0 18.9 %all-to-all-start.9 = ((bf16[16,16,512]{2,1,0:T(8,128)(2,1)}), bf16[16,16,512]{2,1,0:T(8,128)(2,1)S(1)}, u32[]{:S(2)}, u32[]{:S(2)}) async-start(bf16[16,16,512]{2,1,0:T(8,128)(2,1)} %bitcast.110), calls=%async_computation.9 | async-start | bytes 524288 | tf_op jit(solution)/shard_map/all_to_all | solution.py:94
  (124 other events, 795.5 us)
Sparse Core Ops, SparseCore 0:
  10.4 52.8 all-gather.4
  230.5 52.0 all-gather.2
where the time goes:
time: 1330 us; the launch traced here: 1310 us
  other arithmetic  345 us (26%)
  matrix products  318 us (24%)
  waiting for transfers between devices  286 us (22%)
  starting transfers between devices  182 us (14%)
  local copies, waits for them, and re-layouts  166 us (12%)
  between operations  15.3 us (1%)
    ppermute x62, waiting for transfers between devices, from_behind(): lax.ppermute(value, axis, [(i, (i + by) % peers) for i in range(peers)])  231 us
    unnamed x8, other arithmetic  181 us
    dot_general x124, matrix products, contract_leading(): lax.dot_general(left, right, (((0,), (0,)), ((), ())), preferred_element_...  118 us
    dot_general x186, matrix products, contract_trailing(): lax.dot_general(left, right, (((1,), (1,)), ((), ())), preferred_element_...  113 us
    all_to_all x1, starting transfers between devices, body(): lax.all_to_all(accum[1][None].astype(jnp.bfloat16), 'dp', split_axis=2, c...  57.9 us
    convert_element_type x31, other arithmetic, section_backward(): (input_gradient.astype(jnp.float32) + grad_rows).astype(jnp.bfloat16)  52.7 us
    dynamic_update_slice x31, other arithmetic, update(): lax.dynamic_update_index_in_dim(stored_all, jnp.where(active, new_entry,...  50.5 us
    unnamed x45, local copies, waits for them, and re-layouts  47.3 us
  transfers between devices with their start and end apart: 80, of which 39 were waited for; matrix products, arithmetic and copies ran while one was open for 48% of the time, Pallas kernels for 0%

commit v1 on v0

v1 whole, which is shorter than its diff:
```python
import functools

import jax
import jax.numpy as jnp
from jax import lax
from jax.experimental import pallas as pl
from jax.experimental.pallas import tpu as pltpu
from jax.sharding import PartitionSpec as P

adapter_scale = 2.0
norm_eps = 1e-05
block = 256
vmem_bytes = 56 * 1024 * 1024


def mm(left, right):
    return lax.dot_general(
        left, right, (((1,), (0,)), ((), ())), preferred_element_type=jnp.float32
    )


def mm_nt(left, right):
    return lax.dot_general(
        left, right, (((1,), (1,)), ((), ())), preferred_element_type=jnp.float32
    )


def mm_tn(left, right):
    return lax.dot_general(
        left, right, (((0,), (0,)), ((), ())), preferred_element_type=jnp.float32
    )


def layer_mask(rows, columns, hd, compare):
    row_layer = lax.broadcasted_iota(jnp.int32, (rows, columns), 0) // hd
    column_layer = lax.broadcasted_iota(jnp.int32, (rows, columns), 1) // hd
    return compare(row_layer, column_layer)


def gram_kernel(sizes, w_ref, x_ref, s_ref, q_ref, u_ref, v_ref, out_ref):
    layers, hd, rank, tokens, cols = sizes
    for l in range(layers):
        small = q_ref[l, :, 2 * cols : 2 * cols + 2 * hd]
        delta_v = mm_tn(small[:, :hd], q_ref[l, :, :cols])
        delta_u = mm_tn(small[:, hd:], q_ref[l, :, cols : 2 * cols])
        at = pl.ds(l * hd, hd)
        v_ref[at, :] = (w_ref[l, :hd, :].astype(jnp.float32) + adapter_scale * delta_v).astype(
            jnp.bfloat16
        )
        u_ref[at, :] = (
            w_ref[l, hd : 2 * hd, :].astype(jnp.float32) + adapter_scale * delta_u
        ).astype(jnp.bfloat16)
    width = layers * hd
    base = 3 * tokens
    below = layer_mask(block, block, hd, lambda r, c: r < c)
    for bj in range(width // block):
        at_col = pl.ds(bj * block, block)
        u_col, v_col = u_ref[at_col, :], v_ref[at_col, :]
        out_ref[:tokens, at_col] = mm_nt(x_ref[...], v_col).astype(jnp.bfloat16)
        out_ref[tokens : 2 * tokens, at_col] = mm_nt(x_ref[...], u_col).astype(jnp.bfloat16)
        out_ref[2 * tokens : 3 * tokens, at_col] = mm_nt(s_ref[...], u_col).astype(jnp.bfloat16)
        for bi in range(width // block):
            rows = u_ref[pl.ds(bi * block, block), :]
            if bi < bj:
                part = mm_nt(rows, v_col)
            elif bi > bj:
                part = mm_nt(rows, u_col)
            else:
                part = jnp.where(below, mm_nt(rows, v_col), mm_nt(rows, u_col))
            out_ref[pl.ds(base + bi * block, block), at_col] = part.astype(jnp.bfloat16)


def half(pair, l):
    hd = pair.shape[1] // 2
    return pair[:, hd:] if l % 2 else pair[:, :hd]


def solve_kernel(
    sizes,
    features,
    k_ref,
    n_ref,
    x_ref,
    s_ref,
    u_ref,
    v_ref,
    q_ref,
    out_ref,
    c_ref,
    d_ref,
    ec_ref,
    a_ref,
    bp_ref,
    inv_ref,
):
    layers, hd, rank, tokens, cols = sizes
    width = layers * hd
    base = 3 * tokens
    c_ref[...] = jnp.zeros_like(c_ref)
    d_ref[...] = jnp.zeros_like(d_ref)
    ec_ref[...] = jnp.zeros_like(ec_ref)

    def pair_of(l):
        return pl.ds(2 * hd * (l // 2), 2 * hd)

    def upto(l):
        return 2 * hd * ((l + 1) // 2)

    square = n_ref[...]
    for l in range(layers):
        pair = pair_of(l)
        rows_l = pl.ds(base + l * hd, hd)
        a = half(k_ref[:tokens, pair], l).astype(jnp.float32)
        b = half(k_ref[tokens : 2 * tokens, pair], l).astype(jnp.float32)
        if l:
            w = upto(l)
            known = c_ref[:, :w]
            a = a + half(mm(known, k_ref[base : base + w, pair]), l)
            b = b + mm_nt(known, k_ref[rows_l, :w])
        inverse = lax.rsqrt(jnp.maximum(square, 0.0) / features + norm_eps)
        c = (inverse * a).astype(jnp.bfloat16)
        wide = c.astype(jnp.float32)
        after = b + half(mm(c, k_ref[rows_l, pair]), l)
        square = square + jnp.sum(wide * (b + after), axis=1, keepdims=True)
        c_ref[:, l * hd : (l + 1) * hd] = c
        a_ref[l] = a
        bp_ref[l] = after
        inv_ref[l] = inverse

    pull = jnp.zeros_like(square)
    for l in range(layers - 1, -1, -1):
        pair = pair_of(l)
        rows_l = pl.ds(base + l * hd, hd)
        p = half(k_ref[2 * tokens : 3 * tokens, pair], l).astype(jnp.float32) - pull * bp_ref[l]
        if l < layers - 1:
            w = upto(l)
            p = p + mm_nt(d_ref[:, w:], k_ref[rows_l, w:])
            p = p - half(mm(ec_ref[:, w:], k_ref[base + w : base + width, pair]), l)
        inverse = inv_ref[l]
        d_ref[:, l * hd : (l + 1) * hd] = (inverse * p).astype(jnp.bfloat16)
        c = c_ref[:, l * hd : (l + 1) * hd].astype(jnp.float32)
        ec_ref[:, l * hd : (l + 1) * hd] = (pull * c).astype(jnp.bfloat16)
        correction = jnp.sum(p * a_ref[l], axis=1, keepdims=True) / features
        pull = pull + inverse * inverse * inverse * correction

    below = layer_mask(block, block, hd, lambda r, c: r > c)
    upto_diag = layer_mask(block, block, hd, lambda r, c: r >= c)
    blocks = width // block
    for bl in range(blocks):
        mine = pl.ds(bl * block, block)
        c_t = c_ref[:, mine].T
        d_t = d_ref[:, mine].T
        ec_t = ec_ref[:, mine].T
        y = mm(d_t, x_ref[...])
        z = mm(c_t, s_ref[...]) - mm(ec_t, x_ref[...])
        for bk in range(blocks):
            other = pl.ds(bk * block, block)
            u_k = u_ref[other, :]
            if bk <= bl:
                m = mm(d_t, c_ref[:, other])
                if bk == bl:
                    m = jnp.where(below, m, 0.0)
                y = y + mm(m.astype(jnp.bfloat16), u_k)
            if bk >= bl:
                m = mm(c_t, d_ref[:, other])
                if bk == bl:
                    m = jnp.where(upto_diag, 0.0, m)
                z = z + mm(m.astype(jnp.bfloat16), v_ref[other, :])
            if bk < bl:
                m = mm(ec_t, c_ref[:, other])
            elif bk > bl:
                m = mm(c_t, ec_ref[:, other])
            else:
                m = jnp.where(upto_diag, mm(ec_t, c_ref[:, other]), mm(c_t, ec_ref[:, other]))
            z = z - mm(m.astype(jnp.bfloat16), u_k)
        y = y.astype(jnp.bfloat16)
        z = z.astype(jnp.bfloat16)
        for j in range(block // hd):
            l = bl * (block // hd) + j
            y_l, z_l = y[j * hd : (j + 1) * hd], z[j * hd : (j + 1) * hd]
            small = q_ref[l, :, 2 * cols : 2 * cols + 2 * hd]
            out_ref[l, :, :cols] = (adapter_scale * mm(small[:, :hd], y_l)).astype(jnp.bfloat16)
            out_ref[l, :, cols : 2 * cols] = (adapter_scale * mm(small[:, hd:], z_l)).astype(
                jnp.bfloat16
            )
            tail = jnp.concatenate(
                [mm_nt(q_ref[l, :, :cols], y_l), mm_nt(q_ref[l, :, cols : 2 * cols], z_l)], axis=1
            )
            out_ref[l, :, 2 * cols :] = (adapter_scale * tail).astype(jnp.bfloat16)


def params():
    return pltpu.CompilerParams(vmem_limit_bytes=vmem_bytes)


def in_vmem(count):
    return [pl.BlockSpec(memory_space=pltpu.VMEM)] * count


def gram(sizes, w, x, s, q):
    layers, hd, rank, tokens, cols = sizes
    width = layers * hd
    return pl.pallas_call(
        functools.partial(gram_kernel, sizes),
        out_shape=(
            jax.ShapeDtypeStruct((width, cols), jnp.bfloat16),
            jax.ShapeDtypeStruct((width, cols), jnp.bfloat16),
            jax.ShapeDtypeStruct((3 * tokens + width, width), jnp.bfloat16),
        ),
        in_specs=in_vmem(4),
        out_specs=tuple(in_vmem(3)),
        compiler_params=params(),
    )(w, x, s, q)


def solve(sizes, features, k, squares, x, s, u, v, q):
    layers, hd, rank, tokens, cols = sizes
    width = layers * hd
    return pl.pallas_call(
        functools.partial(solve_kernel, sizes, features),
        out_shape=jax.ShapeDtypeStruct(q.shape, jnp.bfloat16),
        in_specs=in_vmem(7),
        out_specs=in_vmem(1)[0],
        scratch_shapes=[
            pltpu.VMEM((tokens, width), jnp.bfloat16),
            pltpu.VMEM((tokens, width), jnp.bfloat16),
            pltpu.VMEM((tokens, width), jnp.bfloat16),
            pltpu.VMEM((layers, tokens, hd), jnp.float32),
            pltpu.VMEM((layers, tokens, hd), jnp.float32),
            pltpu.VMEM((layers, tokens, 1), jnp.float32),
        ],
        compiler_params=params(),
    )(k, squares, x, s, u, v, q)


def swap(value, axis):
    return lax.all_to_all(value, axis, split_axis=0, concat_axis=0, tiled=True)


def by_columns(rows, parts):
    return rows.reshape(rows.shape[0], parts, -1).transpose(1, 0, 2)


def pick(chooser, parts):
    flat = parts.reshape(parts.shape[0], -1)
    return mm(chooser, flat).astype(jnp.bfloat16).reshape((chooser.shape[0],) + parts.shape[1:])


def body(
    inputs,
    cotangent,
    norm_gain,
    w_value,
    w_out,
    value_down,
    value_up_factor,
    out_down,
    output_up_factor,
    block_tenant,
    valid_tokens,
    tenant_slot,
):
    section = lax.axis_index("pipe")
    sections = lax.axis_size("pipe")
    member = lax.axis_index("dp")
    members = lax.axis_size("dp")
    rows, features = inputs.shape[1], inputs.shape[2]
    hd, rank = w_value.shape[1], value_down.shape[2]
    cols = features // sections
    tokens = rows * sections
    sizes = (sections, hd, rank, tokens, cols)

    ids = jnp.arange(tenant_slot.shape[0], dtype=jnp.int32)
    tenant_hot = block_tenant[:, None] == ids[None, :]
    slot_of = jnp.sum(jnp.where(tenant_hot, tenant_slot[None, :], 0), axis=1)
    slot_hot = (slot_of[:, None] == ids[None, :]).astype(jnp.bfloat16)
    member_hot = jnp.arange(members, dtype=jnp.int32) == member
    own_tenant = jnp.sum(jnp.where(member_hot, block_tenant, 0))
    own_valid = jnp.sum(jnp.where(member_hot, valid_tokens, 0))
    tenant_tokens = jnp.sum(jnp.where(block_tenant == own_tenant, valid_tokens, 0)).astype(
        jnp.float32
    )

    gain = norm_gain[0]
    value_down_gained = (value_down[0, 0].astype(jnp.float32) * gain).astype(jnp.bfloat16)
    w_value_gained = (w_value[0].astype(jnp.float32) * gain).astype(jnp.bfloat16)
    small = jnp.concatenate([value_up_factor[0, 0], out_down[0, 0]], axis=1)
    stored = jnp.concatenate(
        [
            by_columns(value_down_gained, members),
            by_columns(output_up_factor[0, 0], members),
            jnp.broadcast_to(small[None], (members,) + small.shape),
        ],
        axis=2,
    )
    adapters = swap(pick(slot_hot, swap(stored, "dp")), "dp")

    position = section * rows + jnp.arange(rows, dtype=jnp.int32)
    weight = jnp.where(position < own_valid, 1.0, 0.0).astype(jnp.float32) / tenant_tokens
    seeded = (cotangent[0].astype(jnp.float32) * weight[:, None]).astype(jnp.bfloat16)
    own_rows = inputs[0].astype(jnp.float32)
    squares = lax.all_gather(jnp.sum(own_rows * own_rows, axis=1), "pipe", axis=0, tiled=True)
    packed = jnp.concatenate(
        [
            by_columns(w_value_gained, sections),
            by_columns(w_out[0], sections),
            by_columns(inputs[0], sections),
            by_columns(seeded, sections),
        ],
        axis=1,
    )
    packed = swap(packed, "pipe")
    adapters = swap(adapters, "pipe")
    x = packed[:, 2 * hd : 2 * hd + rows].reshape(tokens, cols)
    s = packed[:, 2 * hd + rows :].reshape(tokens, cols)

    u, v, partial = gram(sizes, packed, x, s, adapters)
    width = partial.shape[1]
    shares = swap(partial.reshape(sections, -1, width), "pipe")
    share = jnp.sum(shares.astype(jnp.float32), axis=0).astype(jnp.bfloat16)
    whole = swap(jnp.broadcast_to(share[None], shares.shape), "pipe").reshape(partial.shape)

    grads = solve(sizes, features, whole, squares[:, None], x, s, u, v, adapters)

    by_layer = swap(grads, "dp")
    summed = pick(slot_hot.T, by_layer)
    owned = swap(swap(summed, "dp"), "pipe")
    grad_value_down = owned[:, :, :cols].transpose(1, 0, 2).reshape(rank, features)
    grad_value_down = (grad_value_down.astype(jnp.float32) * gain).astype(jnp.bfloat16)
    grad_out_up = owned[:, :, cols : 2 * cols].transpose(1, 0, 2).reshape(rank, features)
    tail = jnp.sum(owned[:, :, 2 * cols :].astype(jnp.float32), axis=0).astype(jnp.bfloat16)
    return (
        grad_value_down[None, None],
        tail[None, None, :, :hd],
        tail[None, None, :, hd:],
        grad_out_up[None, None],
    )


def solution(mesh):
    return jax.shard_map(
        body,
        mesh=mesh,
        in_specs=(
            P("pipe", "dp", None),
            P("pipe", "dp", None),
            P("pipe", None),
            P("pipe", None, None),
            P("pipe", None, None),
            P("pipe", "dp", None, None),
            P("pipe", "dp", None, None),
            P("pipe", "dp", None, None),
            P("pipe", "dp", None, None),
            P(),
            P(),
            P(),
        ),
        out_specs=(
            P("pipe", "dp", None, None),
            P("pipe", "dp", None, None),
            P("pipe", "dp", None, None),
            P("pipe", "dp", None, None),
        ),
        check_vma=False,
    )
```

time: 1330 us -> 328 us (0.25); the launches traced: 1310 us -> 327 us
  other arithmetic: 345 us -> 9.99 us
  matrix products: 318 us -> 0.79 us
  waiting for transfers between devices: 286 us -> 56.2 us
  blocking collectives: 0 us -> 188 us
  starting transfers between devices: 182 us -> 24.2 us
  local copies, waits for them, and re-layouts: 166 us -> 15.5 us
  Pallas kernels: 0 us -> 30.5 us
    dot_general x535 -> x2, matrix products: 318 us -> 0.79 us  [mm(): lax.dot_general(left, right, (((1,), (0,)), ((), ())), preferred_element_...]
    ppermute x62 -> x0, waiting for transfers between devices: 231 us -> none  [from_behind(): lax.ppermute(value, axis, [(i, (i + by) % peers) for i in range(peers)])]
    unnamed x8 -> x1, other arithmetic: 181 us -> 1.48 us
    all_to_all x0 -> x5, blocking collectives: none -> 129 us  [swap(): return lax.all_to_all(value, axis, split_axis=0, concat_axis=0, tiled=True)]
    all_to_all x16 -> x4, starting transfers between devices: 149 us -> 24.2 us  [swap(): return lax.all_to_all(value, axis, split_axis=0, concat_axis=0, tiled=True)]
    unnamed x0 -> x1, blocking collectives: none -> 58.7 us
    convert_element_type x34 -> x1, other arithmetic: 54 us -> 0.74 us  [body(): (grad_value_down.astype(jnp.float32) * gain).astype(jnp.bfloat16)]
    dynamic_update_slice x31 -> x0, other arithmetic: 50.5 us -> none  [update(): lax.dynamic_update_index_in_dim(stored_all, jnp.where(active, new_entry,...]
  transfers between devices with their start and end apart: 80 -> 4, of which waited for: 39 -> 3; matrix products, arithmetic and copies ran while one was open for 48% -> 4% of each run, Pallas kernels for 0% -> 0%
where the time goes in v1:
time: 328 us; the launch traced here: 327 us
  blocking collectives  188 us (57%)
  waiting for transfers between devices  56.2 us (17%)
  Pallas kernels  30.5 us (9%)
  starting transfers between devices  24.2 us (7%)
  local copies, waits for them, and re-layouts  15.5 us (5%)
  other arithmetic  9.99 us (3%)
    all_to_all x5, blocking collectives, swap(): return lax.all_to_all(value, axis, split_axis=0, concat_axis=0, tiled=True)  129 us
    unnamed x1, blocking collectives  58.7 us
    all_to_all x4, waiting for transfers between devices, swap(): return lax.all_to_all(value, axis, split_axis=0, concat_axis=0, tiled=True)  56.2 us
    all_to_all x4, starting transfers between devices, swap(): return lax.all_to_all(value, axis, split_axis=0, concat_axis=0, tiled=True)  24.2 us
    pallas_call x1, Pallas kernels, solve(): pl.pallas_call(functools.partial(solve_kernel, sizes, features), out_shap...  23.8 us
    unnamed x38, local copies, waits for them, and re-layouts  9.32 us
    pallas_call x1, Pallas kernels, gram(): pl.pallas_call(functools.partial(gram_kernel, sizes), out_shape=(jax.Shap...  6.76 us
  transfers between devices with their start and end apart: 4, of which 3 were waited for; matrix products, arithmetic and copies ran while one was open for 4% of the time, Pallas kernels for 0%

profile of v1, /device:TPU:1, one launch (start us, length us, event | category | flops | bytes accessed | tf_op | source)
XLA Modules:
  0.0 327.4 jit_solution(11397933221313207038)
XLA Ops:
  1.2 1.5 reduce.6
  3.7 1.1 copy.36
  6.3 10.0 %all-to-all-start.1 = ((bf16[16,16,1152]{2,1,0:T(8,128)(2,1)}), bf16[16,16,1152]{2,1,0:T(8,128)(2,1)}, u32[]{:S(2)}, u32[]{:S(2)}) async-start(bf16[16,16,1152]{2,1,0:T(8,128)(2,1)} %pad_maximum_fusion.1), calls=%async_computation.1 | async-start | bytes 1179648 | tf_op jit(solution)/shard_map/all_to_all | solution.py:237
  16.9 1.3 fusion.8
  19.3 1.6 copy.34
  22.3 1.2 fusion.1
  23.5 1.6 pad_maximum_fusion
  25.1 9.9 %all-to-all-done.1 = bf16[16,16,1152]{2,1,0:T(8,128)(2,1)} async-done(((bf16[16,16,1152]{2,1,0:T(8,128)(2,1)}), bf16[16,16,1152]{2,1,0:T(8,128)(2,1)}, u32[]{:S(2)}, u32[]{:S(2)}) %all-to-all-start.1) | async-done | bytes 589856 | tf_op jit(solution)/shard_map/all_to_all | solution.py:237
  35.1 6.8 %all-to-all-start = ((bf16[16,144,512]{2,1,0:T(8,128)(2,1)}), bf16[16,144,512]{2,1,0:T(8,128)(2,1)S(1)}, u32[]{:S(2)}, u32[]{:S(2)}) async-start(bf16[16,144,512]{2,1,0:T(8,128)(2,1)} %pad_maximum_fusion), calls=%async_computation | async-start | bytes 4718592 | tf_op jit(solution)/shard_map/all_to_all | solution.py:237
  42.0 1.2 copy.37
  43.6 35.3 %all-to-all-done.w_ref = bf16[16,144,512]{2,1,0:T(8,128)(2,1)S(1)} async-done(((bf16[16,144,512]{2,1,0:T(8,128)(2,1)}), bf16[16,144,512]{2,1,0:T(8,128)(2,1)S(1)}, u32[]{:S(2)}, u32[]{:S(2)}) %all-to-all-start) | async-done | bytes 2359328 | tf_op jit(solution)/shard_map/all_to_all | solution.py:237
  78.9 22.3 %all_to_all.45 = bf16[16,16,1152]{2,1,0:T(8,128)(2,1)} all-to-all(bf16[16,16,1152]{2,1,0:T(8,128)(2,1)S(1)} %bitcast.67), channel_id=1, replica_groups=mesh['pipe'=16,'dp'=16] {'dp'}, dimensions={0} | all-to-all | bytes 1179648 | tf_op jit(solution)/shard_map/all_to_all | solution.py:237
  101.2 3.6 %all-to-all-start.3 = ((bf16[16,16,1152]{2,1,0:T(8,128)(2,1)}), bf16[16,16,1152]{2,1,0:T(8,128)(2,1)S(1)}, u32[]{:S(2)}, u32[]{:S(2)}) async-start(bf16[16,16,1152]{2,1,0:T(8,128)(2,1)} %all_to_all.45), calls=%async_computation.3 | async-start | bytes 1179648 | tf_op jit(solution)/shard_map/all_to_all | solution.py:237
  105.5 11.0 %all-to-all-done.3.q_ref = bf16[16,16,1152]{2,1,0:T(8,128)(2,1)S(1)} async-done(((bf16[16,16,1152]{2,1,0:T(8,128)(2,1)}), bf16[16,16,1152]{2,1,0:T(8,128)(2,1)S(1)}, u32[]{:S(2)}, u32[]{:S(2)}) %all-to-all-start.3) | async-done | bytes 589856 | tf_op jit(solution)/shard_map/all_to_all | solution.py:237
  117.3 6.8 %shard_map.147 = (bf16[1024,512]{1,0:T(8,128)(2,1)}, bf16[1024,512]{1,0:T(8,128)(2,1)}, bf16[1408,1024]{1,0:T(8,128)(2,1)}) custom-call(bf16[16,144,512]{2,1,0:T(8,128)(2,1)} %copy-done.1, bf16[128,512]{1,0:T(8,128)(2,1)} %get-tuple-element.13.x_ref, bf16[128,512]{1,0:T(8,128)(2,1)} %get-tuple-element.12.s_ref, bf16[16,16,1152]{2,1,0:T(8,128)(2,1)} %copy-done.2), custom_call_target="tpu_custom_call" | custom-call | tf_op jit(solution)/shard_map/pallas_call | solution.py:203
  124.1 39.0 %all_to_all.46 = bf16[16,88,1024]{2,1,0:T(8,128)(2,1)S(1)} all-to-all(bf16[16,88,1024]{2,1,0:T(8,128)(2,1)} %bitcast.66), channel_id=1, replica_groups=mesh['pipe'=16,'dp'=16] {'pipe'}, dimensions={0} | all-to-all | bytes 5767168 | tf_op jit(solution)/shard_map/all_to_all | solution.py:237
  163.7 1.9 broadcast_in_dim.60
  165.7 3.9 %all-to-all-start.5 = ((bf16[16,88,1024]{2,1,0:T(8,128)(2,1)}), bf16[16,88,1024]{2,1,0:T(8,128)(2,1)S(1)}, u32[]{:S(2)}, u32[]{:S(2)}) async-start(bf16[16,88,1024]{2,1,0:T(8,128)(2,1)} %broadcast_in_dim.60), calls=%async_computation.5 | async-start | bytes 5767168 | tf_op jit(solution)/shard_map/all_to_all | solution.py:237
  171.2 58.7 %all-reduce = f32[128]{0:T(128)S(1)} all-reduce(f32[128]{0:T(128)S(1)} %dynamic-update-slice), channel_id=1, replica_groups=mesh['pipe'=16,'dp'=16] {'pipe'}, use_global_device_ids=true, to_apply=%add | all-reduce | flops 128 | bytes 1024
  230.7 1.6 copy-done
  232.3 23.8 %shard_map.148 = bf16[16,16,1152]{2,1,0:T(8,128)(2,1)} custom-call(bf16[1408,1024]{1,0:T(8,128)(2,1)} %bitcast.62, f32[128,1]{1,0:T(8,128)} %copy.30.n_ref, bf16[128,512]{1,0:T(8,128)(2,1)} %get-tuple-element.13.x_ref, bf16[128,512]{1,0:T(8,128)(2,1)} %get-tuple-element.12.s_ref, bf16[1024,512]{1,0:T(8,128)(2,1)} %get-tuple-element.8.u_ref, ...), custom_call_target="tpu_custom_call" | custom-call | tf_op jit(solution)/shard_map/pallas_call | solution.py:219
  256.0 31.3 %all_to_all.47 = bf16[16,16,1152]{2,1,0:T(8,128)(2,1)S(1)} all-to-all(bf16[16,16,1152]{2,1,0:T(8,128)(2,1)} %shard_map.148), channel_id=1, replica_groups=mesh['pipe'=16,'dp'=16] {'dp'}, dimensions={0} | all-to-all | bytes 1179648 | tf_op jit(solution)/shard_map/all_to_all | solution.py:237
  288.0 21.6 %all_to_all.48 = bf16[16,16,1152]{2,1,0:T(8,128)(2,1)S(1)} all-to-all(bf16[16,16,1152]{2,1,0:T(8,128)(2,1)S(1)} %bitcast.73), channel_id=1, replica_groups=mesh['pipe'=16,'dp'=16] {'dp'}, dimensions={0} | all-to-all | bytes 1179648 | tf_op jit(solution)/shard_map/all_to_all | solution.py:237
  309.6 14.9 %all_to_all.49 = bf16[16,16,1152]{2,1,0:T(8,128)(2,1)S(1)} all-to-all(bf16[16,16,1152]{2,1,0:T(8,128)(2,1)S(1)} %all_to_all.48), channel_id=1, replica_groups=mesh['pipe'=16,'dp'=16] {'pipe'}, dimensions={0} | all-to-all | bytes 1179648 | tf_op jit(solution)/shard_map/all_to_all | solution.py:237
  (60 shorter events, 13.3 us)
Async XLA Ops:
  0.6 4.7 %copy-start.8 = (bf16[1,1,16,64]{3,2,1,0:T(8,128)(2,1)S(1)}, bf16[1,1,16,64]{3,2,1,0:T(8,128)(2,1)}, u32[]{:S(2)}) copy-start(bf16[1,1,16,64]{3,2,1,0:T(8,128)(2,1)} %param.18) | copy-start | bytes 6148
  0.6 4.7 %copy-start.7 = (bf16[1,1,16,64]{3,2,1,0:T(8,128)(2,1)S(1)}, bf16[1,1,16,64]{3,2,1,0:T(8,128)(2,1)}, u32[]{:S(2)}) copy-start(bf16[1,1,16,64]{3,2,1,0:T(8,128)(2,1)} %param.19) | copy-start | bytes 6148
  3.7 12.6 %copy-start.10 = (s32[16]{0:T(128)S(1)}, s32[16]{0:T(128)}, u32[]{:S(2)}) copy-start(s32[16]{0:T(128)} %param.21) | copy-start | bytes 196
  3.7 13.2 %copy-start.9 = (s32[16]{0:T(128)S(1)}, s32[16]{0:T(128)}, u32[]{:S(2)}) copy-start(s32[16]{0:T(128)} %param.22) | copy-start | bytes 196
  3.7 15.1 %copy-start.3 = (bf16[1,64,8192]{2,1,0:T(8,128)(2,1)S(1)}, bf16[1,64,8192]{2,1,0:T(8,128)(2,1)}, u32[]{:S(2)}) copy-start(bf16[1,64,8192]{2,1,0:T(8,128)(2,1)} %param.15) | copy-start | bytes 3145732
  6.3 28.7 %all-to-all-start.1 = ((bf16[16,16,1152]{2,1,0:T(8,128)(2,1)}), bf16[16,16,1152]{2,1,0:T(8,128)(2,1)}, u32[]{:S(2)}, u32[]{:S(2)}) async-start(bf16[16,16,1152]{2,1,0:T(8,128)(2,1)} %pad_maximum_fusion.1), calls=%async_computation.1 | async-start | bytes 1179648 | tf_op jit(solution)/shard_map/all_to_all | solution.py:237
  19.3 2.9 copy-start.6
  20.9 2.6 copy-start.4
  25.1 16.7 %copy-start.11 = (s32[16]{0:T(128)S(1)}, s32[16]{0:T(128)}, u32[]{:S(2)}) copy-start(s32[16]{0:T(128)} %param.23) | copy-start | bytes 196
  35.1 43.9 %all-to-all-start = ((bf16[16,144,512]{2,1,0:T(8,128)(2,1)}), bf16[16,144,512]{2,1,0:T(8,128)(2,1)S(1)}, u32[]{:S(2)}, u32[]{:S(2)}) async-start(bf16[16,144,512]{2,1,0:T(8,128)(2,1)} %pad_maximum_fusion), calls=%async_computation | async-start | bytes 4718592 | tf_op jit(solution)/shard_map/all_to_all | solution.py:237
  78.9 37.6 %copy-start.1 = (bf16[16,144,512]{2,1,0:T(8,128)(2,1)}, bf16[16,144,512]{2,1,0:T(8,128)(2,1)S(1)}, u32[]{:S(2)}) copy-start(bf16[16,144,512]{2,1,0:T(8,128)(2,1)S(1)} %all-to-all-done.w_ref) | copy-start | bytes 7077892
  101.2 15.3 %all-to-all-start.3 = ((bf16[16,16,1152]{2,1,0:T(8,128)(2,1)}), bf16[16,16,1152]{2,1,0:T(8,128)(2,1)S(1)}, u32[]{:S(2)}, u32[]{:S(2)}) async-start(bf16[16,16,1152]{2,1,0:T(8,128)(2,1)} %all_to_all.45), calls=%async_computation.3 | async-start | bytes 1179648 | tf_op jit(solution)/shard_map/all_to_all | solution.py:237
  116.5 0.8 copy-start.2
  165.6 3.9 %copy-start.12 = (u32[256]{0:T(256)S(1)}, u32[256]{0:T(256)}, u32[]{:S(2)}) copy-start(u32[256]{0:T(256)} %constant.29) | copy-start | bytes 3076
  165.7 65.0 %all-to-all-start.5 = ((bf16[16,88,1024]{2,1,0:T(8,128)(2,1)}), bf16[16,88,1024]{2,1,0:T(8,128)(2,1)S(1)}, u32[]{:S(2)}, u32[]{:S(2)}) async-start(bf16[16,88,1024]{2,1,0:T(8,128)(2,1)} %broadcast_in_dim.60), calls=%async_computation.5 | async-start | bytes 5767168 | tf_op jit(solution)/shard_map/all_to_all | solution.py:237
  230.7 1.6 copy-start
  324.5 2.2 copy-start.5

commit v2 on v1

--- a/solution.py
+++ b/solution.py
@@ -37,19 +37,59 @@
     return compare(row_layer, column_layer)
 
 
-def gram_kernel(sizes, w_ref, x_ref, s_ref, q_ref, u_ref, v_ref, out_ref):
-    layers, hd, rank, tokens, cols = sizes
-    for l in range(layers):
-        small = q_ref[l, :, 2 * cols : 2 * cols + 2 * hd]
-        delta_v = mm_tn(small[:, :hd], q_ref[l, :, :cols])
-        delta_u = mm_tn(small[:, hd:], q_ref[l, :, cols : 2 * cols])
-        at = pl.ds(l * hd, hd)
-        v_ref[at, :] = (w_ref[l, :hd, :].astype(jnp.float32) + adapter_scale * delta_v).astype(
+def spread_kernel(
+    sizes, p_ref, wv_ref, wo_ref, gain_ref, x_ref, cot_ref, weight_ref, *out_refs
+):
+    layers, hd, rank, tokens, cols = sizes
+    rows = tokens // layers
+    section = p_ref[0]
+    for step, out_ref in enumerate(out_refs):
+        at = pl.ds(pl.multiple_of(lax.rem(section + step, layers) * cols, cols), cols)
+        out_ref[:hd, :] = (wv_ref[:, at].astype(jnp.float32) * gain_ref[:, at]).astype(jnp.bfloat16)
+        out_ref[hd : 2 * hd, :] = wo_ref[:, at]
+        seeded = cot_ref[:, at].astype(jnp.float32) * weight_ref[...]
+        out_ref[2 * hd :, :] = jnp.concatenate(
+            [x_ref[:, at].astype(jnp.float32), seeded], axis=0
+        ).astype(jnp.bfloat16)
+
+
+def store_kernel(sizes, vd_ref, ou_ref, gain_ref, vu_ref, od_ref, out_ref):
+    layers, hd, rank, tokens, cols = sizes
+    small = jnp.concatenate([vu_ref[...], od_ref[...]], axis=1)
+    for k in range(out_ref.shape[0]):
+        at = pl.ds(k * cols, cols)
+        out_ref[k, :, :cols] = (vd_ref[:, at].astype(jnp.float32) * gain_ref[:, at]).astype(
             jnp.bfloat16
         )
-        u_ref[at, :] = (
-            w_ref[l, hd : 2 * hd, :].astype(jnp.float32) + adapter_scale * delta_u
-        ).astype(jnp.bfloat16)
+        out_ref[k, :, cols : 2 * cols] = ou_ref[:, at]
+        out_ref[k, :, 2 * cols :] = small
+
+
+def gram_kernel(sizes, p_ref, *refs):
+    layers, hd, rank, tokens, cols = sizes
+    rows = tokens // layers
+    w_refs = refs[:layers]
+    q_ref, u_ref, v_ref, x_ref, s_ref, out_ref, x_wide, s_wide = refs[layers:]
+    section = p_ref[0]
+    for step, w_ref in enumerate(w_refs):
+        l = lax.rem(section + layers - step, layers)
+        q_l = q_ref[l]
+        small = q_l[:, 2 * cols : 2 * cols + 2 * hd]
+        delta_v = mm_tn(small[:, :hd], q_l[:, :cols])
+        delta_u = mm_tn(small[:, hd:], q_l[:, cols : 2 * cols])
+        at = pl.ds(pl.multiple_of(l * hd, hd), hd)
+        v_ref[at, :] = (w_ref[:hd, :].astype(jnp.float32) + adapter_scale * delta_v).astype(
+            jnp.bfloat16
+        )
+        u_ref[at, :] = (w_ref[hd : 2 * hd, :].astype(jnp.float32) + adapter_scale * delta_u).astype(
+            jnp.bfloat16
+        )
+        both = w_ref[2 * hd :, :].astype(jnp.float32)
+        at = pl.ds(pl.multiple_of(l * rows, rows), rows)
+        x_wide[at, :] = both[:rows]
+        s_wide[at, :] = both[rows:]
+    x_ref[...] = x_wide[...].astype(jnp.bfloat16)
+    s_ref[...] = s_wide[...].astype(jnp.bfloat16)
     width = layers * hd
     base = 3 * tokens
     below = layer_mask(block, block, hd, lambda r, c: r < c)
@@ -68,6 +108,14 @@
             else:
                 part = jnp.where(below, mm_nt(rows, v_col), mm_nt(rows, u_col))
             out_ref[pl.ds(base + bi * block, block), at_col] = part.astype(jnp.bfloat16)
+    wide = x_wide[...]
+    wide = wide * wide
+    folded = wide[:, : 2 * hd]
+    for at in range(2 * hd, cols, 2 * hd):
+        folded = folded + wide[:, at : at + 2 * hd]
+    out_ref[tokens : 2 * tokens, width - hd :] = (folded[:, :hd] + folded[:, hd:]).astype(
+        jnp.bfloat16
+    )
 
 
 def half(pair, l):
@@ -79,7 +127,6 @@
     sizes,
     features,
     k_ref,
-    n_ref,
     x_ref,
     s_ref,
     u_ref,
@@ -106,34 +153,39 @@
     def upto(l):
         return 2 * hd * ((l + 1) // 2)
 
-    square = n_ref[...]
+    folded = k_ref[tokens : 2 * tokens, width - 2 * hd :].astype(jnp.float32)[:, hd:]
+    square = jnp.sum(folded, axis=1, keepdims=True)
     for l in range(layers):
         pair = pair_of(l)
         rows_l = pl.ds(base + l * hd, hd)
         a = half(k_ref[:tokens, pair], l).astype(jnp.float32)
-        b = half(k_ref[tokens : 2 * tokens, pair], l).astype(jnp.float32)
         if l:
             w = upto(l)
             known = c_ref[:, :w]
             a = a + half(mm(known, k_ref[base : base + w, pair]), l)
-            b = b + mm_nt(known, k_ref[rows_l, :w])
         inverse = lax.rsqrt(jnp.maximum(square, 0.0) / features + norm_eps)
         c = (inverse * a).astype(jnp.bfloat16)
+        c_ref[:, l * hd : (l + 1) * hd] = c
+        a_ref[l] = a
+        inv_ref[l] = inverse
+        if l == layers - 1:
+            break
+        b = half(k_ref[tokens : 2 * tokens, pair], l).astype(jnp.float32)
+        if l:
+            b = b + mm_nt(known, k_ref[rows_l, :w])
         wide = c.astype(jnp.float32)
         after = b + half(mm(c, k_ref[rows_l, pair]), l)
         square = square + jnp.sum(wide * (b + after), axis=1, keepdims=True)
-        c_ref[:, l * hd : (l + 1) * hd] = c
-        a_ref[l] = a
         bp_ref[l] = after
-        inv_ref[l] = inverse
-
-    pull = jnp.zeros_like(square)
+
+    pull = jnp.zeros((tokens, 1), jnp.float32)
     for l in range(layers - 1, -1, -1):
         pair = pair_of(l)
         rows_l = pl.ds(base + l * hd, hd)
-        p = half(k_ref[2 * tokens : 3 * tokens, pair], l).astype(jnp.float32) - pull * bp_ref[l]
+        p = half(k_ref[2 * tokens : 3 * tokens, pair], l).astype(jnp.float32)
         if l < layers - 1:
             w = upto(l)
+            p = p - pull * bp_ref[l]
             p = p + mm_nt(d_ref[:, w:], k_ref[rows_l, w:])
             p = p - half(mm(ec_ref[:, w:], k_ref[base + w : base + width, pair]), l)
         inverse = inv_ref[l]
@@ -197,7 +249,30 @@
     return [pl.BlockSpec(memory_space=pltpu.VMEM)] * count
 
 
-def gram(sizes, w, x, s, q):
+def spread(sizes, section, w_value, w_out, gain, x, cotangent, weight):
+    layers, hd, rank, tokens, cols = sizes
+    shape = jax.ShapeDtypeStruct((2 * hd + 2 * (tokens // layers), cols), jnp.bfloat16)
+    return pl.pallas_call(
+        functools.partial(spread_kernel, sizes),
+        out_shape=(shape,) * layers,
+        in_specs=[pl.BlockSpec(memory_space=pltpu.SMEM)] + in_vmem(6),
+        out_specs=tuple(in_vmem(layers)),
+        compiler_params=params(),
+    )(section, w_value, w_out, gain, x, cotangent, weight)
+
+
+def store(sizes, members, value_down, output_up, gain, value_up, out_down):
+    layers, hd, rank, tokens, cols = sizes
+    return pl.pallas_call(
+        functools.partial(store_kernel, sizes),
+        out_shape=jax.ShapeDtypeStruct((members, rank, 2 * cols + 2 * hd), jnp.bfloat16),
+        in_specs=in_vmem(5),
+        out_specs=in_vmem(1)[0],
+        compiler_params=params(),
+    )(value_down, output_up, gain, value_up, out_down)
+
+
+def gram(sizes, section, blocks, q):
     layers, hd, rank, tokens, cols = sizes
     width = layers * hd
     return pl.pallas_call(
@@ -205,21 +280,27 @@
         out_shape=(
             jax.ShapeDtypeStruct((width, cols), jnp.bfloat16),
             jax.ShapeDtypeStruct((width, cols), jnp.bfloat16),
+            jax.ShapeDtypeStruct((tokens, cols), jnp.bfloat16),
+            jax.ShapeDtypeStruct((tokens, cols), jnp.bfloat16),
             jax.ShapeDtypeStruct((3 * tokens + width, width), jnp.bfloat16),
         ),
-        in_specs=in_vmem(4),
-        out_specs=tuple(in_vmem(3)),
+        in_specs=[pl.BlockSpec(memory_space=pltpu.SMEM)] + in_vmem(layers + 1),
+        out_specs=tuple(in_vmem(5)),
+        scratch_shapes=[
+            pltpu.VMEM((tokens, cols), jnp.float32),
+            pltpu.VMEM((tokens, cols), jnp.float32),
+        ],
         compiler_params=params(),
-    )(w, x, s, q)
-
-
-def solve(sizes, features, k, squares, x, s, u, v, q):
+    )(section, *blocks, q)
+
+
+def solve(sizes, features, k, x, s, u, v, q):
     layers, hd, rank, tokens, cols = sizes
     width = layers * hd
     return pl.pallas_call(
         functools.partial(solve_kernel, sizes, features),
         out_shape=jax.ShapeDtypeStruct(q.shape, jnp.bfloat16),
-        in_specs=in_vmem(7),
+        in_specs=in_vmem(6),
         out_specs=in_vmem(1)[0],
         scratch_shapes=[
             pltpu.VMEM((tokens, width), jnp.bfloat16),
@@ -230,15 +311,11 @@
             pltpu.VMEM((layers, tokens, 1), jnp.float32),
         ],
         compiler_params=params(),
-    )(k, squares, x, s, u, v, q)
+    )(k, x, s, u, v, q)
 
 
 def swap(value, axis):
     return lax.all_to_all(value, axis, split_axis=0, concat_axis=0, tiled=True)
-
-
-def by_columns(rows, parts):
-    return rows.reshape(rows.shape[0], parts, -1).transpose(1, 0, 2)
 
 
 def pick(chooser, parts):
@@ -281,46 +358,42 @@
         jnp.float32
     )
 
-    gain = norm_gain[0]
-    value_down_gained = (value_down[0, 0].astype(jnp.float32) * gain).astype(jnp.bfloat16)
-    w_value_gained = (w_value[0].astype(jnp.float32) * gain).astype(jnp.bfloat16)
-    small = jnp.concatenate([value_up_factor[0, 0], out_down[0, 0]], axis=1)
-    stored = jnp.concatenate(
-        [
-            by_columns(value_down_gained, members),
-            by_columns(output_up_factor[0, 0], members),
-            jnp.broadcast_to(small[None], (members,) + small.shape),
-        ],
-        axis=2,
-    )
-    adapters = swap(pick(slot_hot, swap(stored, "dp")), "dp")
-
+    gain = norm_gain
+    stored = store(
+        sizes,
+        members,
+        value_down[0, 0],
+        output_up_factor[0, 0],
+        gain,
+        value_up_factor[0, 0],
+        out_down[0, 0],
+    )
     position = section * rows + jnp.arange(rows, dtype=jnp.int32)
     weight = jnp.where(position < own_valid, 1.0, 0.0).astype(jnp.float32) / tenant_tokens
-    seeded = (cotangent[0].astype(jnp.float32) * weight[:, None]).astype(jnp.bfloat16)
-    own_rows = inputs[0].astype(jnp.float32)
-    squares = lax.all_gather(jnp.sum(own_rows * own_rows, axis=1), "pipe", axis=0, tiled=True)
-    packed = jnp.concatenate(
-        [
-            by_columns(w_value_gained, sections),
-            by_columns(w_out[0], sections),
-            by_columns(inputs[0], sections),
-            by_columns(seeded, sections),
-        ],
-        axis=1,
-    )
-    packed = swap(packed, "pipe")
-    adapters = swap(adapters, "pipe")
-    x = packed[:, 2 * hd : 2 * hd + rows].reshape(tokens, cols)
-    s = packed[:, 2 * hd + rows :].reshape(tokens, cols)
-
-    u, v, partial = gram(sizes, packed, x, s, adapters)
+    own_section = section.astype(jnp.int32)[None]
+    blocks = spread(
+        sizes,
+        own_section,
+        w_value[0],
+        w_out[0],
+        gain,
+        inputs[0],
+        cotangent[0],
+        weight[:, None],
+    )
+    blocks = [blocks[0]] + [
+        lax.ppermute(blocks[step], "pipe", [(i, (i + step) % sections) for i in range(sections)])
+        for step in range(1, sections)
+    ]
+    adapters = swap(swap(pick(slot_hot, swap(stored, "dp")), "dp"), "pipe")
+
+    u, v, x, s, partial = gram(sizes, own_section, blocks, adapters)
     width = partial.shape[1]
     shares = swap(partial.reshape(sections, -1, width), "pipe")
     share = jnp.sum(shares.astype(jnp.float32), axis=0).astype(jnp.bfloat16)
     whole = swap(jnp.broadcast_to(share[None], shares.shape), "pipe").reshape(partial.shape)
 
-    grads = solve(sizes, features, whole, squares[:, None], x, s, u, v, adapters)
+    grads = solve(sizes, features, whole, x, s, u, v, adapters)
 
     by_layer = swap(grads, "dp")
     summed = pick(slot_hot.T, by_layer)

time: 328 us -> 294 us (0.90)
  blocking collectives: 188 us -> 144 us
  starting transfers between devices: 24.2 us -> 36.9 us
  local copies, waits for them, and re-layouts: 15.5 us -> 4.38 us
  waiting for transfers between devices: 56.2 us -> 65.6 us
  other arithmetic: 9.99 us -> 5.42 us
  Pallas kernels: 30.5 us -> 34.5 us
    unnamed x1 -> x0, blocking collectives: 58.7 us -> none
    ppermute x0 -> x15, waiting for transfers between devices: none -> 32.7 us  [body(): lax.ppermute(blocks[step], 'pipe', [(i, (i + step) % sections) for i in r...]
    all_to_all x4 -> x3, waiting for transfers between devices: 56.2 us -> 32.8 us  [swap(): return lax.all_to_all(value, axis, split_axis=0, concat_axis=0, tiled=True)]
    ppermute x0 -> x15, starting transfers between devices: none -> 15.9 us  [body(): lax.ppermute(blocks[step], 'pipe', [(i, (i + step) % sections) for i in r...]
    all_to_all x5, blocking collectives: 129 us -> 144 us  [swap(): return lax.all_to_all(value, axis, split_axis=0, concat_axis=0, tiled=True)]
    unnamed x38 -> x42, local copies, waits for them, and re-layouts: 9.32 us -> 1.97 us
    pallas_call x0 -> x2, Pallas kernels: none -> 5.13 us  [the longest x1 3.16 us: spread(): pl.pallas_call(functools.partial(spread_kernel, sizes), out_shape=(shape,...]
    all_to_all x4 -> x3, starting transfers between devices: 24.2 us -> 21 us  [swap(): return lax.all_to_all(value, axis, split_axis=0, concat_axis=0, tiled=True)]
  transfers between devices with their start and end apart: 4 -> 18, of which waited for: 3 -> 10; matrix products, arithmetic and copies ran while one was open for 4% -> 1% of each run, Pallas kernels for 0% -> 1%
where the time goes in v2:
time: 294 us; the launch traced here: 293 us
  blocking collectives  144 us (49%)
  waiting for transfers between devices  65.6 us (22%)
  starting transfers between devices  36.9 us (13%)
  Pallas kernels  34.5 us (12%)
  other arithmetic  5.42 us (2%)
  local copies, waits for them, and re-layouts  4.38 us (1%)
    all_to_all x5, blocking collectives, swap(): return lax.all_to_all(value, axis, split_axis=0, concat_axis=0, tiled=True)  144 us
    all_to_all x3, waiting for transfers between devices, swap(): return lax.all_to_all(value, axis, split_axis=0, concat_axis=0, tiled=True)  32.8 us
    ppermute x15, waiting for transfers between devices, body(): lax.ppermute(blocks[step], 'pipe', [(i, (i + step) % sections) for i in r...  32.7 us
    pallas_call x1, Pallas kernels, solve(): pl.pallas_call(functools.partial(solve_kernel, sizes, features), out_shap...  22.6 us
    all_to_all x3, starting transfers between devices, swap(): return lax.all_to_all(value, axis, split_axis=0, concat_axis=0, tiled=True)  21 us
    ppermute x15, starting transfers between devices, body(): lax.ppermute(blocks[step], 'pipe', [(i, (i + step) % sections) for i in r...  15.9 us
    pallas_call x1, Pallas kernels, gram(): pl.pallas_call(functools.partial(gram_kernel, sizes), out_shape=(jax.Shap...  6.75 us
  transfers between devices with their start and end apart: 18, of which 10 were waited for; matrix products, arithmetic and copies ran while one was open for 1% of the time, Pallas kernels for 1%

profile of v2, /device:TPU:1, one launch (start us, length us, event | category | flops | bytes accessed | tf_op | source)
XLA Modules:
  0.0 293.4 jit_solution(11773005478157980907)
XLA Ops:
  0.6 2.0 shard_map.148
  2.6 10.1 %all-to-all-start = ((bf16[16,16,1152]{2,1,0:T(8,128)(2,1)}), bf16[16,16,1152]{2,1,0:T(8,128)(2,1)S(1)}, u32[]{:S(2)}, u32[]{:S(2)}) async-start(bf16[16,16,1152]{2,1,0:T(8,128)(2,1)} %shard_map.148), calls=%async_computation | async-start | bytes 1179648 | tf_op jit(solution)/shard_map/all_to_all | solution.py:318
  13.6 17.8 %all-to-all-done = bf16[16,16,1152]{2,1,0:T(8,128)(2,1)S(1)} async-done(((bf16[16,16,1152]{2,1,0:T(8,128)(2,1)}), bf16[16,16,1152]{2,1,0:T(8,128)(2,1)S(1)}, u32[]{:S(2)}, u32[]{:S(2)}) %all-to-all-start) | async-done | bytes 589856 | tf_op jit(solution)/shard_map/all_to_all | solution.py:318
  32.7 4.1 %all-to-all-start.1 = ((bf16[16,16,1152]{2,1,0:T(8,128)(2,1)}), bf16[16,16,1152]{2,1,0:T(8,128)(2,1)}, u32[]{:S(2)}, u32[]{:S(2)}) async-start(bf16[16,16,1152]{2,1,0:T(8,128)(2,1)} %bitcast.19), calls=%async_computation.1 | async-start | bytes 1179648 | tf_op jit(solution)/shard_map/all_to_all | solution.py:318
  39.5 15.0 %all-to-all-done.1 = bf16[16,16,1152]{2,1,0:T(8,128)(2,1)} async-done(((bf16[16,16,1152]{2,1,0:T(8,128)(2,1)}), bf16[16,16,1152]{2,1,0:T(8,128)(2,1)}, u32[]{:S(2)}, u32[]{:S(2)}) %all-to-all-start.1) | async-done | bytes 589856 | tf_op jit(solution)/shard_map/all_to_all | solution.py:318
  54.5 6.8 %all-to-all-start.2 = ((bf16[16,16,1152]{2,1,0:T(8,128)(2,1)}), bf16[16,16,1152]{2,1,0:T(8,128)(2,1)S(1)}, u32[]{:S(2)}, u32[]{:S(2)}) async-start(bf16[16,16,1152]{2,1,0:T(8,128)(2,1)} %all-to-all-done.1), calls=%async_computation.2 | async-start | bytes 1179648 | tf_op jit(solution)/shard_map/all_to_all | solution.py:318
  62.5 3.2 %shard_map.147 = (bf16[144,512]{1,0:T(8,128)(2,1)}, bf16[144,512]{1,0:T(8,128)(2,1)}, bf16[144,512]{1,0:T(8,128)(2,1)}, bf16[144,512]{1,0:T(8,128)(2,1)}, bf16[1...) custom-call(s32[1]{0:T(128)} %bitcast.p_ref, ...), custom_call_target="tpu_custom_call" | custom-call | tf_op jit(solution)/shard_map/pallas_call | solution.py:255
  67.0 2.4 collective-permute-start.1
  69.4 2.1 collective-permute-start.2
  73.6 3.6 %collective-permute-done.refs_1_ = bf16[144,512]{1,0:T(8,128)(2,1)S(1)} collective-permute-done((bf16[144,512]{1,0:T(8,128)(2,1)}, bf16[144,512]{1,0:T(8,128)(2,1)S(1)}, u32[]{:S(2)}, u32[]{:S(2)}) %collective-permute-start) | collective-permute-done | bytes 147488 | tf_op jit(solution)/shard_map/ppermute | solution.py:385
  77.2 5.0 %collective-permute-done.1.refs_2_ = bf16[144,512]{1,0:T(8,128)(2,1)S(1)} collective-permute-done((bf16[144,512]{1,0:T(8,128)(2,1)}, bf16[144,512]{1,0:T(8,128)(2,1)S(1)}, u32[]{:S(2)}, u32[]{:S(2)}) %collective-permute-start.1) | collective-permute-done | bytes 147488 | tf_op jit(solution)/shard_map/ppermute | solution.py:385
  82.5 1.4 collective-permute-start.7
  83.9 11.4 %collective-permute-done.3.refs_4_ = bf16[144,512]{1,0:T(8,128)(2,1)S(1)} collective-permute-done((bf16[144,512]{1,0:T(8,128)(2,1)}, bf16[144,512]{1,0:T(8,128)(2,1)S(1)}, u32[]{:S(2)}, u32[]{:S(2)}) %collective-permute-start.3) | collective-permute-done | bytes 147488 | tf_op jit(solution)/shard_map/ppermute | solution.py:385
  95.5 3.0 %collective-permute-start.10 = (bf16[144,512]{1,0:T(8,128)(2,1)}, bf16[144,512]{1,0:T(8,128)(2,1)S(1)}, u32[]{:S(2)}, u32[]{:S(2)}) collective-permute-start(bf16[144,512]{1,0:T(8,128)(2,1)} %get-tuple-element.36), channel_id=1, source_target_pairs={{0,176},{16,192},{32,208},{48,224},{64,240},{80,0},{96,16},{112,32... | collective-permute-start | bytes 442376 | tf_op jit(solution)/shard_map/ppermute | solution.py:385
  98.5 2.9 collective-permute-start.11
  101.8 6.2 %collective-permute-done.8.refs_9_ = bf16[144,512]{1,0:T(8,128)(2,1)S(1)} collective-permute-done((bf16[144,512]{1,0:T(8,128)(2,1)}, bf16[144,512]{1,0:T(8,128)(2,1)S(1)}, u32[]{:S(2)}, u32[]{:S(2)}) %collective-permute-start.8) | collective-permute-done | bytes 147488 | tf_op jit(solution)/shard_map/ppermute | solution.py:385
  108.2 4.7 %collective-permute-done.11.refs_12_ = bf16[144,512]{1,0:T(8,128)(2,1)S(1)} collective-permute-done((bf16[144,512]{1,0:T(8,128)(2,1)}, bf16[144,512]{1,0:T(8,128)(2,1)S(1)}, u32[]{:S(2)}, u32[]{:S(2)}) %collective-permute-start.11) | collective-permute-done | bytes 147488 | tf_op jit(solution)/shard_map/ppermute | solution.py:385
  115.3 6.8 %shard_map.149 = (bf16[1024,512]{1,0:T(8,128)(2,1)}, bf16[1024,512]{1,0:T(8,128)(2,1)}, bf16[128,512]{1,0:T(8,128)(2,1)}, bf16[128,512]{1,0:T(8,128)(2,1)}, bf16[1408,1024]{1,0:T(8,128)(2,1)}) custom-call(s32[1]{0:T(128)} %bitcast.p_ref, bf16[144,512]{1,0:T(8,128)(2,1)} %get-tuple-element.25.refs_0_, bf16[144,512]{1,0:T(8,128)(2,1)} %copy-done.2, ...), custom_call_target="tpu_custom_call" | custom-call | tf_op jit(solution)/shard_map/pallas_call | solution.py:278
  122.1 44.4 %all_to_all.40 = bf16[16,88,1024]{2,1,0:T(8,128)(2,1)S(1)} all-to-all(bf16[16,88,1024]{2,1,0:T(8,128)(2,1)} %bitcast.31), channel_id=1, replica_groups=mesh['pipe'=16,'dp'=16] {'pipe'}, dimensions={0} | all-to-all | bytes 5767168 | tf_op jit(solution)/shard_map/all_to_all | solution.py:318
  167.4 37.8 %all_to_all.41 = bf16[16,88,1024]{2,1,0:T(8,128)(2,1)} all-to-all(bf16[16,88,1024]{2,1,0:T(8,128)(2,1)S(1)} %broadcast_in_dim.54), channel_id=1, replica_groups=mesh['pipe'=16,'dp'=16] {'pipe'}, dimensions={0} | all-to-all | bytes 5767168 | tf_op jit(solution)/shard_map/all_to_all | solution.py:318
  205.2 22.6 %shard_map.150 = bf16[16,16,1152]{2,1,0:T(8,128)(2,1)} custom-call(bf16[1408,1024]{1,0:T(8,128)(2,1)} %bitcast.30, bf16[128,512]{1,0:T(8,128)(2,1)} %get-tuple-element.42.x_ref, bf16[128,512]{1,0:T(8,128)(2,1)} %get-tuple-element.43.s_ref, bf16[1024,512]{1,0:T(8,128)(2,1)} %get-tuple-element.44.u_ref, bf16[1024,512]{1,0:T(8,128)(2,1)} %get-tuple-element.45.v_ref, ...), custom_call_target="tpu_custom_call" | custom-call | tf_op jit(solution)/shard_map/pallas_call | solution.py:300
  227.8 26.0 %all_to_all.42 = bf16[16,16,1152]{2,1,0:T(8,128)(2,1)S(1)} all-to-all(bf16[16,16,1152]{2,1,0:T(8,128)(2,1)} %shard_map.150), channel_id=1, replica_groups=mesh['pipe'=16,'dp'=16] {'dp'}, dimensions={0} | all-to-all | bytes 1179648 | tf_op jit(solution)/shard_map/all_to_all | solution.py:318
  254.4 21.6 %all_to_all.43 = bf16[16,16,1152]{2,1,0:T(8,128)(2,1)S(1)} all-to-all(bf16[16,16,1152]{2,1,0:T(8,128)(2,1)S(1)} %bitcast.38), channel_id=1, replica_groups=mesh['pipe'=16,'dp'=16] {'dp'}, dimensions={0} | all-to-all | bytes 1179648 | tf_op jit(solution)/shard_map/all_to_all | solution.py:318
  276.0 14.5 %all_to_all.44 = bf16[16,16,1152]{2,1,0:T(8,128)(2,1)S(1)} all-to-all(bf16[16,16,1152]{2,1,0:T(8,128)(2,1)S(1)} %all_to_all.43), channel_id=1, replica_groups=mesh['pipe'=16,'dp'=16] {'pipe'}, dimensions={0} | all-to-all | bytes 1179648 | tf_op jit(solution)/shard_map/all_to_all | solution.py:318
  (79 shorter events, 16.4 us)
Async XLA Ops:
  2.6 34.3 %copy-start.18 = (s32[16]{0:T(128)S(1)}, s32[16]{0:T(128)}, u32[]{:S(2)}) copy-start(s32[16]{0:T(128)} %param.21) | copy-start | bytes 196
  2.6 34.9 %copy-start.17 = (s32[16]{0:T(128)S(1)}, s32[16]{0:T(128)}, u32[]{:S(2)}) copy-start(s32[16]{0:T(128)} %param.22) | copy-start | bytes 196
  2.6 28.8 %all-to-all-start = ((bf16[16,16,1152]{2,1,0:T(8,128)(2,1)}), bf16[16,16,1152]{2,1,0:T(8,128)(2,1)S(1)}, u32[]{:S(2)}, u32[]{:S(2)}) async-start(bf16[16,16,1152]{2,1,0:T(8,128)(2,1)} %shard_map.148), calls=%async_computation | async-start | bytes 1179648 | tf_op jit(solution)/shard_map/all_to_all | solution.py:318
  32.7 21.7 %all-to-all-start.1 = ((bf16[16,16,1152]{2,1,0:T(8,128)(2,1)}), bf16[16,16,1152]{2,1,0:T(8,128)(2,1)}, u32[]{:S(2)}, u32[]{:S(2)}) async-start(bf16[16,16,1152]{2,1,0:T(8,128)(2,1)} %bitcast.19), calls=%async_computation.1 | async-start | bytes 1179648 | tf_op jit(solution)/shard_map/all_to_all | solution.py:318
  54.5 59.9 %all-to-all-start.2 = ((bf16[16,16,1152]{2,1,0:T(8,128)(2,1)}), bf16[16,16,1152]{2,1,0:T(8,128)(2,1)S(1)}, u32[]{:S(2)}, u32[]{:S(2)}) async-start(bf16[16,16,1152]{2,1,0:T(8,128)(2,1)} %all-to-all-done.1), calls=%async_computation.2 | async-start | bytes 1179648 | tf_op jit(solution)/shard_map/all_to_all | solution.py:318
  65.7 11.5 %collective-permute-start = (bf16[144,512]{1,0:T(8,128)(2,1)}, bf16[144,512]{1,0:T(8,128)(2,1)S(1)}, u32[]{:S(2)}, u32[]{:S(2)}) collective-permute-start(bf16[144,512]{1,0:T(8,128)(2,1)} %get-tuple-element.26), channel_id=1, source_target_pairs={{0,16},{16,32},{32,48},{48,64},{64,80},{80,96},{96,112},{112,128},... | collective-permute-start | bytes 442376 | tf_op jit(solution)/shard_map/ppermute | solution.py:385
  67.0 15.1 %collective-permute-start.1 = (bf16[144,512]{1,0:T(8,128)(2,1)}, bf16[144,512]{1,0:T(8,128)(2,1)S(1)}, u32[]{:S(2)}, u32[]{:S(2)}) collective-permute-start(bf16[144,512]{1,0:T(8,128)(2,1)} %get-tuple-element.27), channel_id=1, source_target_pairs={{0,32},{16,48},{32,64},{48,80},{64,96},{80,112},{96,128},{112,144}... | collective-permute-start | bytes 442376 | tf_op jit(solution)/shard_map/ppermute | solution.py:385
  69.4 13.0 %collective-permute-start.2 = (bf16[144,512]{1,0:T(8,128)(2,1)}, bf16[144,512]{1,0:T(8,128)(2,1)S(1)}, u32[]{:S(2)}, u32[]{:S(2)}) collective-permute-start(bf16[144,512]{1,0:T(8,128)(2,1)} %get-tuple-element.28), channel_id=1, source_target_pairs={{0,48},{16,64},{32,80},{48,96},{64,112},{80,128},{96,144},{112,160... | collective-permute-start | bytes 442376 | tf_op jit(solution)/shard_map/ppermute | solution.py:385
  71.5 23.8 %collective-permute-start.3 = (bf16[144,512]{1,0:T(8,128)(2,1)}, bf16[144,512]{1,0:T(8,128)(2,1)S(1)}, u32[]{:S(2)}, u32[]{:S(2)}) collective-permute-start(bf16[144,512]{1,0:T(8,128)(2,1)} %get-tuple-element.29), channel_id=1, source_target_pairs={{0,64},{16,80},{32,96},{48,112},{64,128},{80,144},{96,160},{112,17... | collective-permute-start | bytes 442376 | tf_op jit(solution)/shard_map/ppermute | solution.py:385
  72.7 22.6 %collective-permute-start.4 = (bf16[144,512]{1,0:T(8,128)(2,1)}, bf16[144,512]{1,0:T(8,128)(2,1)S(1)}, u32[]{:S(2)}, u32[]{:S(2)}) collective-permute-start(bf16[144,512]{1,0:T(8,128)(2,1)} %get-tuple-element.30), channel_id=1, source_target_pairs={{0,80},{16,96},{32,112},{48,128},{64,144},{80,160},{96,176},{112,1... | collective-permute-start | bytes 442376 | tf_op jit(solution)/shard_map/ppermute | solution.py:385
  77.2 37.2 %copy-start.2 = (bf16[144,512]{1,0:T(8,128)(2,1)}, bf16[144,512]{1,0:T(8,128)(2,1)S(1)}, u32[]{:S(2)}) copy-start(bf16[144,512]{1,0:T(8,128)(2,1)S(1)} %collective-permute-done.refs_1_) | copy-start | bytes 442372
  77.2 18.2 %collective-permute-start.5 = (bf16[144,512]{1,0:T(8,128)(2,1)}, bf16[144,512]{1,0:T(8,128)(2,1)S(1)}, u32[]{:S(2)}, u32[]{:S(2)}) collective-permute-start(bf16[144,512]{1,0:T(8,128)(2,1)} %get-tuple-element.31), channel_id=1, source_target_pairs={{0,96},{16,112},{32,128},{48,144},{64,160},{80,176},{96,192},{112,... | collective-permute-start | bytes 442376 | tf_op jit(solution)/shard_map/ppermute | solution.py:385
  82.2 32.3 %copy-start.3 = (bf16[144,512]{1,0:T(8,128)(2,1)}, bf16[144,512]{1,0:T(8,128)(2,1)S(1)}, u32[]{:S(2)}) copy-start(bf16[144,512]{1,0:T(8,128)(2,1)S(1)} %collective-permute-done.1.refs_2_) | copy-start | bytes 442372
  82.2 16.3 %collective-permute-start.6 = (bf16[144,512]{1,0:T(8,128)(2,1)}, bf16[144,512]{1,0:T(8,128)(2,1)S(1)}, u32[]{:S(2)}, u32[]{:S(2)}) collective-permute-start(bf16[144,512]{1,0:T(8,128)(2,1)} %get-tuple-element.32), channel_id=1, source_target_pairs={{0,112},{16,128},{32,144},{48,160},{64,176},{80,192},{96,208},{112... | collective-permute-start | bytes 442376 | tf_op jit(solution)/shard_map/ppermute | solution.py:385
  82.5 32.0 %copy-start.4 = (bf16[144,512]{1,0:T(8,128)(2,1)}, bf16[144,512]{1,0:T(8,128)(2,1)S(1)}, u32[]{:S(2)}) copy-start(bf16[144,512]{1,0:T(8,128)(2,1)S(1)} %collective-permute-done.2.refs_3_) | copy-start | bytes 442372
  82.5 18.9 %collective-permute-start.7 = (bf16[144,512]{1,0:T(8,128)(2,1)}, bf16[144,512]{1,0:T(8,128)(2,1)S(1)}, u32[]{:S(2)}, u32[]{:S(2)}) collective-permute-start(bf16[144,512]{1,0:T(8,128)(2,1)} %get-tuple-element.33), channel_id=1, source_target_pairs={{0,128},{16,144},{32,160},{48,176},{64,192},{80,208},{96,224},{112... | collective-permute-start | bytes 442376 | tf_op jit(solution)/shard_map/ppermute | solution.py:385
  95.3 19.1 %copy-start.5 = (bf16[144,512]{1,0:T(8,128)(2,1)}, bf16[144,512]{1,0:T(8,128)(2,1)S(1)}, u32[]{:S(2)}) copy-start(bf16[144,512]{1,0:T(8,128)(2,1)S(1)} %collective-permute-done.3.refs_4_) | copy-start | bytes 442372
  95.3 12.7 %collective-permute-start.8 = (bf16[144,512]{1,0:T(8,128)(2,1)}, bf16[144,512]{1,0:T(8,128)(2,1)S(1)}, u32[]{:S(2)}, u32[]{:S(2)}) collective-permute-start(bf16[144,512]{1,0:T(8,128)(2,1)} %get-tuple-element.34), channel_id=1, source_target_pairs={{0,144},{16,160},{32,176},{48,192},{64,208},{80,224},{96,240},{112... | collective-permute-start | bytes 442376 | tf_op jit(solution)/shard_map/ppermute | solution.py:385
  95.4 12.7 %collective-permute-start.9 = (bf16[144,512]{1,0:T(8,128)(2,1)}, bf16[144,512]{1,0:T(8,128)(2,1)S(1)}, u32[]{:S(2)}, u32[]{:S(2)}) collective-permute-start(bf16[144,512]{1,0:T(8,128)(2,1)} %get-tuple-element.35), channel_id=1, source_target_pairs={{0,160},{16,176},{32,192},{48,208},{64,224},{80,240},{96,0},{112,1... | collective-permute-start | bytes 442376 | tf_op jit(solution)/shard_map/ppermute | solution.py:385
  95.5 12.7 %collective-permute-start.10 = (bf16[144,512]{1,0:T(8,128)(2,1)}, bf16[144,512]{1,0:T(8,128)(2,1)S(1)}, u32[]{:S(2)}, u32[]{:S(2)}) collective-permute-start(bf16[144,512]{1,0:T(8,128)(2,1)} %get-tuple-element.36), channel_id=1, source_target_pairs={{0,176},{16,192},{32,208},{48,224},{64,240},{80,0},{96,16},{112,32... | collective-permute-start | bytes 442376 | tf_op jit(solution)/shard_map/ppermute | solution.py:385
  98.5 14.4 %collective-permute-start.11 = (bf16[144,512]{1,0:T(8,128)(2,1)}, bf16[144,512]{1,0:T(8,128)(2,1)S(1)}, u32[]{:S(2)}, u32[]{:S(2)}) collective-permute-start(bf16[144,512]{1,0:T(8,128)(2,1)} %get-tuple-element.37), channel_id=1, source_target_pairs={{0,192},{16,208},{32,224},{48,240},{64,0},{80,16},{96,32},{112,48}... | collective-permute-start | bytes 442376 | tf_op jit(solution)/shard_map/ppermute | solution.py:385
  101.4 11.5 %collective-permute-start.12 = (bf16[144,512]{1,0:T(8,128)(2,1)}, bf16[144,512]{1,0:T(8,128)(2,1)S(1)}, u32[]{:S(2)}, u32[]{:S(2)}) collective-permute-start(bf16[144,512]{1,0:T(8,128)(2,1)} %get-tuple-element.38), channel_id=1, source_target_pairs={{0,208},{16,224},{32,240},{48,0},{64,16},{80,32},{96,48},{112,64},... | collective-permute-start | bytes 442376 | tf_op jit(solution)/shard_map/ppermute | solution.py:385
  108.1 5.7 %collective-permute-start.13 = (bf16[144,512]{1,0:T(8,128)(2,1)}, bf16[144,512]{1,0:T(8,128)(2,1)S(1)}, u32[]{:S(2)}, u32[]{:S(2)}) collective-permute-start(bf16[144,512]{1,0:T(8,128)(2,1)} %get-tuple-element.39), channel_id=1, source_target_pairs={{0,224},{16,240},{32,0},{48,16},{64,32},{80,48},{96,64},{112,80},{... | collective-permute-start | bytes 442376 | tf_op jit(solution)/shard_map/ppermute | solution.py:385
  108.1 6.3 %collective-permute-start.14 = (bf16[144,512]{1,0:T(8,128)(2,1)}, bf16[144,512]{1,0:T(8,128)(2,1)S(1)}, u32[]{:S(2)}, u32[]{:S(2)}) collective-permute-start(bf16[144,512]{1,0:T(8,128)(2,1)} %get-tuple-element.40), channel_id=1, source_target_pairs={{0,240},{16,0},{32,16},{48,32},{64,48},{80,64},{96,80},{112,96},{1... | collective-permute-start | bytes 442376 | tf_op jit(solution)/shard_map/ppermute | solution.py:385
  (13 other events, 108.5 us)

commit v3 on v2

--- a/solution.py
+++ b/solution.py
@@ -37,54 +37,111 @@
     return compare(row_layer, column_layer)
 
 
-def spread_kernel(
-    sizes, p_ref, wv_ref, wo_ref, gain_ref, x_ref, cot_ref, weight_ref, *out_refs
+def pack_kernel(
+    sizes,
+    here_ref,
+    tenant_ref,
+    valid_ref,
+    wv_ref,
+    wo_ref,
+    gain_ref,
+    x_ref,
+    cot_ref,
+    vd_ref,
+    ou_ref,
+    vu_ref,
+    od_ref,
+    stored_ref,
+    *out_refs
 ):
     layers, hd, rank, tokens, cols = sizes
     rows = tokens // layers
-    section = p_ref[0]
-    for step, out_ref in enumerate(out_refs):
-        at = pl.ds(pl.multiple_of(lax.rem(section + step, layers) * cols, cols), cols)
-        out_ref[:hd, :] = (wv_ref[:, at].astype(jnp.float32) * gain_ref[:, at]).astype(jnp.bfloat16)
-        out_ref[hd : 2 * hd, :] = wo_ref[:, at]
-        seeded = cot_ref[:, at].astype(jnp.float32) * weight_ref[...]
-        out_ref[2 * hd :, :] = jnp.concatenate(
-            [x_ref[:, at].astype(jnp.float32), seeded], axis=0
-        ).astype(jnp.bfloat16)
-
-
-def store_kernel(sizes, vd_ref, ou_ref, gain_ref, vu_ref, od_ref, out_ref):
-    layers, hd, rank, tokens, cols = sizes
+    part = hd // 2
+    section, member = here_ref[0], here_ref[1]
+    side = len(out_refs)
+    across = layers // side
+    mine = pl.ds(pl.multiple_of(lax.rem(member, 2) * part, part), part)
+    own = tenant_ref[member]
+    total = jnp.int32(0)
+    for i in range(tenant_ref.shape[0]):
+        total = total + jnp.where(tenant_ref[i] == own, valid_ref[i], 0)
+    position = section * rows + lax.broadcasted_iota(jnp.int32, (rows, 1), 0)
+    weight = jnp.where(position < valid_ref[member], 1.0, 0.0).astype(jnp.float32)
+    weight = weight / jnp.full((rows, 1), total, jnp.int32).astype(jnp.float32)
     small = jnp.concatenate([vu_ref[...], od_ref[...]], axis=1)
-    for k in range(out_ref.shape[0]):
+    for k in range(stored_ref.shape[0]):
         at = pl.ds(k * cols, cols)
-        out_ref[k, :, :cols] = (vd_ref[:, at].astype(jnp.float32) * gain_ref[:, at]).astype(
+        stored_ref[k, :, :cols] = (vd_ref[:, at].astype(jnp.float32) * gain_ref[:, at]).astype(
             jnp.bfloat16
         )
-        out_ref[k, :, cols : 2 * cols] = ou_ref[:, at]
-        out_ref[k, :, 2 * cols :] = small
-
-
-def gram_kernel(sizes, p_ref, *refs):
-    layers, hd, rank, tokens, cols = sizes
+        stored_ref[k, :, cols : 2 * cols] = ou_ref[:, at]
+        stored_ref[k, :, 2 * cols :] = small
+    own_line = section // across
+    for step, out_ref in enumerate(out_refs):
+        line = lax.rem(own_line + step, side)
+        for k in range(across):
+            at = pl.ds(pl.multiple_of((line * across + k) * cols, cols), cols)
+            out_ref[k, :part, :] = (wv_ref[mine, at].astype(jnp.float32) * gain_ref[:, at]).astype(
+                jnp.bfloat16
+            )
+            out_ref[k, part:hd, :] = wo_ref[mine, at]
+            seeded = cot_ref[:, at].astype(jnp.float32) * weight
+            out_ref[k, hd:, :] = jnp.concatenate(
+                [x_ref[:, at].astype(jnp.float32), seeded], axis=0
+            ).astype(jnp.bfloat16)
+
+
+def pick_kernel(side, across, here_ref, tenant_ref, slot_ref, parts_ref, *refs):
+    lines, out_ref, turned = refs[:side], refs[side], refs[side + 1 :]
+    for j in range(out_ref.shape[0]):
+        out_ref[j] = parts_ref[slot_ref[tenant_ref[j]]]
+    place = lax.rem(here_ref[0], across)
+    for step, turned_ref in enumerate(turned):
+        at = lax.rem(place + step, across)
+        for k in range(side):
+            turned_ref[k] = lines[k][at]
+
+
+def finish_kernel(sizes, owned_ref, gain_ref, gvd_ref, gvu_ref, god_ref, gou_ref):
+    layers, hd, rank, tokens, cols = sizes
+    tail = jnp.zeros((rank, 2 * hd), jnp.float32)
+    for c in range(layers):
+        at = pl.ds(c * cols, cols)
+        gvd_ref[:, at] = (owned_ref[c, :, :cols].astype(jnp.float32) * gain_ref[:, at]).astype(
+            jnp.bfloat16
+        )
+        gou_ref[:, at] = owned_ref[c, :, cols : 2 * cols]
+        tail = tail + owned_ref[c, :, 2 * cols :].astype(jnp.float32)
+    gvu_ref[...] = tail[:, :hd].astype(jnp.bfloat16)
+    god_ref[...] = tail[:, hd:].astype(jnp.bfloat16)
+
+
+def gram_kernel(sizes, side, across, here_ref, *refs):
+    layers, hd, rank, tokens, cols = sizes
+    own_refs, other_refs, refs = refs[:across], refs[across : 2 * across], refs[2 * across :]
+    q_ref, u_ref, v_ref, x_ref, s_ref, out_ref, x_wide, s_wide, w_wide = refs
     rows = tokens // layers
-    w_refs = refs[:layers]
-    q_ref, u_ref, v_ref, x_ref, s_ref, out_ref, x_wide, s_wide = refs[layers:]
-    section = p_ref[0]
-    for step, w_ref in enumerate(w_refs):
-        l = lax.rem(section + layers - step, layers)
+    part = hd // 2
+    section, core = here_ref[0], lax.rem(here_ref[1], 2)
+    line, place = section // across, lax.rem(section, across)
+    mine = pl.ds(pl.multiple_of(core * part, part), part)
+    theirs = pl.ds(pl.multiple_of((1 - core) * part, part), part)
+    for step in range(layers):
+        dx, dy = step // side, step % side
+        l = lax.rem(line + side - dy, side) * across + lax.rem(place + across - dx, across)
+        slot = step % 2
+        for kind in range(2):
+            at = pl.ds(kind * part, part)
+            w_wide[slot, kind, mine, :] = own_refs[dx][dy, at, :].astype(jnp.float32)
+            w_wide[slot, kind, theirs, :] = other_refs[dx][dy, at, :].astype(jnp.float32)
         q_l = q_ref[l]
         small = q_l[:, 2 * cols : 2 * cols + 2 * hd]
         delta_v = mm_tn(small[:, :hd], q_l[:, :cols])
         delta_u = mm_tn(small[:, hd:], q_l[:, cols : 2 * cols])
         at = pl.ds(pl.multiple_of(l * hd, hd), hd)
-        v_ref[at, :] = (w_ref[:hd, :].astype(jnp.float32) + adapter_scale * delta_v).astype(
-            jnp.bfloat16
-        )
-        u_ref[at, :] = (w_ref[hd : 2 * hd, :].astype(jnp.float32) + adapter_scale * delta_u).astype(
-            jnp.bfloat16
-        )
-        both = w_ref[2 * hd :, :].astype(jnp.float32)
+        v_ref[at, :] = (w_wide[slot, 0] + adapter_scale * delta_v).astype(jnp.bfloat16)
+        u_ref[at, :] = (w_wide[slot, 1] + adapter_scale * delta_u).astype(jnp.bfloat16)
+        both = own_refs[dx][dy, hd:, :].astype(jnp.float32)
         at = pl.ds(pl.multiple_of(l * rows, rows), rows)
         x_wide[at, :] = both[:rows]
         s_wide[at, :] = both[rows:]
@@ -249,34 +306,70 @@
     return [pl.BlockSpec(memory_space=pltpu.VMEM)] * count
 
 
-def spread(sizes, section, w_value, w_out, gain, x, cotangent, weight):
-    layers, hd, rank, tokens, cols = sizes
-    shape = jax.ShapeDtypeStruct((2 * hd + 2 * (tokens // layers), cols), jnp.bfloat16)
+def in_smem(count):
+    return [pl.BlockSpec(memory_space=pltpu.SMEM)] * count
+
+
+def pack(sizes, side, members, scalars, arrays):
+    layers, hd, rank, tokens, cols = sizes
+    line = jax.ShapeDtypeStruct(
+        (layers // side, hd + 2 * (tokens // layers), cols), jnp.bfloat16
+    )
+    stored = jax.ShapeDtypeStruct((members, rank, 2 * cols + 2 * hd), jnp.bfloat16)
     return pl.pallas_call(
-        functools.partial(spread_kernel, sizes),
-        out_shape=(shape,) * layers,
-        in_specs=[pl.BlockSpec(memory_space=pltpu.SMEM)] + in_vmem(6),
-        out_specs=tuple(in_vmem(layers)),
+        functools.partial(pack_kernel, sizes),
+        out_shape=(stored,) + (line,) * side,
+        in_specs=in_smem(len(scalars)) + in_vmem(len(arrays)),
+        out_specs=tuple(in_vmem(1 + side)),
         compiler_params=params(),
-    )(section, w_value, w_out, gain, x, cotangent, weight)
-
-
-def store(sizes, members, value_down, output_up, gain, value_up, out_down):
-    layers, hd, rank, tokens, cols = sizes
+    )(*scalars, *arrays)
+
+
+def pick_rows(scalars, parts, lines):
+    side = len(lines)
+    across = lines[0].shape[0]
+    turned = jax.ShapeDtypeStruct((side,) + lines[0].shape[1:], jnp.bfloat16)
     return pl.pallas_call(
-        functools.partial(store_kernel, sizes),
-        out_shape=jax.ShapeDtypeStruct((members, rank, 2 * cols + 2 * hd), jnp.bfloat16),
-        in_specs=in_vmem(5),
-        out_specs=in_vmem(1)[0],
+        functools.partial(pick_kernel, side, across),
+        out_shape=(jax.ShapeDtypeStruct(parts.shape, parts.dtype),) + (turned,) * across,
+        in_specs=in_smem(len(scalars)) + in_vmem(1 + side),
+        out_specs=tuple(in_vmem(1 + across)),
         compiler_params=params(),
-    )(value_down, output_up, gain, value_up, out_down)
-
-
-def gram(sizes, section, blocks, q):
+    )(*scalars, parts, *lines)
+
+
+def relay_kernel(*refs):
+    pass
+
+
+def relay(value, after):
+    return pl.pallas_call(
+        relay_kernel,
+        out_shape=jax.ShapeDtypeStruct(value.shape, value.dtype),
+        in_specs=[pl.BlockSpec(memory_space=pl.ANY)] * (1 + len(after)),
+        out_specs=pl.BlockSpec(memory_space=pl.ANY),
+        input_output_aliases={0: 0},
+    )(value, *after)
+
+
+def finish(sizes, owned, gain):
+    layers, hd, rank, tokens, cols = sizes
+    wide = jax.ShapeDtypeStruct((rank, layers * cols), jnp.bfloat16)
+    narrow = jax.ShapeDtypeStruct((rank, hd), jnp.bfloat16)
+    return pl.pallas_call(
+        functools.partial(finish_kernel, sizes),
+        out_shape=(wide, narrow, narrow, wide),
+        in_specs=in_vmem(2),
+        out_specs=tuple(in_vmem(4)),
+        compiler_params=params(),
+    )(owned, gain)
+
+
+def gram(sizes, side, here, own, other, q):
     layers, hd, rank, tokens, cols = sizes
     width = layers * hd
     return pl.pallas_call(
-        functools.partial(gram_kernel, sizes),
+        functools.partial(gram_kernel, sizes, side, len(own)),
         out_shape=(
             jax.ShapeDtypeStruct((width, cols), jnp.bfloat16),
             jax.ShapeDtypeStruct((width, cols), jnp.bfloat16),
@@ -284,14 +377,15 @@
             jax.ShapeDtypeStruct((tokens, cols), jnp.bfloat16),
             jax.ShapeDtypeStruct((3 * tokens + width, width), jnp.bfloat16),
         ),
-        in_specs=[pl.BlockSpec(memory_space=pltpu.SMEM)] + in_vmem(layers + 1),
+        in_specs=in_smem(1) + in_vmem(2 * len(own) + 1),
         out_specs=tuple(in_vmem(5)),
         scratch_shapes=[
             pltpu.VMEM((tokens, cols), jnp.float32),
             pltpu.VMEM((tokens, cols), jnp.float32),
+            pltpu.VMEM((2, 2, hd, cols), jnp.float32),
         ],
         compiler_params=params(),
-    )(section, *blocks, q)
+    )(here, *own, *other, q)
 
 
 def solve(sizes, features, k, x, s, u, v, q):
@@ -351,43 +445,46 @@
     tenant_hot = block_tenant[:, None] == ids[None, :]
     slot_of = jnp.sum(jnp.where(tenant_hot, tenant_slot[None, :], 0), axis=1)
     slot_hot = (slot_of[:, None] == ids[None, :]).astype(jnp.bfloat16)
-    member_hot = jnp.arange(members, dtype=jnp.int32) == member
-    own_tenant = jnp.sum(jnp.where(member_hot, block_tenant, 0))
-    own_valid = jnp.sum(jnp.where(member_hot, valid_tokens, 0))
-    tenant_tokens = jnp.sum(jnp.where(block_tenant == own_tenant, valid_tokens, 0)).astype(
-        jnp.float32
-    )
-
     gain = norm_gain
-    stored = store(
+    here = jnp.stack([section, member]).astype(jnp.int32)
+    side = 4 if sections % 4 == 0 else 2
+    across = sections // side
+    stored, *lines = pack(
         sizes,
+        side,
         members,
-        value_down[0, 0],
-        output_up_factor[0, 0],
-        gain,
-        value_up_factor[0, 0],
-        out_down[0, 0],
-    )
-    position = section * rows + jnp.arange(rows, dtype=jnp.int32)
-    weight = jnp.where(position < own_valid, 1.0, 0.0).astype(jnp.float32) / tenant_tokens
-    own_section = section.astype(jnp.int32)[None]
-    blocks = spread(
-        sizes,
-        own_section,
-        w_value[0],
-        w_out[0],
-        gain,
-        inputs[0],
-        cotangent[0],
-        weight[:, None],
-    )
-    blocks = [blocks[0]] + [
-        lax.ppermute(blocks[step], "pipe", [(i, (i + step) % sections) for i in range(sections)])
-        for step in range(1, sections)
+        (here, block_tenant, valid_tokens),
+        (
+            w_value[0],
+            w_out[0],
+            gain,
+            inputs[0],
+            cotangent[0],
+            value_down[0, 0],
+            output_up_factor[0, 0],
+            value_up_factor[0, 0],
+            out_down[0, 0],
+        ),
+    )
+    lines = [lines[0]] + [
+        lax.ppermute(
+            lines[step], "pipe", [(i, (i + step * across) % sections) for i in range(sections)]
+        )
+        for step in range(1, side)
     ]
-    adapters = swap(swap(pick(slot_hot, swap(stored, "dp")), "dp"), "pipe")
-
-    u, v, x, s, partial = gram(sizes, own_section, blocks, adapters)
+    adapters, *turned = pick_rows((here, block_tenant, tenant_slot), swap(stored, "dp"), lines)
+    turned = [turned[0]] + [
+        lax.ppermute(
+            turned[step],
+            "pipe",
+            [(i, i // across * across + (i + step) % across) for i in range(sections)],
+        )
+        for step in range(1, across)
+    ]
+    adapters = swap(relay(swap(adapters, "dp"), turned[1:]), "pipe")
+    other = [lax.ppermute(part, "dp", [(i, i ^ 1) for i in range(members)]) for part in turned]
+
+    u, v, x, s, partial = gram(sizes, side, here, turned, other, adapters)
     width = partial.shape[1]
     shares = swap(partial.reshape(sections, -1, width), "pipe")
     share = jnp.sum(shares.astype(jnp.float32), axis=0).astype(jnp.bfloat16)
@@ -398,16 +495,7 @@
     by_layer = swap(grads, "dp")
     summed = pick(slot_hot.T, by_layer)
     owned = swap(swap(summed, "dp"), "pipe")
-    grad_value_down = owned[:, :, :cols].transpose(1, 0, 2).reshape(rank, features)
-    grad_value_down = (grad_value_down.astype(jnp.float32) * gain).astype(jnp.bfloat16)
-    grad_out_up = owned[:, :, cols : 2 * cols].transpose(1, 0, 2).reshape(rank, features)
-    tail = jnp.sum(owned[:, :, 2 * cols :].astype(jnp.float32), axis=0).astype(jnp.bfloat16)
-    return (
-        grad_value_down[None, None],
-        tail[None, None, :, :hd],
-        tail[None, None, :, hd:],
-        grad_out_up[None, None],
-    )
+    return tuple(part[None, None] for part in finish(sizes, owned, gain))
 
 
 def solution(mesh):

time: 294 us -> 261 us (0.89)
  blocking collectives: 144 us -> 114 us
  waiting for transfers between devices: 65.6 us -> 55.4 us
  starting transfers between devices: 36.9 us -> 46.1 us
  other arithmetic: 5.42 us -> 1.41 us
  Pallas kernels: 34.5 us -> 38.5 us
    all_to_all x5 -> x4, blocking collectives: 144 us -> 114 us  [swap(): return lax.all_to_all(value, axis, split_axis=0, concat_axis=0, tiled=True)]
    all_to_all x3 -> x4, starting transfers between devices: 21 us -> 34.4 us  [swap(): return lax.all_to_all(value, axis, split_axis=0, concat_axis=0, tiled=True)]
    all_to_all x3 -> x4, waiting for transfers between devices: 32.8 us -> 25.5 us  [swap(): return lax.all_to_all(value, axis, split_axis=0, concat_axis=0, tiled=True)]
    ppermute x15 -> x10, starting transfers between devices: 15.9 us -> 11.7 us  [the longest x3 4.99 us: body(): lax.ppermute(lines[step], 'pipe', [(i, (i + step * across) % sections) fo...]
    pallas_call x3 -> x5, Pallas kernels: 11.9 us -> 16.1 us  [the longest x1 8.23 us: gram(): pl.pallas_call(functools.partial(gram_kernel, sizes, side, len(own)), out...]
    ppermute x15 -> x10, waiting for transfers between devices: 32.7 us -> 29.8 us  [the longest x3 13.8 us: body(): lax.ppermute(lines[step], 'pipe', [(i, (i + step * across) % sections) fo...]
  transfers between devices with their start and end apart: 18 -> 14, of which waited for: 10 -> 11; matrix products, arithmetic and copies ran while one was open for 1% -> 0% of each run, Pallas kernels for 1% -> 0%
where the time goes in v3:
time: 261 us; the launch traced here: 260 us
  blocking collectives  114 us (44%)
  waiting for transfers between devices  55.4 us (21%)
  starting transfers between devices  46.1 us (18%)
  Pallas kernels  38.5 us (15%)
  local copies, waits for them, and re-layouts  4.03 us (2%)
    all_to_all x4, blocking collectives, swap(): return lax.all_to_all(value, axis, split_axis=0, concat_axis=0, tiled=True)  114 us
    all_to_all x4, starting transfers between devices, swap(): return lax.all_to_all(value, axis, split_axis=0, concat_axis=0, tiled=True)  34.4 us
    all_to_all x4, waiting for transfers between devices, swap(): return lax.all_to_all(value, axis, split_axis=0, concat_axis=0, tiled=True)  25.5 us
    pallas_call x1, Pallas kernels, solve(): pl.pallas_call(functools.partial(solve_kernel, sizes, features), out_shap...  22.4 us
    ppermute x3, waiting for transfers between devices, body(): lax.ppermute(lines[step], 'pipe', [(i, (i + step * across) % sections) fo...  13.8 us
    ppermute x3, waiting for transfers between devices, body(): lax.ppermute(turned[step], 'pipe', [(i, i // across * across + (i + step)...  13.8 us
    pallas_call x1, Pallas kernels, gram(): pl.pallas_call(functools.partial(gram_kernel, sizes, side, len(own)), out...  8.23 us
  transfers between devices with their start and end apart: 14, of which 11 were waited for; matrix products, arithmetic and copies ran while one was open for 0% of the time, Pallas kernels for 0%

profile of v3, /device:TPU:1, one launch (start us, length us, event | category | flops | bytes accessed | tf_op | source)
XLA Modules:
  0.0 260.1 jit_solution(1694946458956117596)
XLA Ops:
  1.3 3.1 %shard_map.147 = (bf16[16,16,1152]{2,1,0:T(8,128)(2,1)}, bf16[4,80,512]{2,1,0:T(8,128)(2,1)}, bf16[4,80,512]{2,1,0:T(8,128)(2,1)}, bf16[4,80,512]{2,1,0:T(8,128)(2,1)}, bf16[4,80,512]{2,1,0:T(8,128)(2,1)}) custom-call(s32[2]{0:T(128)} %pad_add_fusion.here_ref, s32[16]{0:T(128)} %tenant_ref.3, s32[16]{0:T(128)} %valid_ref.1, bf16[64,8192]{1,0:T(8,128)(2,1)} %bitcast.27, ...), custom_call_target="tpu_custom_call" | custom-call | tf_op jit(solution)/shard_map/pallas_call | solution.py:319
  4.4 10.0 %all-to-all-start = ((bf16[16,16,1152]{2,1,0:T(8,128)(2,1)}), bf16[16,16,1152]{2,1,0:T(8,128)(2,1)S(1)}, u32[]{:S(2)}, u32[]{:S(2)}) async-start(bf16[16,16,1152]{2,1,0:T(8,128)(2,1)} %get-tuple-element.23), calls=%async_computation | async-start | bytes 1179648 | tf_op jit(solution)/shard_map/all_to_all | solution.py:412
  14.4 1.3 collective-permute-start
  15.7 2.6 %collective-permute-start.1 = (bf16[4,80,512]{2,1,0:T(8,128)(2,1)}, bf16[4,80,512]{2,1,0:T(8,128)(2,1)S(1)}, u32[]{:S(2)}, u32[]{:S(2)}) collective-permute-start(bf16[4,80,512]{2,1,0:T(8,128)(2,1)} %get-tuple-element.26), channel_id=1, source_target_pairs={{0,128},{16,144},{32,160},{48,176},{64,192},{80,208},{96,224},{112... | collective-permute-start | bytes 983048 | tf_op jit(solution)/shard_map/ppermute | solution.py:470
  19.4 5.7 %collective-permute-done.refs_1_ = bf16[4,80,512]{2,1,0:T(8,128)(2,1)S(1)} collective-permute-done((bf16[4,80,512]{2,1,0:T(8,128)(2,1)}, bf16[4,80,512]{2,1,0:T(8,128)(2,1)S(1)}, u32[]{:S(2)}, u32[]{:S(2)}) %collective-permute-start) | collective-permute-done | bytes 327712 | tf_op jit(solution)/shard_map/ppermute | solution.py:470
  25.1 8.1 %collective-permute-done.1.refs_2_ = bf16[4,80,512]{2,1,0:T(8,128)(2,1)S(1)} collective-permute-done((bf16[4,80,512]{2,1,0:T(8,128)(2,1)}, bf16[4,80,512]{2,1,0:T(8,128)(2,1)S(1)}, u32[]{:S(2)}, u32[]{:S(2)}) %collective-permute-start.1) | collective-permute-done | bytes 327712 | tf_op jit(solution)/shard_map/ppermute | solution.py:470
  34.3 2.9 %shard_map.148 = (bf16[16,16,1152]{2,1,0:T(8,128)(2,1)}, bf16[4,80,512]{2,1,0:T(8,128)(2,1)}, bf16[4,80,512]{2,1,0:T(8,128)(2,1)}, bf16[4,80,512]{2,1,0:T(8,128)(2,1)}, bf16[4,80,512]{2,1,0:T(8,128)(2,1)}) custom-call(s32[2]{0:T(128)} %pad_add_fusion.here_ref, s32[16]{0:T(128)} %tenant_ref.3, s32[16]{0:T(128)} %slot_ref.1, bf16[16,16,1152]{2,1,0:T(8,128)(2,1)} %copy-done.2, ...), custom_call_target="tpu_custom_call" | custom-call | tf_op jit(solution)/shard_map/pallas_call | solution.py:332
  37.1 8.0 %all-to-all-start.1 = ((bf16[16,16,1152]{2,1,0:T(8,128)(2,1)}), bf16[16,16,1152]{2,1,0:T(8,128)(2,1)S(1)}, u32[]{:S(2)}, u32[]{:S(2)}) async-start(bf16[16,16,1152]{2,1,0:T(8,128)(2,1)} %get-tuple-element.32), calls=%async_computation.1 | async-start | bytes 1179648 | tf_op jit(solution)/shard_map/all_to_all | solution.py:412
  45.1 1.2 collective-permute-start.3
  46.3 2.5 collective-permute-start.4
  49.9 5.7 %collective-permute-done.3.refs_1_ = bf16[4,80,512]{2,1,0:T(8,128)(2,1)S(1)} collective-permute-done((bf16[4,80,512]{2,1,0:T(8,128)(2,1)}, bf16[4,80,512]{2,1,0:T(8,128)(2,1)S(1)}, u32[]{:S(2)}, u32[]{:S(2)}) %collective-permute-start.3) | collective-permute-done | bytes 327712 | tf_op jit(solution)/shard_map/ppermute | solution.py:477
  55.7 8.0 %collective-permute-done.4.refs_2_ = bf16[4,80,512]{2,1,0:T(8,128)(2,1)S(1)} collective-permute-done((bf16[4,80,512]{2,1,0:T(8,128)(2,1)}, bf16[4,80,512]{2,1,0:T(8,128)(2,1)S(1)}, u32[]{:S(2)}, u32[]{:S(2)}) %collective-permute-start.4) | collective-permute-done | bytes 327712 | tf_op jit(solution)/shard_map/ppermute | solution.py:477
  65.4 5.6 %all-to-all-start.2 = ((bf16[16,16,1152]{2,1,0:T(8,128)(2,1)}), bf16[16,16,1152]{2,1,0:T(8,128)(2,1)S(1)}, u32[]{:S(2)}, u32[]{:S(2)}) async-start(bf16[16,16,1152]{2,1,0:T(8,128)(2,1)} %shard_map.149), calls=%async_computation.2 | async-start | bytes 1179648 | tf_op jit(solution)/shard_map/all_to_all | solution.py:412
  71.0 1.3 collective-permute-start.6
  75.2 7.0 %all-to-all-done.2.refs_8_.q_ref = bf16[16,16,1152]{2,1,0:T(8,128)(2,1)S(1)} async-done(((bf16[16,16,1152]{2,1,0:T(8,128)(2,1)}), bf16[16,16,1152]{2,1,0:T(8,128)(2,1)S(1)}, u32[]{:S(2)}, u32[]{:S(2)}) %all-to-all-start.2) | async-done | bytes 589856 | tf_op jit(solution)/shard_map/all_to_all | solution.py:412
  83.0 8.2 %shard_map.150 = (bf16[1024,512]{1,0:T(8,128)(2,1)}, bf16[1024,512]{1,0:T(8,128)(2,1)}, bf16[128,512]{1,0:T(8,128)(2,1)}, bf16[128,512]{1,0:T(8,128)(2,1)}, bf16[1408,1024]{1,0:T(8,128)(2,1)}) custom-call(s32[2]{0:T(128)} %pad_add_fusion.here_ref, bf16[4,80,512]{2,1,0:T(8,128)(2,1)} %get-tuple-element.28.refs_0_, bf16[4,80,512]{2,1,0:T(8,128)(2,1)} %copy-done.3, ...), custom_call_target="tpu_custom_call" | custom-call | tf_op jit(solution)/shard_map/pallas_call | solution.py:371
  91.3 39.1 %all_to_all.40 = bf16[16,88,1024]{2,1,0:T(8,128)(2,1)S(1)} all-to-all(bf16[16,88,1024]{2,1,0:T(8,128)(2,1)} %bitcast.22), channel_id=1, replica_groups=mesh['pipe'=16,'dp'=16] {'pipe'}, dimensions={0} | all-to-all | bytes 5767168 | tf_op jit(solution)/shard_map/all_to_all | solution.py:412
  131.3 37.3 %all_to_all.41 = bf16[16,88,1024]{2,1,0:T(8,128)(2,1)} all-to-all(bf16[16,88,1024]{2,1,0:T(8,128)(2,1)S(1)} %broadcast_in_dim.37), channel_id=1, replica_groups=mesh['pipe'=16,'dp'=16] {'pipe'}, dimensions={0} | all-to-all | bytes 5767168 | tf_op jit(solution)/shard_map/all_to_all | solution.py:412
  168.6 22.4 %shard_map.151 = bf16[16,16,1152]{2,1,0:T(8,128)(2,1)} custom-call(bf16[1408,1024]{1,0:T(8,128)(2,1)} %bitcast.21, bf16[128,512]{1,0:T(8,128)(2,1)} %get-tuple-element.34.x_ref, bf16[128,512]{1,0:T(8,128)(2,1)} %get-tuple-element.35.s_ref, bf16[1024,512]{1,0:T(8,128)(2,1)} %get-tuple-element.36.u_ref, bf16[1024,512]{1,0:T(8,128)(2,1)} %get-tuple-element.37.v_ref, ...), custom_call_target="tpu_custom_call" | custom-call | tf_op jit(solution)/shard_map/pallas_call | solution.py:394
  191.0 10.8 %all-to-all-start.5 = ((bf16[16,16,1152]{2,1,0:T(8,128)(2,1)}), bf16[16,16,1152]{2,1,0:T(8,128)(2,1)S(1)}, u32[]{:S(2)}, u32[]{:S(2)}) async-start(bf16[16,16,1152]{2,1,0:T(8,128)(2,1)} %shard_map.151), calls=%async_computation.5 | async-start | bytes 1179648 | tf_op jit(solution)/shard_map/all_to_all | solution.py:412
  202.0 18.5 %all-to-all-done.5 = bf16[16,16,1152]{2,1,0:T(8,128)(2,1)S(1)} async-done(((bf16[16,16,1152]{2,1,0:T(8,128)(2,1)}), bf16[16,16,1152]{2,1,0:T(8,128)(2,1)S(1)}, u32[]{:S(2)}, u32[]{:S(2)}) %all-to-all-start.5) | async-done | bytes 589856 | tf_op jit(solution)/shard_map/all_to_all | solution.py:412
  221.1 21.7 %all_to_all.42 = bf16[16,16,1152]{2,1,0:T(8,128)(2,1)S(1)} all-to-all(bf16[16,16,1152]{2,1,0:T(8,128)(2,1)S(1)} %bitcast.26), channel_id=1, replica_groups=mesh['pipe'=16,'dp'=16] {'dp'}, dimensions={0} | all-to-all | bytes 1179648 | tf_op jit(solution)/shard_map/all_to_all | solution.py:412
  242.8 15.5 %all_to_all.43.owned_ref = bf16[16,16,1152]{2,1,0:T(8,128)(2,1)} all-to-all(bf16[16,16,1152]{2,1,0:T(8,128)(2,1)S(1)} %all_to_all.42), channel_id=1, replica_groups=mesh['pipe'=16,'dp'=16] {'pipe'}, dimensions={0} | all-to-all | bytes 1179648 | tf_op jit(solution)/shard_map/all_to_all | solution.py:412
  258.2 1.9 shard_map.152
  (53 shorter events, 11.0 us)
Async XLA Ops:
  4.4 28.8 %all-to-all-start = ((bf16[16,16,1152]{2,1,0:T(8,128)(2,1)}), bf16[16,16,1152]{2,1,0:T(8,128)(2,1)S(1)}, u32[]{:S(2)}, u32[]{:S(2)}) async-start(bf16[16,16,1152]{2,1,0:T(8,128)(2,1)} %get-tuple-element.23), calls=%async_computation | async-start | bytes 1179648 | tf_op jit(solution)/shard_map/all_to_all | solution.py:412
  14.4 10.7 %collective-permute-start = (bf16[4,80,512]{2,1,0:T(8,128)(2,1)}, bf16[4,80,512]{2,1,0:T(8,128)(2,1)S(1)}, u32[]{:S(2)}, u32[]{:S(2)}) collective-permute-start(bf16[4,80,512]{2,1,0:T(8,128)(2,1)} %get-tuple-element.25), channel_id=1, source_target_pairs={{0,64},{16,80},{32,96},{48,112},{64,128},{80,144},{96,160},{112,17... | collective-permute-start | bytes 983048 | tf_op jit(solution)/shard_map/ppermute | solution.py:470
  15.7 17.5 %collective-permute-start.1 = (bf16[4,80,512]{2,1,0:T(8,128)(2,1)}, bf16[4,80,512]{2,1,0:T(8,128)(2,1)S(1)}, u32[]{:S(2)}, u32[]{:S(2)}) collective-permute-start(bf16[4,80,512]{2,1,0:T(8,128)(2,1)} %get-tuple-element.26), channel_id=1, source_target_pairs={{0,128},{16,144},{32,160},{48,176},{64,192},{80,208},{96,224},{112... | collective-permute-start | bytes 983048 | tf_op jit(solution)/shard_map/ppermute | solution.py:470
  18.3 14.9 %collective-permute-start.2 = (bf16[4,80,512]{2,1,0:T(8,128)(2,1)}, bf16[4,80,512]{2,1,0:T(8,128)(2,1)S(1)}, u32[]{:S(2)}, u32[]{:S(2)}) collective-permute-start(bf16[4,80,512]{2,1,0:T(8,128)(2,1)} %get-tuple-element.27), channel_id=1, source_target_pairs={{0,192},{16,208},{32,224},{48,240},{64,0},{80,16},{96,32},{112,48}... | collective-permute-start | bytes 983048 | tf_op jit(solution)/shard_map/ppermute | solution.py:470
  25.1 8.2 %copy-start.9 = (bf16[4,80,512]{2,1,0:T(8,128)(2,1)}, bf16[4,80,512]{2,1,0:T(8,128)(2,1)S(1)}, u32[]{:S(2)}) copy-start(bf16[4,80,512]{2,1,0:T(8,128)(2,1)S(1)} %collective-permute-done.refs_1_) | copy-start | bytes 983044
  33.2 1.0 copy-start.2
  37.1 33.9 %copy-start.6 = (bf16[4,80,512]{2,1,0:T(8,128)(2,1)S(1)}, bf16[4,80,512]{2,1,0:T(8,128)(2,1)}, u32[]{:S(2)}) copy-start(bf16[4,80,512]{2,1,0:T(8,128)(2,1)} %get-tuple-element.28.refs_0_) | copy-start | bytes 983044
  37.1 26.6 %all-to-all-start.1 = ((bf16[16,16,1152]{2,1,0:T(8,128)(2,1)}), bf16[16,16,1152]{2,1,0:T(8,128)(2,1)S(1)}, u32[]{:S(2)}, u32[]{:S(2)}) async-start(bf16[16,16,1152]{2,1,0:T(8,128)(2,1)} %get-tuple-element.32), calls=%async_computation.1 | async-start | bytes 1179648 | tf_op jit(solution)/shard_map/all_to_all | solution.py:412
  45.1 10.6 %collective-permute-start.3 = (bf16[4,80,512]{2,1,0:T(8,128)(2,1)}, bf16[4,80,512]{2,1,0:T(8,128)(2,1)S(1)}, u32[]{:S(2)}, u32[]{:S(2)}) collective-permute-start(bf16[4,80,512]{2,1,0:T(8,128)(2,1)} %get-tuple-element.29), channel_id=1, source_target_pairs={{0,16},{16,32},{32,48},{48,0},{64,80},{80,96},{96,112},{112,64},{1... | collective-permute-start | bytes 983048 | tf_op jit(solution)/shard_map/ppermute | solution.py:477
  46.3 17.4 %collective-permute-start.4 = (bf16[4,80,512]{2,1,0:T(8,128)(2,1)}, bf16[4,80,512]{2,1,0:T(8,128)(2,1)S(1)}, u32[]{:S(2)}, u32[]{:S(2)}) collective-permute-start(bf16[4,80,512]{2,1,0:T(8,128)(2,1)} %get-tuple-element.30), channel_id=1, source_target_pairs={{0,32},{16,48},{32,0},{48,16},{64,96},{80,112},{96,64},{112,80},{1... | collective-permute-start | bytes 983048 | tf_op jit(solution)/shard_map/ppermute | solution.py:477
  48.8 14.9 %collective-permute-start.5 = (bf16[4,80,512]{2,1,0:T(8,128)(2,1)}, bf16[4,80,512]{2,1,0:T(8,128)(2,1)S(1)}, u32[]{:S(2)}, u32[]{:S(2)}) collective-permute-start(bf16[4,80,512]{2,1,0:T(8,128)(2,1)} %get-tuple-element.31), channel_id=1, source_target_pairs={{0,48},{16,0},{32,16},{48,32},{64,112},{80,64},{96,80},{112,96},{1... | collective-permute-start | bytes 983048 | tf_op jit(solution)/shard_map/ppermute | solution.py:477
  55.7 8.1 %copy-start.3 = (bf16[4,80,512]{2,1,0:T(8,128)(2,1)}, bf16[4,80,512]{2,1,0:T(8,128)(2,1)S(1)}, u32[]{:S(2)}) copy-start(bf16[4,80,512]{2,1,0:T(8,128)(2,1)S(1)} %collective-permute-done.3.refs_1_) | copy-start | bytes 983044
  65.4 16.8 %all-to-all-start.2 = ((bf16[16,16,1152]{2,1,0:T(8,128)(2,1)}), bf16[16,16,1152]{2,1,0:T(8,128)(2,1)S(1)}, u32[]{:S(2)}, u32[]{:S(2)}) async-start(bf16[16,16,1152]{2,1,0:T(8,128)(2,1)} %shard_map.149), calls=%async_computation.2 | async-start | bytes 1179648 | tf_op jit(solution)/shard_map/all_to_all | solution.py:412
  71.0 2.5 collective-permute-start.6
  72.3 1.9 collective-permute-start.7
  72.4 2.3 collective-permute-start.8
  72.8 2.4 collective-permute-start.9
  73.5 8.6 %copy-start.7 = (bf16[4,80,512]{2,1,0:T(8,128)(2,1)}, bf16[4,80,512]{2,1,0:T(8,128)(2,1)S(1)}, u32[]{:S(2)}) copy-start(bf16[4,80,512]{2,1,0:T(8,128)(2,1)S(1)} %collective-permute-done.6.refs_4_) | copy-start | bytes 983044
  74.2 7.9 %copy-start.8 = (bf16[4,80,512]{2,1,0:T(8,128)(2,1)}, bf16[4,80,512]{2,1,0:T(8,128)(2,1)S(1)}, u32[]{:S(2)}) copy-start(bf16[4,80,512]{2,1,0:T(8,128)(2,1)S(1)} %collective-permute-done.7.refs_5_) | copy-start | bytes 983044
  74.7 7.5 %copy-start.10 = (bf16[4,80,512]{2,1,0:T(8,128)(2,1)}, bf16[4,80,512]{2,1,0:T(8,128)(2,1)S(1)}, u32[]{:S(2)}) copy-start(bf16[4,80,512]{2,1,0:T(8,128)(2,1)S(1)} %collective-permute-done.8.refs_6_) | copy-start | bytes 983044
  75.1 7.0 %copy-start.12 = (bf16[4,80,512]{2,1,0:T(8,128)(2,1)}, bf16[4,80,512]{2,1,0:T(8,128)(2,1)S(1)}, u32[]{:S(2)}) copy-start(bf16[4,80,512]{2,1,0:T(8,128)(2,1)S(1)} %collective-permute-done.9.refs_7_) | copy-start | bytes 983044
  168.6 33.2 %copy-start.14 = (s32[16]{0:T(128)S(1)}, s32[16]{0:T(128)}, u32[]{:S(2)}) copy-start(s32[16]{0:T(128)} %tenant_ref.3) | copy-start | bytes 196
  168.6 33.2 %copy-start.15 = (s32[16]{0:T(128)S(1)}, s32[16]{0:T(128)}, u32[]{:S(2)}) copy-start(s32[16]{0:T(128)} %slot_ref.1) | copy-start | bytes 196
  191.0 29.5 %all-to-all-start.5 = ((bf16[16,16,1152]{2,1,0:T(8,128)(2,1)}), bf16[16,16,1152]{2,1,0:T(8,128)(2,1)S(1)}, u32[]{:S(2)}, u32[]{:S(2)}) async-start(bf16[16,16,1152]{2,1,0:T(8,128)(2,1)} %shard_map.151), calls=%async_computation.5 | async-start | bytes 1179648 | tf_op jit(solution)/shard_map/all_to_all | solution.py:412
  (6 other events, 4.9 us)

commit v4 on v3

v4 whole, which is shorter than its diff:
```python
import functools

import jax
import jax.numpy as jnp
from jax import lax
from jax.experimental import pallas as pl
from jax.experimental.pallas import tpu as pltpu
from jax.sharding import PartitionSpec as P

adapter_scale = 2.0
norm_eps = 1e-05
block = 256
vmem_bytes = 20 * 1024 * 1024
whole_vmem_bytes = 56 * 1024 * 1024
pipe = ("a", "b", "x")
dp = ("z", "core")


def mm(left, right):
    return lax.dot_general(
        left, right, (((1,), (0,)), ((), ())), preferred_element_type=jnp.float32
    )


def mm_nt(left, right):
    return lax.dot_general(
        left, right, (((1,), (1,)), ((), ())), preferred_element_type=jnp.float32
    )


def mm_tn(left, right):
    return lax.dot_general(
        left, right, (((0,), (0,)), ((), ())), preferred_element_type=jnp.float32
    )


def layer_mask(rows, columns, hd, compare):
    row_layer = lax.broadcasted_iota(jnp.int32, (rows, columns), 0) // hd
    column_layer = lax.broadcasted_iota(jnp.int32, (rows, columns), 1) // hd
    return compare(row_layer, column_layer)


def store_kernel(sizes, vd_ref, ou_ref, gain_ref, vu_ref, od_ref, out_ref):
    layers, hd, rank, tokens, cols = sizes
    small = jnp.concatenate([vu_ref[...], od_ref[...]], axis=1)
    for k in range(out_ref.shape[0]):
        at = pl.ds(k * cols, cols)
        out_ref[k, :, :cols] = (vd_ref[:, at].astype(jnp.float32) * gain_ref[:, at]).astype(
            jnp.bfloat16
        )
        out_ref[k, :, cols : 2 * cols] = ou_ref[:, at]
        out_ref[k, :, 2 * cols :] = small


def lines_kernel(
    sizes,
    here_ref,
    tenant_ref,
    valid_ref,
    wv_ref,
    wo_ref,
    gain_ref,
    x_ref,
    cot_ref,
    other_x_ref,
    other_cot_ref,
    *out_refs
):
    layers, hd, rank, tokens, cols = sizes
    rows = tokens // layers
    part = hd // 2
    section, member = here_ref[0], here_ref[1]
    core = lax.rem(member, 2)
    side = len(out_refs)
    across = layers // side
    mine = pl.ds(pl.multiple_of(lax.rem(member // 2, 2) * part, part), part)
    position = section * rows + lax.broadcasted_iota(jnp.int32, (rows, 1), 0)

    def token_weight(index):
        total = jnp.int32(0)
        for i in range(tenant_ref.shape[0]):
            total = total + jnp.where(tenant_ref[i] == tenant_ref[index], valid_ref[i], 0)
        kept = jnp.where(position < valid_ref[index], 1.0, 0.0).astype(jnp.float32)
        return kept / jnp.full((rows, 1), total, jnp.int32).astype(jnp.float32)

    own_weight = token_weight(member)
    other_weight = token_weight(member + 1 - 2 * core)
    for step, out_ref in enumerate(out_refs):
        line = lax.rem(section // across + step, side)
        own = lax.div(line, side // 2) == core
        for k in range(across):
            column = (lax.rem(line, side // 2) * across + k) * 2 + core
            at = pl.ds(pl.multiple_of(column * cols, cols), cols)
            out_ref[k, :part, :] = (wv_ref[mine, at].astype(jnp.float32) * gain_ref[:, at]).astype(
                jnp.bfloat16
            )
            out_ref[k, part:hd, :] = wo_ref[mine, at]
            x = jnp.where(
                own, x_ref[:, at].astype(jnp.float32), other_x_ref[:, at].astype(jnp.float32)
            )
            seeded = jnp.where(
                own,
                cot_ref[:, at].astype(jnp.float32) * own_weight,
                other_cot_ref[:, at].astype(jnp.float32) * other_weight,
            )
            out_ref[k, hd:, :] = jnp.concatenate([x, seeded], axis=0).astype(jnp.bfloat16)


def pick_kernel(side, across, here_ref, tenant_ref, slot_ref, parts_ref, *refs):
    lines, out_ref, turned = refs[:side], refs[side], refs[side + 1 :]
    for j in range(out_ref.shape[0]):
        out_ref[j] = parts_ref[slot_ref[tenant_ref[j]]]
    place = lax.rem(here_ref[0], across)
    for step, turned_ref in enumerate(turned):
        at = lax.rem(place + step, across)
        for k in range(side):
            turned_ref[k] = lines[k][at]


def finish_kernel(sizes, owned_ref, gain_ref, gvd_ref, gvu_ref, god_ref, gou_ref):
    layers, hd, rank, tokens, cols = sizes
    tail = jnp.zeros((rank, 2 * hd), jnp.float32)
    for c in range(layers):
        at = pl.ds(c * cols, cols)
        gvd_ref[:, at] = (owned_ref[c, :, :cols].astype(jnp.float32) * gain_ref[:, at]).astype(
            jnp.bfloat16
        )
        gou_ref[:, at] = owned_ref[c, :, cols : 2 * cols]
        tail = tail + owned_ref[c, :, 2 * cols :].astype(jnp.float32)
    gvu_ref[...] = tail[:, :hd].astype(jnp.bfloat16)
    god_ref[...] = tail[:, hd:].astype(jnp.bfloat16)


def turned_index(l, layers):
    return l % (layers // 2) * 2 + l // (layers // 2)


def gram_kernel(sizes, side, across, here_ref, *refs):
    layers, hd, rank, tokens, cols = sizes
    own_refs, other_refs, refs = refs[:across], refs[across : across + 2], refs[across + 2 :]
    pairs = across // 2
    q_ref, u_ref, v_ref, x_ref, s_ref, keep_ref, give_ref, x_wide, s_wide, w_wide = refs
    rows = tokens // layers
    part = hd // 2
    section, core = here_ref[0], lax.rem(here_ref[1], 2)
    plane = lax.rem(here_ref[1] // 2, 2)
    line, place = section // across, lax.rem(section, across)
    mine = pl.ds(pl.multiple_of(plane * part, part), part)
    theirs = pl.ds(pl.multiple_of((1 - plane) * part, part), part)
    for step in range(layers):
        dx, dy = step // side, step % side
        l = lax.rem(line + side - dy, side) * across + lax.rem(place + across - dx, across)
        slot = step % 2
        for kind in range(2):
            at = pl.ds(kind * part, part)
            w_wide[slot, kind, mine, :] = own_refs[dx][dy, at, :].astype(jnp.float32)
            w_wide[slot, kind, theirs, :] = other_refs[dx // pairs][
                dx % pairs * side + dy, at, :
            ].astype(jnp.float32)
        q_l = q_ref[turned_index(l, layers)]
        small = q_l[:, 2 * cols : 2 * cols + 2 * hd]
        delta_v = mm_tn(small[:, :hd], q_l[:, :cols])
        delta_u = mm_tn(small[:, hd:], q_l[:, cols : 2 * cols])
        at = pl.ds(pl.multiple_of(l * hd, hd), hd)
        v_ref[at, :] = (w_wide[slot, 0] + adapter_scale * delta_v).astype(jnp.bfloat16)
        u_ref[at, :] = (w_wide[slot, 1] + adapter_scale * delta_u).astype(jnp.bfloat16)
        both = own_refs[dx][dy, hd:, :].astype(jnp.float32)
        at = pl.ds(pl.multiple_of(l * rows, rows), rows)
        x_wide[at, :] = both[:rows]
        s_wide[at, :] = both[rows:]
    x_ref[...] = x_wide[...].astype(jnp.bfloat16)
    s_ref[...] = s_wide[...].astype(jnp.bfloat16)
    width = layers * hd
    base = 3 * tokens
    below = layer_mask(block, block, hd, lambda r, c: r < c)
    lane = 2 * hd
    half_count = width // lane // 2

    def put(own_core, start, column, value):
        value = value.astype(jnp.bfloat16)
        for at in range(0, value.shape[1], lane):
            index = (column + at) // lane
            out_ref = keep_ref if index // half_count == own_core else give_ref
            out_ref[index % half_count, pl.ds(start, value.shape[0]), :] = value[:, at : at + lane]

    def products(own_core):
        for bj in range(width // block):
            column = bj * block
            at_col = pl.ds(column, block)
            u_col, v_col = u_ref[at_col, :], v_ref[at_col, :]
            put(own_core, 0, column, mm_nt(x_ref[...], v_col))
            x_u = mm_nt(x_ref[...], u_col)
            if column + block == width:
                wide = x_wide[...]
                wide = wide * wide
                folded = wide[:, :lane]
                for at in range(lane, cols, lane):
                    folded = folded + wide[:, at : at + lane]
                x_u = jnp.concatenate([x_u[:, : block - hd], folded[:, :hd] + folded[:, hd:]], axis=1)
            put(own_core, tokens, column, x_u)
            put(own_core, 2 * tokens, column, mm_nt(s_ref[...], u_col))
            for bi in range(width // block):
                height = min(block, width - hd - bi * block)
                rows_at = pl.ds(bi * block, height)
                rows_u = u_ref[rows_at, :]
                if bi < bj:
                    part = mm_nt(rows_u, v_col)
                elif bi > bj:
                    part = mm_nt(rows_u, u_col)
                else:
                    part = jnp.where(below[:height], mm_nt(rows_u, v_col), mm_nt(rows_u, u_col))
                put(own_core, base + bi * block, column, part)

    for own_core in range(2):
        pl.when(core == own_core)(functools.partial(products, own_core))


def half(pair, l):
    hd = pair.shape[1] // 2
    return pair[:, hd:] if l % 2 else pair[:, :hd]


def solve_kernel(
    sizes,
    features,
    here_ref,
    own_ref,
    other_ref,
    x_ref,
    s_ref,
    u_ref,
    v_ref,
    q_ref,
    out_ref,
    c_ref,
    d_ref,
    ec_ref,
    a_ref,
    bp_ref,
    inv_ref,
    k_ref,
    sems,
):
    layers, hd, rank, tokens, cols = sizes
    width = layers * hd
    base = 3 * tokens
    half_count = own_ref.shape[0]
    core = lax.rem(here_ref[1], 2)
    copies = [
        pltpu.make_async_copy(
            source, k_ref.at[pl.ds(place * half_count, half_count)], sems.at[index]
        )
        for index, (source, place) in enumerate(((own_ref, core), (other_ref, 1 - core)))
    ]
    for copy in copies:
        copy.start()
    c_ref[...] = jnp.zeros_like(c_ref)
    d_ref[...] = jnp.zeros_like(d_ref)
    ec_ref[...] = jnp.zeros_like(ec_ref)

    def upto(l):
        return 2 * hd * ((l + 1) // 2)

    def across_row(l, start, stop):
        rows_l = pl.ds(base + l * hd, hd)
        return jnp.concatenate(
            [k_ref[index, rows_l, :] for index in range(start // (2 * hd), stop // (2 * hd))],
            axis=1,
        )

    for copy in copies:
        copy.wait()
    folded = k_ref[width // (2 * hd) - 1, tokens : 2 * tokens, :].astype(jnp.float32)[:, hd:]
    square = jnp.sum(folded, axis=1, keepdims=True)
    for l in range(layers):
        pair = l // 2
        a = half(k_ref[pair, :tokens, :], l).astype(jnp.float32)
        if l:
            w = upto(l)
            known = c_ref[:, :w]
            top = min(w, width - hd)
            a = a + half(mm(known[:, :top], k_ref[pair, base : base + top, :]), l)
        inverse = lax.rsqrt(jnp.maximum(square, 0.0) / features + norm_eps)
        c = (inverse * a).astype(jnp.bfloat16)
        c_ref[:, l * hd : (l + 1) * hd] = c
        a_ref[l] = a
        inv_ref[l] = inverse
        if l == layers - 1:
            break
        b = half(k_ref[pair, tokens : 2 * tokens, :], l).astype(jnp.float32)
        if l:
            b = b + mm_nt(known, across_row(l, 0, w))
        wide = c.astype(jnp.float32)
        after = b + half(mm(c, k_ref[pair, pl.ds(base + l * hd, hd), :]), l)
        square = square + jnp.sum(wide * (b + after), axis=1, keepdims=True)
        bp_ref[l] = after

    pull = jnp.zeros((tokens, 1), jnp.float32)
    for l in range(layers - 1, -1, -1):
        pair = l // 2
        p = half(k_ref[pair, 2 * tokens : 3 * tokens, :], l).astype(jnp.float32)
        if l < layers - 1:
            w = upto(l)
            top = width - hd
            p = p - pull * bp_ref[l]
            p = p + mm_nt(d_ref[:, w:], across_row(l, w, width))
            if w < top:
                p = p - half(mm(ec_ref[:, w:top], k_ref[pair, base + w : base + top, :]), l)
        inverse = inv_ref[l]
        d_ref[:, l * hd : (l + 1) * hd] = (inverse * p).astype(jnp.bfloat16)
        c = c_ref[:, l * hd : (l + 1) * hd].astype(jnp.float32)
        ec_ref[:, l * hd : (l + 1) * hd] = (pull * c).astype(jnp.bfloat16)
        correction = jnp.sum(p * a_ref[l], axis=1, keepdims=True) / features
        pull = pull + inverse * inverse * inverse * correction

    below = layer_mask(block, block, hd, lambda r, c: r > c)
    upto_diag = layer_mask(block, block, hd, lambda r, c: r >= c)
    blocks = width // block
    for bl in range(blocks):
        mine = pl.ds(bl * block, block)
        c_t = c_ref[:, mine].T
        d_t = d_ref[:, mine].T
        ec_t = ec_ref[:, mine].T
        y = mm(d_t, x_ref[...])
        z = mm(c_t, s_ref[...]) - mm(ec_t, x_ref[...])
        for bk in range(blocks):
            other = pl.ds(bk * block, block)
            u_k = u_ref[other, :]
            if bk <= bl:
                m = mm(d_t, c_ref[:, other])
                if bk == bl:
                    m = jnp.where(below, m, 0.0)
                y = y + mm(m.astype(jnp.bfloat16), u_k)
            if bk >= bl:
                m = mm(c_t, d_ref[:, other])
                if bk == bl:
                    m = jnp.where(upto_diag, 0.0, m)
                z = z + mm(m.astype(jnp.bfloat16), v_ref[other, :])
            if bk < bl:
                m = mm(ec_t, c_ref[:, other])
            elif bk > bl:
                m = mm(c_t, ec_ref[:, other])
            else:
                m = jnp.where(upto_diag, mm(ec_t, c_ref[:, other]), mm(c_t, ec_ref[:, other]))
            z = z - mm(m.astype(jnp.bfloat16), u_k)
        y = y.astype(jnp.bfloat16)
        z = z.astype(jnp.bfloat16)
        for j in range(block // hd):
            l = bl * (block // hd) + j
            y_l, z_l = y[j * hd : (j + 1) * hd], z[j * hd : (j + 1) * hd]
            at = turned_index(l, layers)
            small = q_ref[at, :, 2 * cols : 2 * cols + 2 * hd]
            out_ref[at, :, :cols] = (adapter_scale * mm(small[:, :hd], y_l)).astype(jnp.bfloat16)
            out_ref[at, :, cols : 2 * cols] = (adapter_scale * mm(small[:, hd:], z_l)).astype(
                jnp.bfloat16
            )
            tail = jnp.concatenate(
                [mm_nt(q_ref[at, :, :cols], y_l), mm_nt(q_ref[at, :, cols : 2 * cols], z_l)], axis=1
            )
            out_ref[at, :, 2 * cols :] = (adapter_scale * tail).astype(jnp.bfloat16)


def params(limit=vmem_bytes):
    return pltpu.CompilerParams(vmem_limit_bytes=limit)


def in_vmem(count):
    return [pl.BlockSpec(memory_space=pltpu.VMEM)] * count


def in_smem(count):
    return [pl.BlockSpec(memory_space=pltpu.SMEM)] * count


def store(sizes, members, arrays):
    layers, hd, rank, tokens, cols = sizes
    return pl.pallas_call(
        functools.partial(store_kernel, sizes),
        out_shape=jax.ShapeDtypeStruct((members, rank, 2 * cols + 2 * hd), jnp.bfloat16),
        in_specs=in_vmem(len(arrays)),
        out_specs=in_vmem(1)[0],
        compiler_params=params(whole_vmem_bytes),
    )(*arrays)


def spread_lines(sizes, side, scalars, arrays):
    layers, hd, rank, tokens, cols = sizes
    line = jax.ShapeDtypeStruct((layers // side, hd + 2 * (tokens // layers), cols), jnp.bfloat16)
    return pl.pallas_call(
        functools.partial(lines_kernel, sizes),
        out_shape=(line,) * side,
        in_specs=in_smem(len(scalars)) + in_vmem(len(arrays)),
        out_specs=tuple(in_vmem(side)),
        compiler_params=params(),
    )(*scalars, *arrays)


def pick_rows(scalars, parts, lines):
    side = len(lines)
    across = lines[0].shape[0]
    turned = jax.ShapeDtypeStruct((side,) + lines[0].shape[1:], jnp.bfloat16)
    return pl.pallas_call(
        functools.partial(pick_kernel, side, across),
        out_shape=(jax.ShapeDtypeStruct(parts.shape, parts.dtype),) + (turned,) * across,
        in_specs=in_smem(len(scalars)) + in_vmem(1 + side),
        out_specs=tuple(in_vmem(1 + across)),
        compiler_params=params(),
    )(*scalars, parts, *lines)


def relay_kernel(*refs):
    pass


def relay(value, after):
    return pl.pallas_call(
        relay_kernel,
        out_shape=jax.ShapeDtypeStruct(value.shape, value.dtype),
        in_specs=[pl.BlockSpec(memory_space=pl.ANY)] * (1 + len(after)),
        out_specs=pl.BlockSpec(memory_space=pl.ANY),
        input_output_aliases={0: 0},
    )(value, *after)


def finish(sizes, owned, gain):
    layers, hd, rank, tokens, cols = sizes
    wide = jax.ShapeDtypeStruct((rank, layers * cols), jnp.bfloat16)
    narrow = jax.ShapeDtypeStruct((rank, hd), jnp.bfloat16)
    return pl.pallas_call(
        functools.partial(finish_kernel, sizes),
        out_shape=(wide, narrow, narrow, wide),
        in_specs=in_vmem(2),
        out_specs=tuple(in_vmem(4)),
        compiler_params=params(),
    )(owned, gain)


def gram(sizes, side, here, own, other, q):
    layers, hd, rank, tokens, cols = sizes
    width = layers * hd
    share = jax.ShapeDtypeStruct(
        (width // (4 * hd), 3 * tokens + width - hd, 2 * hd), jnp.bfloat16
    )
    return pl.pallas_call(
        functools.partial(gram_kernel, sizes, side, len(own)),
        out_shape=(
            jax.ShapeDtypeStruct((width, cols), jnp.bfloat16),
            jax.ShapeDtypeStruct((width, cols), jnp.bfloat16),
            jax.ShapeDtypeStruct((tokens, cols), jnp.bfloat16),
            jax.ShapeDtypeStruct((tokens, cols), jnp.bfloat16),
            share,
            share,
        ),
        in_specs=in_smem(1) + in_vmem(len(own) + len(other) + 1),
        out_specs=tuple(in_vmem(6)),
        scratch_shapes=[
            pltpu.VMEM((tokens, cols), jnp.float32),
            pltpu.VMEM((tokens, cols), jnp.float32),
            pltpu.VMEM((2, 2, hd, cols), jnp.float32),
        ],
        compiler_params=params(),
    )(here, *own, *other, q)


def solve(sizes, features, here, own, other, x, s, u, v, q):
    layers, hd, rank, tokens, cols = sizes
    width = layers * hd
    return pl.pallas_call(
        functools.partial(solve_kernel, sizes, features),
        out_shape=jax.ShapeDtypeStruct(q.shape, jnp.bfloat16),
        in_specs=in_smem(1) + [pl.BlockSpec(memory_space=pl.ANY)] * 2 + in_vmem(5),
        out_specs=in_vmem(1)[0],
        scratch_shapes=[
            pltpu.VMEM((tokens, width), jnp.bfloat16),
            pltpu.VMEM((tokens, width), jnp.bfloat16),
            pltpu.VMEM((tokens, width), jnp.bfloat16),
            pltpu.VMEM((layers, tokens, hd), jnp.float32),
            pltpu.VMEM((layers, tokens, hd), jnp.float32),
            pltpu.VMEM((layers, tokens, 1), jnp.float32),
            pltpu.VMEM((2 * own.shape[0],) + own.shape[1:], jnp.bfloat16),
            pltpu.SemaphoreType.DMA((2,)),
        ],
        compiler_params=params(),
    )(here, own, other, x, s, u, v, q)


def swap(value, axis):
    return lax.all_to_all(value, axis, split_axis=0, concat_axis=0, tiled=True)


def pick(chooser, parts):
    flat = parts.reshape(parts.shape[0], -1)
    return mm(chooser, flat).astype(jnp.bfloat16).reshape((chooser.shape[0],) + parts.shape[1:])


def body(
    inputs,
    cotangent,
    norm_gain,
    w_value,
    w_out,
    value_down,
    value_up_factor,
    out_down,
    output_up_factor,
    block_tenant,
    valid_tokens,
    tenant_slot,
):
    section, sections = lax.axis_index(pipe), lax.axis_size(pipe)
    member, members = lax.axis_index(dp), lax.axis_size(dp)
    rows, features = inputs.shape[1], inputs.shape[2]
    hd, rank = w_value.shape[1], value_down.shape[2]
    cols = features // sections
    tokens = rows * sections
    sizes = (sections, hd, rank, tokens, cols)
    side = lax.axis_size("a") * lax.axis_size("b")
    across = lax.axis_size("x")
    planes = lax.axis_size("z")
    here = jnp.stack([section, member]).astype(jnp.int32)
    gain = norm_gain
    both_cores = [(0, 1), (1, 0)]

    stored = store(
        sizes,
        members,
        (value_down[0, 0], output_up_factor[0, 0], gain, value_up_factor[0, 0], out_down[0, 0]),
    )
    lines = spread_lines(
        sizes,
        side,
        (here, block_tenant, valid_tokens),
        (
            w_value[0],
            w_out[0],
            gain,
            inputs[0],
            cotangent[0],
            lax.ppermute(inputs[0], "core", both_cores),
            lax.ppermute(cotangent[0], "core", both_cores),
        ),
    )
    lines = [lines[0]] + [
        lax.ppermute(lines[step], ("a", "b"), [(i, (i + step) % side) for i in range(side)])
        for step in range(1, side)
    ]
    adapters, *turned = pick_rows((here, block_tenant, tenant_slot), swap(stored, dp), lines)
    turned = [turned[0]] + [
        lax.ppermute(turned[step], "x", [(i, (i + step) % across) for i in range(across)])
        for step in range(1, across)
    ]
    adapters = swap(relay(swap(adapters, "z"), turned[1:]), ("b", "x", "a"))
    pairs = across // 2
    other = [
        lax.ppermute(
            jnp.concatenate([part[:, :hd] for part in turned[at : at + pairs]], axis=0),
            "z",
            [(i, (i + turn) % planes) for i in range(planes)],
        )
        for at, turn in ((0, 1), (pairs, -1))
    ]

    u, v, x, s, kept, given = gram(sizes, side, here, turned, other, adapters)
    theirs = lax.ppermute(given, "core", both_cores)
    summed = (kept.astype(jnp.float32) + theirs.astype(jnp.float32)).astype(jnp.bfloat16)
    shares = swap(summed.reshape(sections // 2, -1, summed.shape[-1]), ("b", "x"))
    share = jnp.sum(shares.astype(jnp.float32), axis=0).astype(jnp.bfloat16)
    own = swap(jnp.broadcast_to(share[None], shares.shape), ("b", "x")).reshape(summed.shape)
    other = lax.ppermute(own, "core", both_cores)

    grads = solve(sizes, features, here, own, other, x, s, u, v, adapters)

    ids = jnp.arange(members, dtype=jnp.int32)
    tenant_hot = block_tenant[:, None] == ids[None, :]
    slot_of = jnp.sum(jnp.where(tenant_hot, tenant_slot[None, :], 0), axis=1)
    slot_hot = (ids[:, None] == slot_of[None, :]).astype(jnp.bfloat16)
    by_member = swap(swap(grads, ("b", "x", "a")), "z")
    owned = swap(pick(slot_hot, by_member), dp)
    return tuple(part[None, None] for part in finish(sizes, owned, gain))


def solution(mesh):
    sections, members = mesh.devices.shape
    finer = jax.sharding.Mesh(
        mesh.devices.reshape(2, 2, sections // 4, members // 2, 2), pipe + dp
    )
    return jax.shard_map(
        body,
        mesh=finer,
        in_specs=(
            P(pipe, dp, None),
            P(pipe, dp, None),
            P(pipe, None),
            P(pipe, None, None),
            P(pipe, None, None),
            P(pipe, dp, None, None),
            P(pipe, dp, None, None),
            P(pipe, dp, None, None),
            P(pipe, dp, None, None),
            P(),
            P(),
            P(),
        ),
        out_specs=(
            P(pipe, dp, None, None),
            P(pipe, dp, None, None),
            P(pipe, dp, None, None),
            P(pipe, dp, None, None),
        ),
        check_vma=False,
    )
```

time: 261 us -> 234 us (0.90)
  blocking collectives: 114 us -> 84.7 us
  waiting for transfers between devices: 55.4 us -> 63.7 us
  Pallas kernels: 38.5 us -> 30.3 us
    all_to_all x4, blocking collectives: 114 us -> 84.7 us  [swap(): return lax.all_to_all(value, axis, split_axis=0, concat_axis=0, tiled=True)]
    ppermute x10 -> x12, waiting for transfers between devices: 29.8 us -> 46.7 us  [the longest x2 13.6 us: body(): lax.ppermute(jnp.concatenate([part[:, :hd] for part in turned[at:at + pai...]
    all_to_all x4, waiting for transfers between devices: 25.5 us -> 17 us  [swap(): return lax.all_to_all(value, axis, split_axis=0, concat_axis=0, tiled=True)]
    all_to_all x4, starting transfers between devices: 34.4 us -> 28.2 us  [swap(): return lax.all_to_all(value, axis, split_axis=0, concat_axis=0, tiled=True)]
    ppermute x10 -> x12, starting transfers between devices: 11.7 us -> 17.1 us  [the longest x3 5.06 us: body(): lax.ppermute(lines[step], ('a', 'b'), [(i, (i + step) % side) for i in ra...]
    pallas_call x1, Pallas kernels: 8.23 us -> 5 us  [gram(): pl.pallas_call(functools.partial(gram_kernel, sizes, side, len(own)), out...]
  transfers between devices with their start and end apart: 14 -> 16, of which waited for: 11 -> 11; matrix products, arithmetic and copies ran while one was open for 0% -> 1% of each run, Pallas kernels for 0% -> 0%
where the time goes in v4:
time: 234 us; the launch traced here: 233 us
  blocking collectives  84.7 us (36%)
  waiting for transfers between devices  63.7 us (27%)
  starting transfers between devices  45.3 us (19%)
  Pallas kernels  30.3 us (13%)
  local copies, waits for them, and re-layouts  4.61 us (2%)
  other arithmetic  3.12 us (1%)
    all_to_all x4, blocking collectives, swap(): return lax.all_to_all(value, axis, split_axis=0, concat_axis=0, tiled=True)  84.7 us
    all_to_all x4, starting transfers between devices, swap(): return lax.all_to_all(value, axis, split_axis=0, concat_axis=0, tiled=True)  28.2 us
    pallas_call x1, Pallas kernels, solve(): pl.pallas_call(functools.partial(solve_kernel, sizes, features), out_shap...  19.8 us
    all_to_all x4, waiting for transfers between devices, swap(): return lax.all_to_all(value, axis, split_axis=0, concat_axis=0, tiled=True)  17 us
    ppermute x2, waiting for transfers between devices, body(): lax.ppermute(jnp.concatenate([part[:, :hd] for part in turned[at:at + pai...  13.6 us
    ppermute x3, waiting for transfers between devices, body(): lax.ppermute(lines[step], ('a', 'b'), [(i, (i + step) % side) for i in ra...  13.5 us
    ppermute x3, waiting for transfers between devices, body(): lax.ppermute(turned[step], 'x', [(i, (i + step) % across) for i in range(...  13.2 us
    ppermute x3, starting transfers between devices, body(): lax.ppermute(lines[step], ('a', 'b'), [(i, (i + step) % side) for i in ra...  5.06 us
  transfers between devices with their start and end apart: 16, of which 11 were waited for; matrix products, arithmetic and copies ran while one was open for 1% of the time, Pallas kernels for 0%

profile of v4, /device:TPU:1, one launch (start us, length us, event | category | flops | bytes accessed | tf_op | source)
XLA Modules:
  0.0 232.9 jit_solution(15782250166831820577)
XLA Ops:
  0.7 2.1 shard_map.147
  2.8 10.0 %all-to-all-start = ((bf16[16,16,1152]{2,1,0:T(8,128)(2,1)}), bf16[16,16,1152]{2,1,0:T(8,128)(2,1)S(1)}, u32[]{:S(2)}, u32[]{:S(2)}) async-start(bf16[16,16,1152]{2,1,0:T(8,128)(2,1)} %shard_map.147), calls=%async_computation | async-start | bytes 1179648 | tf_op jit(solution)/shard_map/all_to_all | solution.py:488
  18.2 2.6 %collective-permute-start.3 = (bf16[4,80,512]{2,1,0:T(8,128)(2,1)S(1)}, bf16[4,80,512]{2,1,0:T(8,128)(2,1)S(1)}, u32[]{:S(2)}, u32[]{:S(2)}) collective-permute-start(bf16[4,80,512]{2,1,0:T(8,128)(2,1)S(1)} %get-tuple-element.25), channel_id=1, source_target_pairs={{0,128},{64,192},{128,0},{192,64},{1,129},{65,193},{129,1},{193,65... | collective-permute-start | bytes 983048 | tf_op jit(solution)/shard_map/ppermute | solution.py:544
  21.9 5.3 %collective-permute-done.2.refs_1_ = bf16[4,80,512]{2,1,0:T(8,128)(2,1)S(1)} collective-permute-done((bf16[4,80,512]{2,1,0:T(8,128)(2,1)S(1)}, bf16[4,80,512]{2,1,0:T(8,128)(2,1)S(1)}, u32[]{:S(2)}, u32[]{:S(2)}) %collective-permute-start.2) | collective-permute-done | bytes 327712 | tf_op jit(solution)/shard_map/ppermute | solution.py:544
  27.2 8.1 %collective-permute-done.3.refs_2_ = bf16[4,80,512]{2,1,0:T(8,128)(2,1)S(1)} collective-permute-done((bf16[4,80,512]{2,1,0:T(8,128)(2,1)S(1)}, bf16[4,80,512]{2,1,0:T(8,128)(2,1)S(1)}, u32[]{:S(2)}, u32[]{:S(2)}) %collective-permute-start.3) | collective-permute-done | bytes 327712 | tf_op jit(solution)/shard_map/ppermute | solution.py:544
  37.1 6.9 %all-to-all-start.1 = ((bf16[16,16,1152]{2,1,0:T(8,128)(2,1)}), bf16[16,16,1152]{2,1,0:T(8,128)(2,1)}, u32[]{:S(2)}, u32[]{:S(2)}) async-start(bf16[16,16,1152]{2,1,0:T(8,128)(2,1)} %get-tuple-element.31), calls=%async_computation.1 | async-start | bytes 1179648 | tf_op jit(solution)/shard_map/all_to_all | solution.py:488
  44.0 2.7 %collective-permute-start.6 = (bf16[4,80,512]{2,1,0:T(8,128)(2,1)}, bf16[4,80,512]{2,1,0:T(8,128)(2,1)S(1)}, u32[]{:S(2)}, u32[]{:S(2)}) collective-permute-start(bf16[4,80,512]{2,1,0:T(8,128)(2,1)} %get-tuple-element.29), channel_id=1, source_target_pairs={{0,32},{16,48},{32,0},{48,16},{1,33},{17,49},{33,1},{49,17},{2,34}... | collective-permute-start | bytes 983048 | tf_op jit(solution)/shard_map/ppermute | solution.py:549
  48.2 5.6 %collective-permute-done.6.refs_2_ = bf16[4,80,512]{2,1,0:T(8,128)(2,1)S(1)} collective-permute-done((bf16[4,80,512]{2,1,0:T(8,128)(2,1)}, bf16[4,80,512]{2,1,0:T(8,128)(2,1)S(1)}, u32[]{:S(2)}, u32[]{:S(2)}) %collective-permute-start.6) | collective-permute-done | bytes 327712 | tf_op jit(solution)/shard_map/ppermute | solution.py:549
  53.8 7.6 %collective-permute-done.7.refs_3_ = bf16[4,80,512]{2,1,0:T(8,128)(2,1)S(1)} collective-permute-done((bf16[4,80,512]{2,1,0:T(8,128)(2,1)S(1)}, bf16[4,80,512]{2,1,0:T(8,128)(2,1)S(1)}, u32[]{:S(2)}, u32[]{:S(2)}) %collective-permute-start.7) | collective-permute-done | bytes 327712 | tf_op jit(solution)/shard_map/ppermute | solution.py:549
  62.4 2.7 %collective-permute-start.9 = (bf16[8,64,512]{2,1,0:T(8,128)(2,1)}, bf16[8,64,512]{2,1,0:T(8,128)(2,1)S(1)}, u32[]{:S(2)}, u32[]{:S(2)}) collective-permute-start(bf16[8,64,512]{2,1,0:T(8,128)(2,1)} %pad_maximum_fusion.1), channel_id=1, source_target_pairs={{0,14},{2,0},{4,2},{6,4},{8,6},{10,8},{12,10},{14,12},{1,15},{3,1}... | collective-permute-start | bytes 1572872 | tf_op jit(solution)/shard_map/ppermute | solution.py:555
  65.8 7.0 %all-to-all-start.2 = ((bf16[16,16,1152]{2,1,0:T(8,128)(2,1)}), bf16[16,16,1152]{2,1,0:T(8,128)(2,1)S(1)}, u32[]{:S(2)}, u32[]{:S(2)}) async-start(bf16[16,16,1152]{2,1,0:T(8,128)(2,1)} %shard_map.150), calls=%async_computation.2 | async-start | bytes 1179648 | tf_op jit(solution)/shard_map/all_to_all | solution.py:488
  75.0 11.5 %collective-permute-done.8.refs_4_ = bf16[8,64,512]{2,1,0:T(8,128)(2,1)S(1)} collective-permute-done((bf16[8,64,512]{2,1,0:T(8,128)(2,1)S(1)}, bf16[8,64,512]{2,1,0:T(8,128)(2,1)S(1)}, u32[]{:S(2)}, u32[]{:S(2)}) %collective-permute-start.8) | collective-permute-done | bytes 524320 | tf_op jit(solution)/shard_map/ppermute | solution.py:555
  88.4 5.0 %shard_map.151 = (bf16[1024,512]{1,0:T(8,128)(2,1)S(1)}, bf16[1024,512]{1,0:T(8,128)(2,1)S(1)}, bf16[128,512]{1,0:T(8,128)(2,1)S(1)}, bf16[128,512]{1,0:T(8,128)...) custom-call(s32[2]{0:T(128)S(1)} %pad_add_fusion.here_ref, ...), custom_call_target="tpu_custom_call" | custom-call | tf_op jit(solution)/shard_map/pallas_call | solution.py:444
  93.5 2.1 collective-permute-start.10
  95.5 2.8 %collective-permute-done.10 = bf16[4,1344,128]{2,1,0:T(8,128)(2,1)S(1)} collective-permute-done((bf16[4,1344,128]{2,1,0:T(8,128)(2,1)S(1)}, bf16[4,1344,128]{2,1,0:T(8,128)(2,1)S(1)}, u32[]{:S(2)}, u32[]{:S(2)}) %collective-permute-start.10) | collective-permute-done | bytes 1376288 | tf_op jit(solution)/shard_map/ppermute | solution.py:564
  98.7 24.1 %all_to_all.40 = bf16[8,672,128]{2,1,0:T(8,128)(2,1)} all-to-all(bf16[8,672,128]{2,1,0:T(8,128)(2,1)S(1)} %bitcast.29), channel_id=1, replica_groups=mesh['a'=2,'b'=2,'x'=4,'z'=8,'core'=2] {'b','x'}, dimensions={0} | all-to-all | bytes 2752512 | tf_op jit(solution)/shard_map/all_to_all | solution.py:488
  124.6 20.4 %all_to_all.41 = bf16[8,672,128]{2,1,0:T(8,128)(2,1)S(1)} all-to-all(bf16[8,672,128]{2,1,0:T(8,128)(2,1)S(1)} %broadcast_in_dim.37), channel_id=1, replica_groups=mesh['a'=2,'b'=2,'x'=4,'z'=8,'core'=2] {'b','x'}, dimensions={0} | all-to-all | bytes 2752512 | tf_op jit(solution)/shard_map/all_to_all | solution.py:488
  145.0 2.4 %collective-permute-start.11 = (bf16[4,1344,128]{2,1,0:T(8,128)(2,1)S(1)}, bf16[4,1344,128]{2,1,0:T(8,128)(2,1)S(1)}, u32[]{:S(2)}, u32[]{:S(2)}) collective-permute-start(bf16[4,1344,128]{2,1,0:T(8,128)(2,1)S(1)} %bitcast.21), channel_id=1, source_target_pairs={{0,1},{1,0},{2,3},{3,2},{4,5},{5,4},{6,7},{7,6},{8,9},{9,8},{10,11... | collective-permute-start | bytes 4128776 | tf_op jit(solution)/shard_map/ppermute | solution.py:569
  147.4 2.8 %collective-permute-done.11.other_ref = bf16[4,1344,128]{2,1,0:T(8,128)(2,1)S(1)} collective-permute-done((bf16[4,1344,128]{2,1,0:T(8,128)(2,1)S(1)}, bf16[4,1344,128]{2,1,0:T(8,128)(2,1)S(1)}, u32[]{:S(2)}, u32[]{:S(2)}) %collective-permute-start.11) | collective-permute-done | bytes 1376288 | tf_op jit(solution)/shard_map/ppermute | solution.py:569
  150.2 19.8 %shard_map.152 = bf16[16,16,1152]{2,1,0:T(8,128)(2,1)S(1)} custom-call(s32[2]{0:T(128)S(1)} %pad_add_fusion.here_ref, bf16[4,1344,128]{2,1,0:T(8,128)(2,1)S(1)} %bitcast.22, bf16[4,1344,128]{2,1,0:T(8,128)(2,1)S(1)} %collective-permute-done.11.other_ref, bf16[128,512]{1,0:T(8,128)(2,1)S(1)} %copy-done.14, bf16[128,512]{1,0:T(8,128)(2,1)S(1)} %copy-done.16, ...), custom_call_target="tpu_custom_call" | custom-call | tf_op jit(solution)/shard_map/pallas_call | solution.py:468
  170.0 16.0 %all_to_all.42 = bf16[16,16,1152]{2,1,0:T(8,128)(2,1)} all-to-all(bf16[16,16,1152]{2,1,0:T(8,128)(2,1)S(1)} %shard_map.152), channel_id=1, replica_groups=mesh['a'=2,'b'=2,'x'=4,'z'=8,'core'=2] {'b','x','a'}, dimensions={0} | all-to-all | bytes 1179648 | tf_op jit(solution)/shard_map/all_to_all | solution.py:488
  186.0 4.3 %all-to-all-start.6 = ((bf16[16,16,1152]{2,1,0:T(8,128)(2,1)}), bf16[16,16,1152]{2,1,0:T(8,128)(2,1)S(1)}, u32[]{:S(2)}, u32[]{:S(2)}) async-start(bf16[16,16,1152]{2,1,0:T(8,128)(2,1)} %all_to_all.42), calls=%async_computation.6 | async-start | bytes 1179648 | tf_op jit(solution)/shard_map/all_to_all | solution.py:488
  190.4 17.0 %all-to-all-done.6 = bf16[16,16,1152]{2,1,0:T(8,128)(2,1)S(1)} async-done(((bf16[16,16,1152]{2,1,0:T(8,128)(2,1)}), bf16[16,16,1152]{2,1,0:T(8,128)(2,1)S(1)}, u32[]{:S(2)}, u32[]{:S(2)}) %all-to-all-start.6) | async-done | bytes 589856 | tf_op jit(solution)/shard_map/all_to_all | solution.py:488
  207.9 24.2 %all_to_all.43.owned_ref = bf16[16,16,1152]{2,1,0:T(8,128)(2,1)S(1)} all-to-all(bf16[16,16,1152]{2,1,0:T(8,128)(2,1)S(1)} %bitcast.33), channel_id=1, replica_groups=mesh['a'=2,'b'=2,'x'=4,'z'=8,'core'=2] {'z','core'}, dimensions={0} | all-to-all | bytes 1179648 | tf_op jit(solution)/shard_map/all_to_all | solution.py:488
  (81 shorter events, 19.0 us)
Async XLA Ops:
  0.6 14.5 %copy-start.12 = (f32[1,8192]{1,0:T(1,128)S(1)}, f32[1,8192]{1,0:T(1,128)}, u32[]{:S(2)}) copy-start(f32[1,8192]{1,0:T(1,128)} %gain_ref.5) | copy-start | bytes 98308
  2.8 32.5 %all-to-all-start = ((bf16[16,16,1152]{2,1,0:T(8,128)(2,1)}), bf16[16,16,1152]{2,1,0:T(8,128)(2,1)S(1)}, u32[]{:S(2)}, u32[]{:S(2)}) async-start(bf16[16,16,1152]{2,1,0:T(8,128)(2,1)} %shard_map.147), calls=%async_computation | async-start | bytes 1179648 | tf_op jit(solution)/shard_map/all_to_all | solution.py:488
  12.8 22.6 %copy-start.23 = (s32[16]{0:T(128)S(1)}, s32[16]{0:T(128)}, u32[]{:S(2)}) copy-start(s32[16]{0:T(128)} %slot_ref.1) | copy-start | bytes 196
  12.8 1.4 collective-permute-start
  13.0 1.4 collective-permute-start.1
  16.8 10.4 %collective-permute-start.2 = (bf16[4,80,512]{2,1,0:T(8,128)(2,1)S(1)}, bf16[4,80,512]{2,1,0:T(8,128)(2,1)S(1)}, u32[]{:S(2)}, u32[]{:S(2)}) collective-permute-start(bf16[4,80,512]{2,1,0:T(8,128)(2,1)S(1)} %get-tuple-element.24), channel_id=1, source_target_pairs={{0,64},{64,128},{128,192},{192,0},{1,65},{65,129},{129,193},{193,1... | collective-permute-start | bytes 983048 | tf_op jit(solution)/shard_map/ppermute | solution.py:544
  18.2 17.1 %collective-permute-start.3 = (bf16[4,80,512]{2,1,0:T(8,128)(2,1)S(1)}, bf16[4,80,512]{2,1,0:T(8,128)(2,1)S(1)}, u32[]{:S(2)}, u32[]{:S(2)}) collective-permute-start(bf16[4,80,512]{2,1,0:T(8,128)(2,1)S(1)} %get-tuple-element.25), channel_id=1, source_target_pairs={{0,128},{64,192},{128,0},{192,64},{1,129},{65,193},{129,1},{193,65... | collective-permute-start | bytes 983048 | tf_op jit(solution)/shard_map/ppermute | solution.py:544
  20.8 14.5 %collective-permute-start.4 = (bf16[4,80,512]{2,1,0:T(8,128)(2,1)S(1)}, bf16[4,80,512]{2,1,0:T(8,128)(2,1)S(1)}, u32[]{:S(2)}, u32[]{:S(2)}) collective-permute-start(bf16[4,80,512]{2,1,0:T(8,128)(2,1)S(1)} %get-tuple-element.26), channel_id=1, source_target_pairs={{0,192},{64,0},{128,64},{192,128},{1,193},{65,1},{129,65},{193,129... | collective-permute-start | bytes 983048 | tf_op jit(solution)/shard_map/ppermute | solution.py:544
  37.1 28.0 %all-to-all-start.1 = ((bf16[16,16,1152]{2,1,0:T(8,128)(2,1)}), bf16[16,16,1152]{2,1,0:T(8,128)(2,1)}, u32[]{:S(2)}, u32[]{:S(2)}) async-start(bf16[16,16,1152]{2,1,0:T(8,128)(2,1)} %get-tuple-element.31), calls=%async_computation.1 | async-start | bytes 1179648 | tf_op jit(solution)/shard_map/all_to_all | solution.py:488
  44.0 9.8 %collective-permute-start.6 = (bf16[4,80,512]{2,1,0:T(8,128)(2,1)}, bf16[4,80,512]{2,1,0:T(8,128)(2,1)S(1)}, u32[]{:S(2)}, u32[]{:S(2)}) collective-permute-start(bf16[4,80,512]{2,1,0:T(8,128)(2,1)} %get-tuple-element.29), channel_id=1, source_target_pairs={{0,32},{16,48},{32,0},{48,16},{1,33},{17,49},{33,1},{49,17},{2,34}... | collective-permute-start | bytes 983048 | tf_op jit(solution)/shard_map/ppermute | solution.py:549
  46.7 14.7 %collective-permute-start.7 = (bf16[4,80,512]{2,1,0:T(8,128)(2,1)S(1)}, bf16[4,80,512]{2,1,0:T(8,128)(2,1)S(1)}, u32[]{:S(2)}, u32[]{:S(2)}) collective-permute-start(bf16[4,80,512]{2,1,0:T(8,128)(2,1)S(1)} %get-tuple-element.30), channel_id=1, source_target_pairs={{0,48},{16,0},{32,16},{48,32},{1,49},{17,1},{33,17},{49,33},{2,50}... | collective-permute-start | bytes 983048 | tf_op jit(solution)/shard_map/ppermute | solution.py:549
  47.6 17.4 %collective-permute-start.5 = (bf16[4,80,512]{2,1,0:T(8,128)(2,1)}, bf16[4,80,512]{2,1,0:T(8,128)(2,1)S(1)}, u32[]{:S(2)}, u32[]{:S(2)}) collective-permute-start(bf16[4,80,512]{2,1,0:T(8,128)(2,1)} %get-tuple-element.28), channel_id=1, source_target_pairs={{0,16},{16,32},{32,48},{48,0},{1,17},{17,33},{33,49},{49,1},{2,18}... | collective-permute-start | bytes 983048 | tf_op jit(solution)/shard_map/ppermute | solution.py:549
  62.4 12.7 %collective-permute-start.9 = (bf16[8,64,512]{2,1,0:T(8,128)(2,1)}, bf16[8,64,512]{2,1,0:T(8,128)(2,1)S(1)}, u32[]{:S(2)}, u32[]{:S(2)}) collective-permute-start(bf16[8,64,512]{2,1,0:T(8,128)(2,1)} %pad_maximum_fusion.1), channel_id=1, source_target_pairs={{0,14},{2,0},{4,2},{6,4},{8,6},{10,8},{12,10},{14,12},{1,15},{3,1}... | collective-permute-start | bytes 1572872 | tf_op jit(solution)/shard_map/ppermute | solution.py:555
  65.8 21.6 %copy-start.1 = (bf16[4,80,512]{2,1,0:T(8,128)(2,1)S(1)}, bf16[4,80,512]{2,1,0:T(8,128)(2,1)}, u32[]{:S(2)}) copy-start(bf16[4,80,512]{2,1,0:T(8,128)(2,1)} %copy-done) | copy-start | bytes 983044
  65.8 21.6 %copy-start.3 = (bf16[4,80,512]{2,1,0:T(8,128)(2,1)S(1)}, bf16[4,80,512]{2,1,0:T(8,128)(2,1)}, u32[]{:S(2)}) copy-start(bf16[4,80,512]{2,1,0:T(8,128)(2,1)} %copy-done.2) | copy-start | bytes 983044
  65.8 21.6 %copy-start.5 = (bf16[4,80,512]{2,1,0:T(8,128)(2,1)S(1)}, bf16[4,80,512]{2,1,0:T(8,128)(2,1)}, u32[]{:S(2)}) copy-start(bf16[4,80,512]{2,1,0:T(8,128)(2,1)} %copy-done.4) | copy-start | bytes 983044
  65.8 21.6 %all-to-all-start.2 = ((bf16[16,16,1152]{2,1,0:T(8,128)(2,1)}), bf16[16,16,1152]{2,1,0:T(8,128)(2,1)S(1)}, u32[]{:S(2)}, u32[]{:S(2)}) async-start(bf16[16,16,1152]{2,1,0:T(8,128)(2,1)} %shard_map.150), calls=%async_computation.2 | async-start | bytes 1179648 | tf_op jit(solution)/shard_map/all_to_all | solution.py:488
  72.9 13.7 %collective-permute-start.8 = (bf16[8,64,512]{2,1,0:T(8,128)(2,1)S(1)}, bf16[8,64,512]{2,1,0:T(8,128)(2,1)S(1)}, u32[]{:S(2)}, u32[]{:S(2)}) collective-permute-start(bf16[8,64,512]{2,1,0:T(8,128)(2,1)S(1)} %pad_maximum_fusion), channel_id=1, source_target_pairs={{0,2},{2,4},{4,6},{6,8},{8,10},{10,12},{12,14},{14,0},{1,3},{3,5},... | collective-permute-start | bytes 1572872 | tf_op jit(solution)/shard_map/ppermute | solution.py:555
  93.5 4.8 %collective-permute-start.10 = (bf16[4,1344,128]{2,1,0:T(8,128)(2,1)S(1)}, bf16[4,1344,128]{2,1,0:T(8,128)(2,1)S(1)}, u32[]{:S(2)}, u32[]{:S(2)}) collective-permute-start(bf16[4,1344,128]{2,1,0:T(8,128)(2,1)S(1)} %get-tuple-element.33), channel_id=1, source_target_pairs={{0,1},{1,0},{2,3},{3,2},{4,5},{5,4},{6,7},{7,6},{8,9},{9,8},{10,11... | collective-permute-start | bytes 4128776 | tf_op jit(solution)/shard_map/ppermute | solution.py:564
  124.5 25.6 %copy-start.7 = (bf16[1024,512]{1,0:T(8,128)(2,1)S(1)}, bf16[1024,512]{1,0:T(8,128)(2,1)}, u32[]{:S(2)}) copy-start(bf16[1024,512]{1,0:T(8,128)(2,1)} %copy-done.6) | copy-start | bytes 3145732
  124.6 25.6 %copy-start.14 = (bf16[128,512]{1,0:T(8,128)(2,1)S(1)}, bf16[128,512]{1,0:T(8,128)(2,1)}, u32[]{:S(2)}) copy-start(bf16[128,512]{1,0:T(8,128)(2,1)} %copy-done.13) | copy-start | bytes 393220
  124.6 25.6 %copy-start.16 = (bf16[128,512]{1,0:T(8,128)(2,1)S(1)}, bf16[128,512]{1,0:T(8,128)(2,1)}, u32[]{:S(2)}) copy-start(bf16[128,512]{1,0:T(8,128)(2,1)} %copy-done.15) | copy-start | bytes 393220
  145.0 5.2 %collective-permute-start.11 = (bf16[4,1344,128]{2,1,0:T(8,128)(2,1)S(1)}, bf16[4,1344,128]{2,1,0:T(8,128)(2,1)S(1)}, u32[]{:S(2)}, u32[]{:S(2)}) collective-permute-start(bf16[4,1344,128]{2,1,0:T(8,128)(2,1)S(1)} %bitcast.21), channel_id=1, source_target_pairs={{0,1},{1,0},{2,3},{3,2},{4,5},{5,4},{6,7},{7,6},{8,9},{9,8},{10,11... | collective-permute-start | bytes 4128776 | tf_op jit(solution)/shard_map/ppermute | solution.py:569
  186.0 21.4 %all-to-all-start.6 = ((bf16[16,16,1152]{2,1,0:T(8,128)(2,1)}), bf16[16,16,1152]{2,1,0:T(8,128)(2,1)S(1)}, u32[]{:S(2)}, u32[]{:S(2)}) async-start(bf16[16,16,1152]{2,1,0:T(8,128)(2,1)} %all_to_all.42), calls=%async_computation.6 | async-start | bytes 1179648 | tf_op jit(solution)/shard_map/all_to_all | solution.py:488
  (16 other events, 117.0 us)

commit v5 on v4

--- a/solution.py
+++ b/solution.py
@@ -40,41 +40,54 @@
     return compare(row_layer, column_layer)
 
 
-def store_kernel(sizes, vd_ref, ou_ref, gain_ref, vu_ref, od_ref, out_ref):
+def pack_kernel(
+    sizes, here_ref, wv_ref, wo_ref, gain_ref, vd_ref, ou_ref, vu_ref, od_ref, stored_ref, *out_refs
+):
     layers, hd, rank, tokens, cols = sizes
     small = jnp.concatenate([vu_ref[...], od_ref[...]], axis=1)
-    for k in range(out_ref.shape[0]):
+    for k in range(stored_ref.shape[0]):
         at = pl.ds(k * cols, cols)
-        out_ref[k, :, :cols] = (vd_ref[:, at].astype(jnp.float32) * gain_ref[:, at]).astype(
+        stored_ref[k, :, :cols] = (vd_ref[:, at].astype(jnp.float32) * gain_ref[:, at]).astype(
             jnp.bfloat16
         )
-        out_ref[k, :, cols : 2 * cols] = ou_ref[:, at]
-        out_ref[k, :, 2 * cols :] = small
-
-
-def lines_kernel(
-    sizes,
-    here_ref,
-    tenant_ref,
-    valid_ref,
-    wv_ref,
-    wo_ref,
-    gain_ref,
-    x_ref,
-    cot_ref,
-    other_x_ref,
-    other_cot_ref,
-    *out_refs
-):
-    layers, hd, rank, tokens, cols = sizes
-    rows = tokens // layers
+        stored_ref[k, :, cols : 2 * cols] = ou_ref[:, at]
+        stored_ref[k, :, 2 * cols :] = small
     part = hd // 2
     section, member = here_ref[0], here_ref[1]
     core = lax.rem(member, 2)
     side = len(out_refs)
     across = layers // side
     mine = pl.ds(pl.multiple_of(lax.rem(member // 2, 2) * part, part), part)
+    for step, out_ref in enumerate(out_refs):
+        line = lax.rem(section // across + step, side)
+        for k in range(across):
+            column = (lax.rem(line, side // 2) * across + k) * 2 + core
+            at = pl.ds(pl.multiple_of(column * cols, cols), cols)
+            out_ref[k, :part, :] = (wv_ref[mine, at].astype(jnp.float32) * gain_ref[:, at]).astype(
+                jnp.bfloat16
+            )
+            out_ref[k, part:, :] = wo_ref[mine, at]
+
+
+def join_kernel(
+    sizes,
+    here_ref,
+    tenant_ref,
+    valid_ref,
+    parts_ref,
+    x_ref,
+    cot_ref,
+    other_x_ref,
+    other_cot_ref,
+    *refs
+):
+    out_ref = refs[-1]
+    layers, hd, rank, tokens, cols = sizes
+    rows = tokens // layers
+    section, member = here_ref[0], here_ref[1]
+    core = lax.rem(member, 2)
     position = section * rows + lax.broadcasted_iota(jnp.int32, (rows, 1), 0)
+    width = 2 * cols + 2 * hd
 
     def token_weight(index):
         total = jnp.int32(0)
@@ -85,25 +98,18 @@
 
     own_weight = token_weight(member)
     other_weight = token_weight(member + 1 - 2 * core)
-    for step, out_ref in enumerate(out_refs):
-        line = lax.rem(section // across + step, side)
-        own = lax.div(line, side // 2) == core
-        for k in range(across):
-            column = (lax.rem(line, side // 2) * across + k) * 2 + core
-            at = pl.ds(pl.multiple_of(column * cols, cols), cols)
-            out_ref[k, :part, :] = (wv_ref[mine, at].astype(jnp.float32) * gain_ref[:, at]).astype(
-                jnp.bfloat16
-            )
-            out_ref[k, part:hd, :] = wo_ref[mine, at]
-            x = jnp.where(
-                own, x_ref[:, at].astype(jnp.float32), other_x_ref[:, at].astype(jnp.float32)
-            )
-            seeded = jnp.where(
-                own,
-                cot_ref[:, at].astype(jnp.float32) * own_weight,
-                other_cot_ref[:, at].astype(jnp.float32) * other_weight,
-            )
-            out_ref[k, hd:, :] = jnp.concatenate([x, seeded], axis=0).astype(jnp.bfloat16)
+    for k in range(layers // 2):
+        at = pl.ds(pl.multiple_of((2 * k + core) * cols, cols), cols)
+        own_x = x_ref[:, at].astype(jnp.float32)
+        other_x = other_x_ref[:, at].astype(jnp.float32)
+        own_seed = cot_ref[:, at].astype(jnp.float32) * own_weight
+        other_seed = other_cot_ref[:, at].astype(jnp.float32) * other_weight
+        for a in range(2):
+            own = core == a
+            out_ref[2 * k + a, :, :width] = parts_ref[2 * k + a]
+            out_ref[2 * k + a, :, width:] = jnp.concatenate(
+                [jnp.where(own, own_x, other_x), jnp.where(own, own_seed, other_seed)], axis=0
+            ).astype(jnp.bfloat16)
 
 
 def pick_kernel(side, across, here_ref, tenant_ref, slot_ref, parts_ref, *refs):
@@ -139,7 +145,7 @@
     layers, hd, rank, tokens, cols = sizes
     own_refs, other_refs, refs = refs[:across], refs[across : across + 2], refs[across + 2 :]
     pairs = across // 2
-    q_ref, u_ref, v_ref, x_ref, s_ref, keep_ref, give_ref, x_wide, s_wide, w_wide = refs
+    q_ref, u_ref, v_ref, xs_ref, keep_ref, give_ref, x_wide, s_wide, w_wide = refs
     rows = tokens // layers
     part = hd // 2
     section, core = here_ref[0], lax.rem(here_ref[1], 2)
@@ -164,12 +170,12 @@
         at = pl.ds(pl.multiple_of(l * hd, hd), hd)
         v_ref[at, :] = (w_wide[slot, 0] + adapter_scale * delta_v).astype(jnp.bfloat16)
         u_ref[at, :] = (w_wide[slot, 1] + adapter_scale * delta_u).astype(jnp.bfloat16)
-        both = own_refs[dx][dy, hd:, :].astype(jnp.float32)
+        both = q_l[:, 2 * cols + 2 * hd :].astype(jnp.float32)
         at = pl.ds(pl.multiple_of(l * rows, rows), rows)
         x_wide[at, :] = both[:rows]
         s_wide[at, :] = both[rows:]
-    x_ref[...] = x_wide[...].astype(jnp.bfloat16)
-    s_ref[...] = s_wide[...].astype(jnp.bfloat16)
+    xs_ref[:tokens, :] = x_wide[...].astype(jnp.bfloat16)
+    xs_ref[tokens:, :] = s_wide[...].astype(jnp.bfloat16)
     width = layers * hd
     base = 3 * tokens
     below = layer_mask(block, block, hd, lambda r, c: r < c)
@@ -188,8 +194,9 @@
             column = bj * block
             at_col = pl.ds(column, block)
             u_col, v_col = u_ref[at_col, :], v_ref[at_col, :]
-            put(own_core, 0, column, mm_nt(x_ref[...], v_col))
-            x_u = mm_nt(x_ref[...], u_col)
+            x_rows, s_rows = xs_ref[:tokens, :], xs_ref[tokens:, :]
+            put(own_core, 0, column, mm_nt(x_rows, v_col))
+            x_u = mm_nt(x_rows, u_col)
             if column + block == width:
                 wide = x_wide[...]
                 wide = wide * wide
@@ -198,7 +205,7 @@
                     folded = folded + wide[:, at : at + lane]
                 x_u = jnp.concatenate([x_u[:, : block - hd], folded[:, :hd] + folded[:, hd:]], axis=1)
             put(own_core, tokens, column, x_u)
-            put(own_core, 2 * tokens, column, mm_nt(s_ref[...], u_col))
+            put(own_core, 2 * tokens, column, mm_nt(s_rows, u_col))
             for bi in range(width // block):
                 height = min(block, width - hd - bi * block)
                 rows_at = pl.ds(bi * block, height)
@@ -226,8 +233,7 @@
     here_ref,
     own_ref,
     other_ref,
-    x_ref,
-    s_ref,
+    xs_ref,
     u_ref,
     v_ref,
     q_ref,
@@ -246,14 +252,14 @@
     base = 3 * tokens
     half_count = own_ref.shape[0]
     core = lax.rem(here_ref[1], 2)
-    copies = [
-        pltpu.make_async_copy(
-            source, k_ref.at[pl.ds(place * half_count, half_count)], sems.at[index]
-        )
-        for index, (source, place) in enumerate(((own_ref, core), (other_ref, 1 - core)))
-    ]
-    for copy in copies:
-        copy.start()
+    for index in range(half_count):
+        for source, place in ((own_ref, core), (other_ref, 1 - core)):
+            to = place * half_count + index
+            pltpu.make_async_copy(source.at[index], k_ref.at[to], sems.at[to]).start()
+
+    def arrive(index):
+        pltpu.make_async_copy(own_ref.at[0], k_ref.at[index], sems.at[index]).wait()
+
     c_ref[...] = jnp.zeros_like(c_ref)
     d_ref[...] = jnp.zeros_like(d_ref)
     ec_ref[...] = jnp.zeros_like(ec_ref)
@@ -268,12 +274,14 @@
             axis=1,
         )
 
-    for copy in copies:
-        copy.wait()
-    folded = k_ref[width // (2 * hd) - 1, tokens : 2 * tokens, :].astype(jnp.float32)[:, hd:]
+    last = width // (2 * hd) - 1
+    arrive(last)
+    folded = k_ref[last, tokens : 2 * tokens, :].astype(jnp.float32)[:, hd:]
     square = jnp.sum(folded, axis=1, keepdims=True)
     for l in range(layers):
         pair = l // 2
+        if l % 2 == 0 and pair < last:
+            arrive(pair)
         a = half(k_ref[pair, :tokens, :], l).astype(jnp.float32)
         if l:
             w = upto(l)
@@ -315,47 +323,60 @@
 
     below = layer_mask(block, block, hd, lambda r, c: r > c)
     upto_diag = layer_mask(block, block, hd, lambda r, c: r >= c)
-    blocks = width // block
-    for bl in range(blocks):
-        mine = pl.ds(bl * block, block)
+    group = block // hd
+    diagonal = lax.broadcasted_iota(jnp.int32, (group * rank, block), 0) // rank == (
+        lax.broadcasted_iota(jnp.int32, (group * rank, block), 1) // hd
+    )
+
+    def side_by_side(parts):
+        return parts[0] if len(parts) == 1 else jnp.concatenate(parts, axis=1)
+
+    def spread_diagonal(parts):
+        tall = jnp.concatenate(parts, axis=0)
+        return jnp.where(diagonal, side_by_side([tall] * group), jnp.zeros((), jnp.bfloat16))
+
+    for start in range(0, width, block):
+        stop = start + block
+        mine = pl.ds(start, block)
         c_t = c_ref[:, mine].T
         d_t = d_ref[:, mine].T
         ec_t = ec_ref[:, mine].T
-        y = mm(d_t, x_ref[...])
-        z = mm(c_t, s_ref[...]) - mm(ec_t, x_ref[...])
-        for bk in range(blocks):
-            other = pl.ds(bk * block, block)
-            u_k = u_ref[other, :]
-            if bk <= bl:
-                m = mm(d_t, c_ref[:, other])
-                if bk == bl:
-                    m = jnp.where(below, m, 0.0)
-                y = y + mm(m.astype(jnp.bfloat16), u_k)
-            if bk >= bl:
-                m = mm(c_t, d_ref[:, other])
-                if bk == bl:
-                    m = jnp.where(upto_diag, 0.0, m)
-                z = z + mm(m.astype(jnp.bfloat16), v_ref[other, :])
-            if bk < bl:
-                m = mm(ec_t, c_ref[:, other])
-            elif bk > bl:
-                m = mm(c_t, ec_ref[:, other])
-            else:
-                m = jnp.where(upto_diag, mm(ec_t, c_ref[:, other]), mm(c_t, ec_ref[:, other]))
-            z = z - mm(m.astype(jnp.bfloat16), u_k)
+
+        m = [jnp.where(below, mm(d_t, c_ref[:, mine]), 0.0).astype(jnp.bfloat16)]
+        if start:
+            m = [mm(d_t, c_ref[:, :start]).astype(jnp.bfloat16)] + m
+        y = mm(d_t, xs_ref[:tokens, :]) + mm(side_by_side(m), u_ref[:stop, :])
+
+        m = [jnp.where(upto_diag, 0.0, mm(c_t, d_ref[:, mine])).astype(jnp.bfloat16)]
+        if stop < width:
+            m = m + [mm(c_t, d_ref[:, stop:]).astype(jnp.bfloat16)]
+        z = mm(side_by_side([-ec_t, c_t]), xs_ref[...]) + mm(side_by_side(m), v_ref[start:, :])
+        m = [
+            jnp.where(upto_diag, mm(ec_t, c_ref[:, mine]), mm(c_t, ec_ref[:, mine])).astype(
+                jnp.bfloat16
+            )
+        ]
+        if start:
+            m = [mm(ec_t, c_ref[:, :start]).astype(jnp.bfloat16)] + m
+        if stop < width:
+            m = m + [mm(c_t, ec_ref[:, stop:]).astype(jnp.bfloat16)]
+        z = z - mm(side_by_side(m), u_ref[...])
+
         y = y.astype(jnp.bfloat16)
         z = z.astype(jnp.bfloat16)
-        for j in range(block // hd):
-            l = bl * (block // hd) + j
-            y_l, z_l = y[j * hd : (j + 1) * hd], z[j * hd : (j + 1) * hd]
-            at = turned_index(l, layers)
-            small = q_ref[at, :, 2 * cols : 2 * cols + 2 * hd]
-            out_ref[at, :, :cols] = (adapter_scale * mm(small[:, :hd], y_l)).astype(jnp.bfloat16)
-            out_ref[at, :, cols : 2 * cols] = (adapter_scale * mm(small[:, hd:], z_l)).astype(
-                jnp.bfloat16
-            )
+        places = [turned_index(l, layers) for l in range(start // hd, stop // hd)]
+        smalls = [q_ref[at, :, 2 * cols : 2 * cols + 2 * hd] for at in places]
+        up = adapter_scale * mm(spread_diagonal([small[:, :hd] for small in smalls]), y)
+        down = adapter_scale * mm(spread_diagonal([small[:, hd:] for small in smalls]), z)
+        tail_y = mm_nt(jnp.concatenate([q_ref[at, :, :cols] for at in places], axis=0), y)
+        tail_z = mm_nt(jnp.concatenate([q_ref[at, :, cols : 2 * cols] for at in places], axis=0), z)
+        for j, at in enumerate(places):
+            rows_j = slice(j * rank, (j + 1) * rank)
+            out_ref[at, :, :cols] = up[rows_j].astype(jnp.bfloat16)
+            out_ref[at, :, cols : 2 * cols] = down[rows_j].astype(jnp.bfloat16)
             tail = jnp.concatenate(
-                [mm_nt(q_ref[at, :, :cols], y_l), mm_nt(q_ref[at, :, cols : 2 * cols], z_l)], axis=1
+                [tail_y[rows_j, j * hd : (j + 1) * hd], tail_z[rows_j, j * hd : (j + 1) * hd]],
+                axis=1,
             )
             out_ref[at, :, 2 * cols :] = (adapter_scale * tail).astype(jnp.bfloat16)
 
@@ -372,27 +393,17 @@
     return [pl.BlockSpec(memory_space=pltpu.SMEM)] * count
 
 
-def store(sizes, members, arrays):
-    layers, hd, rank, tokens, cols = sizes
+def pack(sizes, side, members, here, arrays):
+    layers, hd, rank, tokens, cols = sizes
+    line = jax.ShapeDtypeStruct((layers // side, hd, cols), jnp.bfloat16)
+    stored = jax.ShapeDtypeStruct((members, rank, 2 * cols + 2 * hd), jnp.bfloat16)
     return pl.pallas_call(
-        functools.partial(store_kernel, sizes),
-        out_shape=jax.ShapeDtypeStruct((members, rank, 2 * cols + 2 * hd), jnp.bfloat16),
-        in_specs=in_vmem(len(arrays)),
-        out_specs=in_vmem(1)[0],
+        functools.partial(pack_kernel, sizes),
+        out_shape=(stored,) + (line,) * side,
+        in_specs=in_smem(1) + in_vmem(len(arrays)),
+        out_specs=tuple(in_vmem(1 + side)),
         compiler_params=params(whole_vmem_bytes),
-    )(*arrays)
-
-
-def spread_lines(sizes, side, scalars, arrays):
-    layers, hd, rank, tokens, cols = sizes
-    line = jax.ShapeDtypeStruct((layers // side, hd + 2 * (tokens // layers), cols), jnp.bfloat16)
-    return pl.pallas_call(
-        functools.partial(lines_kernel, sizes),
-        out_shape=(line,) * side,
-        in_specs=in_smem(len(scalars)) + in_vmem(len(arrays)),
-        out_specs=tuple(in_vmem(side)),
-        compiler_params=params(),
-    )(*scalars, *arrays)
+    )(here, *arrays)
 
 
 def pick_rows(scalars, parts, lines):
@@ -408,18 +419,17 @@
     )(*scalars, parts, *lines)
 
 
-def relay_kernel(*refs):
-    pass
-
-
-def relay(value, after):
+def join(sizes, scalars, parts, arrays, after):
+    layers, hd, rank, tokens, cols = sizes
     return pl.pallas_call(
-        relay_kernel,
-        out_shape=jax.ShapeDtypeStruct(value.shape, value.dtype),
-        in_specs=[pl.BlockSpec(memory_space=pl.ANY)] * (1 + len(after)),
-        out_specs=pl.BlockSpec(memory_space=pl.ANY),
-        input_output_aliases={0: 0},
-    )(value, *after)
+        functools.partial(join_kernel, sizes),
+        out_shape=jax.ShapeDtypeStruct(parts.shape[:2] + (3 * cols + 2 * hd,), jnp.bfloat16),
+        in_specs=in_smem(len(scalars))
+        + in_vmem(1 + len(arrays))
+        + [pl.BlockSpec(memory_space=pl.ANY)] * len(after),
+        out_specs=in_vmem(1)[0],
+        compiler_params=params(),
+    )(*scalars, parts, *arrays, *after)
 
 
 def finish(sizes, owned, gain):
@@ -446,13 +456,12 @@
         out_shape=(
             jax.ShapeDtypeStruct((width, cols), jnp.bfloat16),
             jax.ShapeDtypeStruct((width, cols), jnp.bfloat16),
-            jax.ShapeDtypeStruct((tokens, cols), jnp.bfloat16),
-            jax.ShapeDtypeStruct((tokens, cols), jnp.bfloat16),
+            jax.ShapeDtypeStruct((2 * tokens, cols), jnp.bfloat16),
             share,
             share,
         ),
         in_specs=in_smem(1) + in_vmem(len(own) + len(other) + 1),
-        out_specs=tuple(in_vmem(6)),
+        out_specs=tuple(in_vmem(5)),
         scratch_shapes=[
             pltpu.VMEM((tokens, cols), jnp.float32),
             pltpu.VMEM((tokens, cols), jnp.float32),
@@ -462,13 +471,13 @@
     )(here, *own, *other, q)
 
 
-def solve(sizes, features, here, own, other, x, s, u, v, q):
+def solve(sizes, features, here, own, other, xs, u, v, q):
     layers, hd, rank, tokens, cols = sizes
     width = layers * hd
     return pl.pallas_call(
         functools.partial(solve_kernel, sizes, features),
-        out_shape=jax.ShapeDtypeStruct(q.shape, jnp.bfloat16),
-        in_specs=in_smem(1) + [pl.BlockSpec(memory_space=pl.ANY)] * 2 + in_vmem(5),
+        out_shape=jax.ShapeDtypeStruct(q.shape[:2] + (2 * cols + 2 * hd,), jnp.bfloat16),
+        in_specs=in_smem(1) + [pl.BlockSpec(memory_space=pl.ANY)] * 2 + in_vmem(4),
         out_specs=in_vmem(1)[0],
         scratch_shapes=[
             pltpu.VMEM((tokens, width), jnp.bfloat16),
@@ -478,10 +487,10 @@
             pltpu.VMEM((layers, tokens, hd), jnp.float32),
             pltpu.VMEM((layers, tokens, 1), jnp.float32),
             pltpu.VMEM((2 * own.shape[0],) + own.shape[1:], jnp.bfloat16),
-            pltpu.SemaphoreType.DMA((2,)),
+            pltpu.SemaphoreType.DMA((2 * own.shape[0],)),
         ],
         compiler_params=params(),
-    )(here, own, other, x, s, u, v, q)
+    )(here, own, other, xs, u, v, q)
 
 
 def swap(value, axis):
@@ -521,23 +530,19 @@
     gain = norm_gain
     both_cores = [(0, 1), (1, 0)]
 
-    stored = store(
-        sizes,
-        members,
-        (value_down[0, 0], output_up_factor[0, 0], gain, value_up_factor[0, 0], out_down[0, 0]),
-    )
-    lines = spread_lines(
+    stored, *lines = pack(
         sizes,
         side,
-        (here, block_tenant, valid_tokens),
+        members,
+        here,
         (
             w_value[0],
             w_out[0],
             gain,
-            inputs[0],
-            cotangent[0],
-            lax.ppermute(inputs[0], "core", both_cores),
-            lax.ppermute(cotangent[0], "core", both_cores),
+            value_down[0, 0],
+            output_up_factor[0, 0],
+            value_up_factor[0, 0],
+            out_down[0, 0],
         ),
     )
     lines = [lines[0]] + [
@@ -549,18 +554,30 @@
         lax.ppermute(turned[step], "x", [(i, (i + step) % across) for i in range(across)])
         for step in range(1, across)
     ]
-    adapters = swap(relay(swap(adapters, "z"), turned[1:]), ("b", "x", "a"))
+    joined = join(
+        sizes,
+        (here, block_tenant, valid_tokens),
+        swap(adapters, "z"),
+        (
+            inputs[0],
+            cotangent[0],
+            lax.ppermute(inputs[0], "core", both_cores),
+            lax.ppermute(cotangent[0], "core", both_cores),
+        ),
+        turned[1:],
+    )
+    adapters = swap(joined, ("b", "x", "a"))
     pairs = across // 2
     other = [
         lax.ppermute(
-            jnp.concatenate([part[:, :hd] for part in turned[at : at + pairs]], axis=0),
+            jnp.concatenate(turned[at : at + pairs], axis=0),
             "z",
             [(i, (i + turn) % planes) for i in range(planes)],
         )
         for at, turn in ((0, 1), (pairs, -1))
     ]
 
-    u, v, x, s, kept, given = gram(sizes, side, here, turned, other, adapters)
+    u, v, rows_xs, kept, given = gram(sizes, side, here, turned, other, adapters)
     theirs = lax.ppermute(given, "core", both_cores)
     summed = (kept.astype(jnp.float32) + theirs.astype(jnp.float32)).astype(jnp.bfloat16)
     shares = swap(summed.reshape(sections // 2, -1, summed.shape[-1]), ("b", "x"))
@@ -568,7 +585,7 @@
     own = swap(jnp.broadcast_to(share[None], shares.shape), ("b", "x")).reshape(summed.shape)
     other = lax.ppermute(own, "core", both_cores)
 
-    grads = solve(sizes, features, here, own, other, x, s, u, v, adapters)
+    grads = solve(sizes, features, here, own, other, rows_xs, u, v, adapters)
 
     ids = jnp.arange(members, dtype=jnp.int32)
     tenant_hot = block_tenant[:, None] == ids[None, :]

time: 234 us -> 225 us (0.962)
  waiting for transfers between devices: 63.7 us -> 60 us
    ppermute x3, waiting for transfers between devices: 13.2 us -> 5.67 us  [body(): lax.ppermute(turned[step], 'x', [(i, (i + step) % across) for i in range(...]
    all_to_all x4, waiting for transfers between devices: 17 us -> 24 us  [swap(): return lax.all_to_all(value, axis, split_axis=0, concat_axis=0, tiled=True)]
    all_to_all x4, starting transfers between devices: 28.2 us -> 25 us  [swap(): return lax.all_to_all(value, axis, split_axis=0, concat_axis=0, tiled=True)]
    ppermute x3, waiting for transfers between devices: 13.5 us -> 11 us  [body(): lax.ppermute(lines[step], ('a', 'b'), [(i, (i + step) % side) for i in ra...]
  transfers between devices with their start and end apart: 16 -> 16, of which waited for: 11 -> 12; matrix products, arithmetic and copies ran while one was open for 1% -> 0% of each run, Pallas kernels for 0% -> 0%
where the time goes in v5:
time: 225 us; the launch traced here: 224 us
  blocking collectives  84.2 us (37%)
  waiting for transfers between devices  60 us (27%)
  starting transfers between devices  43 us (19%)
  Pallas kernels  29.6 us (13%)
  local copies, waits for them, and re-layouts  3.19 us (1%)
  other arithmetic  2.86 us (1%)
    all_to_all x4, blocking collectives, swap(): return lax.all_to_all(value, axis, split_axis=0, concat_axis=0, tiled=True)  84.2 us
    all_to_all x4, starting transfers between devices, swap(): return lax.all_to_all(value, axis, split_axis=0, concat_axis=0, tiled=True)  25 us
    all_to_all x4, waiting for transfers between devices, swap(): return lax.all_to_all(value, axis, split_axis=0, concat_axis=0, tiled=True)  24 us
    pallas_call x1, Pallas kernels, solve(): pl.pallas_call(functools.partial(solve_kernel, sizes, features), out_shap...  17.6 us
    ppermute x2, waiting for transfers between devices, body(): lax.ppermute(jnp.concatenate(turned[at:at + pairs], axis=0), 'z', [(i, (i...  12.4 us
    ppermute x3, waiting for transfers between devices, body(): lax.ppermute(lines[step], ('a', 'b'), [(i, (i + step) % side) for i in ra...  11 us
    ppermute x3, waiting for transfers between devices, body(): lax.ppermute(turned[step], 'x', [(i, (i + step) % across) for i in range(...  5.67 us
    pallas_call x1, Pallas kernels, gram(): pl.pallas_call(functools.partial(gram_kernel, sizes, side, len(own)), out...  5.07 us
  transfers between devices with their start and end apart: 16, of which 12 were waited for; matrix products, arithmetic and copies ran while one was open for 0% of the time, Pallas kernels for 0%

profile of v5, /device:TPU:1, one launch (start us, length us, event | category | flops | bytes accessed | tf_op | source)
XLA Modules:
  0.0 223.8 jit_solution(9236985310825120610)
XLA Ops:
  1.3 3.0 %shard_map.147 = (bf16[16,16,1152]{2,1,0:T(8,128)(2,1)}, bf16[4,64,512]{2,1,0:T(8,128)(2,1)}, bf16[4,64,512]{2,1,0:T(8,128)(2,1)}, bf16[4,64,512]{2,1,0:T(8,128)(2,1)}, bf16[4,64,512]{2,1,0:T(8,128)(2,1)}) custom-call(s32[2]{0:T(128)} %pad_add_fusion.here_ref, bf16[64,8192]{1,0:T(8,128)(2,1)} %bitcast.32, bf16[64,8192]{1,0:T(8,128)(2,1)} %bitcast.33, ...), custom_call_target="tpu_custom_call" | custom-call | tf_op jit(solution)/shard_map/pallas_call | solution.py:400
  4.3 10.0 %all-to-all-start = ((bf16[16,16,1152]{2,1,0:T(8,128)(2,1)}), bf16[16,16,1152]{2,1,0:T(8,128)(2,1)S(1)}, u32[]{:S(2)}, u32[]{:S(2)}) async-start(bf16[16,16,1152]{2,1,0:T(8,128)(2,1)} %get-tuple-element.23), calls=%async_computation | async-start | bytes 1179648 | tf_op jit(solution)/shard_map/all_to_all | solution.py:497
  15.6 2.6 %collective-permute-start.1 = (bf16[4,64,512]{2,1,0:T(8,128)(2,1)}, bf16[4,64,512]{2,1,0:T(8,128)(2,1)S(1)}, u32[]{:S(2)}, u32[]{:S(2)}) collective-permute-start(bf16[4,64,512]{2,1,0:T(8,128)(2,1)} %get-tuple-element.26), channel_id=1, source_target_pairs={{0,128},{64,192},{128,0},{192,64},{1,129},{65,193},{129,1},{193,65... | collective-permute-start | bytes 786440 | tf_op jit(solution)/shard_map/ppermute | solution.py:549
  19.2 4.3 %collective-permute-done.refs_1_ = bf16[4,64,512]{2,1,0:T(8,128)(2,1)S(1)} collective-permute-done((bf16[4,64,512]{2,1,0:T(8,128)(2,1)}, bf16[4,64,512]{2,1,0:T(8,128)(2,1)S(1)}, u32[]{:S(2)}, u32[]{:S(2)}) %collective-permute-start) | collective-permute-done | bytes 262176 | tf_op jit(solution)/shard_map/ppermute | solution.py:549
  23.5 6.7 %collective-permute-done.1.refs_2_ = bf16[4,64,512]{2,1,0:T(8,128)(2,1)S(1)} collective-permute-done((bf16[4,64,512]{2,1,0:T(8,128)(2,1)}, bf16[4,64,512]{2,1,0:T(8,128)(2,1)S(1)}, u32[]{:S(2)}, u32[]{:S(2)}) %collective-permute-start.1) | collective-permute-done | bytes 262176 | tf_op jit(solution)/shard_map/ppermute | solution.py:549
  30.3 2.6 %all-to-all-done.parts_ref = bf16[16,16,1152]{2,1,0:T(8,128)(2,1)S(1)} async-done(((bf16[16,16,1152]{2,1,0:T(8,128)(2,1)}), bf16[16,16,1152]{2,1,0:T(8,128)(2,1)S(1)}, u32[]{:S(2)}, u32[]{:S(2)}) %all-to-all-start) | async-done | bytes 589856 | tf_op jit(solution)/shard_map/all_to_all | solution.py:497
  35.4 3.7 %all-to-all-start.1 = ((bf16[16,16,1152]{2,1,0:T(8,128)(2,1)}), bf16[16,16,1152]{2,1,0:T(8,128)(2,1)S(1)}, u32[]{:S(2)}, u32[]{:S(2)}) async-start(bf16[16,16,1152]{2,1,0:T(8,128)(2,1)} %get-tuple-element.32), calls=%async_computation.1 | async-start | bytes 1179648 | tf_op jit(solution)/shard_map/all_to_all | solution.py:497
  40.3 2.5 %collective-permute-start.4 = (bf16[4,64,512]{2,1,0:T(8,128)(2,1)S(1)}, bf16[4,64,512]{2,1,0:T(8,128)(2,1)S(1)}, u32[]{:S(2)}, u32[]{:S(2)}) collective-permute-start(bf16[4,64,512]{2,1,0:T(8,128)(2,1)S(1)} %get-tuple-element.30), channel_id=1, source_target_pairs={{0,32},{16,48},{32,0},{48,16},{1,33},{17,49},{33,1},{49,17},{2,34}... | collective-permute-start | bytes 786440 | tf_op jit(solution)/shard_map/ppermute | solution.py:554
  43.9 2.3 %collective-permute-start.8 = (bf16[8,8192]{1,0:T(8,128)(2,1)S(1)}, bf16[8,8192]{1,0:T(8,128)(2,1)S(1)}, u32[]{:S(2)}, u32[]{:S(2)}) collective-permute-start(bf16[8,8192]{1,0:T(8,128)(2,1)S(1)} %bitcast.23), channel_id=1, source_target_pairs={{0,1},{1,0},{2,3},{3,2},{4,5},{5,4},{6,7},{7,6},{8,9},{9,8},{10,11... | collective-permute-start | bytes 393224 | tf_op jit(solution)/shard_map/ppermute | solution.py:564
  47.6 5.7 %collective-permute-done.4.refs_1_.refs_2_ = bf16[4,64,512]{2,1,0:T(8,128)(2,1)S(1)} collective-permute-done((bf16[4,64,512]{2,1,0:T(8,128)(2,1)S(1)}, bf16[4,64,512]{2,1,0:T(8,128)(2,1)S(1)}, u32[]{:S(2)}, u32[]{:S(2)}) %collective-permute-start.4) | collective-permute-done | bytes 262176 | tf_op jit(solution)/shard_map/ppermute | solution.py:554
  53.3 4.0 %all-to-all-done.1.parts_ref = bf16[16,16,1152]{2,1,0:T(8,128)(2,1)S(1)} async-done(((bf16[16,16,1152]{2,1,0:T(8,128)(2,1)}), bf16[16,16,1152]{2,1,0:T(8,128)(2,1)S(1)}, u32[]{:S(2)}, u32[]{:S(2)}) %all-to-all-start.1) | async-done | bytes 589856 | tf_op jit(solution)/shard_map/all_to_all | solution.py:497
  58.8 7.7 %all-to-all-start.2 = ((bf16[16,16,1664]{2,1,0:T(8,128)(2,1)}), bf16[16,16,1664]{2,1,0:T(8,128)(2,1)S(1)}, u32[]{:S(2)}, u32[]{:S(2)}) async-start(bf16[16,16,1664]{2,1,0:T(8,128)(2,1)} %shard_map.149), calls=%async_computation.2 | async-start | bytes 1703936 | tf_op jit(solution)/shard_map/all_to_all | solution.py:497
  68.3 11.1 %collective-permute-done.7.refs_5_ = bf16[8,64,512]{2,1,0:T(8,128)(2,1)S(1)} collective-permute-done((bf16[8,64,512]{2,1,0:T(8,128)(2,1)S(1)}, bf16[8,64,512]{2,1,0:T(8,128)(2,1)S(1)}, u32[]{:S(2)}, u32[]{:S(2)}) %collective-permute-start.7) | collective-permute-done | bytes 524320 | tf_op jit(solution)/shard_map/ppermute | solution.py:572
  82.6 5.1 %shard_map.150 = (bf16[1024,512]{1,0:T(8,128)(2,1)S(1)}, bf16[1024,512]{1,0:T(8,128)(2,1)S(1)}, bf16[256,512]{1,0:T(8,128)(2,1)S(1)}, bf16[4,1344,128]{2,1,0:T(8,128)(2,1)S(1)}, bf16[4,1344,128]{2,1,0:T(8,128)(2,1)S(1)}) custom-call(s32[2]{0:T(128)S(1)} %copy-done.10, bf16[4,64,512]{2,1,0:T(8,128)(2,1)S(1)} %get-tuple-element.28.refs_0_, ...), custom_call_target="tpu_custom_call" | custom-call | tf_op jit(solution)/shard_map/pallas_call | solution.py:454
  89.4 2.8 %collective-permute-done.10 = bf16[4,1344,128]{2,1,0:T(8,128)(2,1)S(1)} collective-permute-done((bf16[4,1344,128]{2,1,0:T(8,128)(2,1)S(1)}, bf16[4,1344,128]{2,1,0:T(8,128)(2,1)S(1)}, u32[]{:S(2)}, u32[]{:S(2)}) %collective-permute-start.10) | collective-permute-done | bytes 1376288 | tf_op jit(solution)/shard_map/ppermute | solution.py:581
  92.6 24.1 %all_to_all.40 = bf16[8,672,128]{2,1,0:T(8,128)(2,1)} all-to-all(bf16[8,672,128]{2,1,0:T(8,128)(2,1)S(1)} %bitcast.27), channel_id=1, replica_groups=mesh['a'=2,'b'=2,'x'=4,'z'=8,'core'=2] {'b','x'}, dimensions={0} | all-to-all | bytes 2752512 | tf_op jit(solution)/shard_map/all_to_all | solution.py:497
  118.5 20.4 %all_to_all.41 = bf16[8,672,128]{2,1,0:T(8,128)(2,1)S(1)} all-to-all(bf16[8,672,128]{2,1,0:T(8,128)(2,1)S(1)} %broadcast_in_dim.37), channel_id=1, replica_groups=mesh['a'=2,'b'=2,'x'=4,'z'=8,'core'=2] {'b','x'}, dimensions={0} | all-to-all | bytes 2752512 | tf_op jit(solution)/shard_map/all_to_all | solution.py:497
  138.9 2.4 %collective-permute-start.11 = (bf16[4,1344,128]{2,1,0:T(8,128)(2,1)S(1)}, bf16[4,1344,128]{2,1,0:T(8,128)(2,1)S(1)}, u32[]{:S(2)}, u32[]{:S(2)}) collective-permute-start(bf16[4,1344,128]{2,1,0:T(8,128)(2,1)S(1)} %bitcast.21), channel_id=1, source_target_pairs={{0,1},{1,0},{2,3},{3,2},{4,5},{5,4},{6,7},{7,6},{8,9},{9,8},{10,11... | collective-permute-start | bytes 4128776 | tf_op jit(solution)/shard_map/ppermute | solution.py:586
  141.3 2.8 %collective-permute-done.11.other_ref = bf16[4,1344,128]{2,1,0:T(8,128)(2,1)S(1)} collective-permute-done((bf16[4,1344,128]{2,1,0:T(8,128)(2,1)S(1)}, bf16[4,1344,128]{2,1,0:T(8,128)(2,1)S(1)}, u32[]{:S(2)}, u32[]{:S(2)}) %collective-permute-start.11) | collective-permute-done | bytes 1376288 | tf_op jit(solution)/shard_map/ppermute | solution.py:586
  144.0 17.6 %shard_map.151 = bf16[16,16,1152]{2,1,0:T(8,128)(2,1)S(1)} custom-call(s32[2]{0:T(128)S(1)} %copy-done.10, bf16[4,1344,128]{2,1,0:T(8,128)(2,1)S(1)} %bitcast.22, bf16[4,1344,128]{2,1,0:T(8,128)(2,1)S(1)} %collective-permute-done.11.other_ref, bf16[256,512]{1,0:T(8,128)(2,1)S(1)} %copy-done.6, bf16[1024,512]{1,0:T(8,128)(2,1)S(1)} %get-tuple-element.36.u_ref, ...), custom_call_target="tpu_custom_call" | custom-call | tf_op jit(solution)/shard_map/pallas_call | solution.py:477
  161.7 16.0 %all_to_all.42 = bf16[16,16,1152]{2,1,0:T(8,128)(2,1)} all-to-all(bf16[16,16,1152]{2,1,0:T(8,128)(2,1)S(1)} %shard_map.151), channel_id=1, replica_groups=mesh['a'=2,'b'=2,'x'=4,'z'=8,'core'=2] {'b','x','a'}, dimensions={0} | all-to-all | bytes 1179648 | tf_op jit(solution)/shard_map/all_to_all | solution.py:497
  177.7 3.5 %all-to-all-start.6 = ((bf16[16,16,1152]{2,1,0:T(8,128)(2,1)}), bf16[16,16,1152]{2,1,0:T(8,128)(2,1)S(1)}, u32[]{:S(2)}, u32[]{:S(2)}) async-start(bf16[16,16,1152]{2,1,0:T(8,128)(2,1)} %all_to_all.42), calls=%async_computation.6 | async-start | bytes 1179648 | tf_op jit(solution)/shard_map/all_to_all | solution.py:497
  181.4 17.4 %all-to-all-done.6 = bf16[16,16,1152]{2,1,0:T(8,128)(2,1)S(1)} async-done(((bf16[16,16,1152]{2,1,0:T(8,128)(2,1)}), bf16[16,16,1152]{2,1,0:T(8,128)(2,1)S(1)}, u32[]{:S(2)}, u32[]{:S(2)}) %all-to-all-start.6) | async-done | bytes 589856 | tf_op jit(solution)/shard_map/all_to_all | solution.py:497
  199.3 23.6 %all_to_all.43.owned_ref = bf16[16,16,1152]{2,1,0:T(8,128)(2,1)S(1)} all-to-all(bf16[16,16,1152]{2,1,0:T(8,128)(2,1)S(1)} %bitcast.31), channel_id=1, replica_groups=mesh['a'=2,'b'=2,'x'=4,'z'=8,'core'=2] {'z','core'}, dimensions={0} | all-to-all | bytes 1179648 | tf_op jit(solution)/shard_map/all_to_all | solution.py:497
  (56 shorter events, 21.1 us)
Async XLA Ops:
  1.3 31.6 %copy-start.10 = (s32[2]{0:T(128)S(1)}, s32[2]{0:T(128)}, u32[]{:S(2)}) copy-start(s32[2]{0:T(128)} %pad_add_fusion.here_ref) | copy-start | bytes 28
  1.3 31.6 %copy-start.11 = (s32[16]{0:T(128)S(1)}, s32[16]{0:T(128)}, u32[]{:S(2)}) copy-start(s32[16]{0:T(128)} %tenant_ref.3) | copy-start | bytes 196
  1.3 31.6 %copy-start.12 = (s32[16]{0:T(128)S(1)}, s32[16]{0:T(128)}, u32[]{:S(2)}) copy-start(s32[16]{0:T(128)} %slot_ref.1) | copy-start | bytes 196
  4.3 28.6 %all-to-all-start = ((bf16[16,16,1152]{2,1,0:T(8,128)(2,1)}), bf16[16,16,1152]{2,1,0:T(8,128)(2,1)S(1)}, u32[]{:S(2)}, u32[]{:S(2)}) async-start(bf16[16,16,1152]{2,1,0:T(8,128)(2,1)} %get-tuple-element.23), calls=%async_computation | async-start | bytes 1179648 | tf_op jit(solution)/shard_map/all_to_all | solution.py:497
  14.3 9.3 %collective-permute-start = (bf16[4,64,512]{2,1,0:T(8,128)(2,1)}, bf16[4,64,512]{2,1,0:T(8,128)(2,1)S(1)}, u32[]{:S(2)}, u32[]{:S(2)}) collective-permute-start(bf16[4,64,512]{2,1,0:T(8,128)(2,1)} %get-tuple-element.25), channel_id=1, source_target_pairs={{0,64},{64,128},{128,192},{192,0},{1,65},{65,129},{129,193},{193,1... | collective-permute-start | bytes 786440 | tf_op jit(solution)/shard_map/ppermute | solution.py:549
  15.6 14.7 %collective-permute-start.1 = (bf16[4,64,512]{2,1,0:T(8,128)(2,1)}, bf16[4,64,512]{2,1,0:T(8,128)(2,1)S(1)}, u32[]{:S(2)}, u32[]{:S(2)}) collective-permute-start(bf16[4,64,512]{2,1,0:T(8,128)(2,1)} %get-tuple-element.26), channel_id=1, source_target_pairs={{0,128},{64,192},{128,0},{192,64},{1,129},{65,193},{129,1},{193,65... | collective-permute-start | bytes 786440 | tf_op jit(solution)/shard_map/ppermute | solution.py:549
  18.2 12.1 %collective-permute-start.2 = (bf16[4,64,512]{2,1,0:T(8,128)(2,1)}, bf16[4,64,512]{2,1,0:T(8,128)(2,1)S(1)}, u32[]{:S(2)}, u32[]{:S(2)}) collective-permute-start(bf16[4,64,512]{2,1,0:T(8,128)(2,1)} %get-tuple-element.27), channel_id=1, source_target_pairs={{0,192},{64,0},{128,64},{192,128},{1,193},{65,1},{129,65},{193,129... | collective-permute-start | bytes 786440 | tf_op jit(solution)/shard_map/ppermute | solution.py:549
  33.9 12.4 %copy-start.9 = (bf16[1,8,8192]{2,1,0:T(8,128)(2,1)S(1)}, bf16[1,8,8192]{2,1,0:T(8,128)(2,1)}, u32[]{:S(2)}) copy-start(bf16[1,8,8192]{2,1,0:T(8,128)(2,1)} %param.13) | copy-start | bytes 393220
  33.9 23.4 %copy-start.13 = (s32[16]{0:T(128)S(1)}, s32[16]{0:T(128)}, u32[]{:S(2)}) copy-start(s32[16]{0:T(128)} %valid_ref.1) | copy-start | bytes 196
  35.4 21.9 %all-to-all-start.1 = ((bf16[16,16,1152]{2,1,0:T(8,128)(2,1)}), bf16[16,16,1152]{2,1,0:T(8,128)(2,1)S(1)}, u32[]{:S(2)}, u32[]{:S(2)}) async-start(bf16[16,16,1152]{2,1,0:T(8,128)(2,1)} %get-tuple-element.32), calls=%async_computation.1 | async-start | bytes 1179648 | tf_op jit(solution)/shard_map/all_to_all | solution.py:497
  39.1 8.5 %collective-permute-start.3 = (bf16[4,64,512]{2,1,0:T(8,128)(2,1)S(1)}, bf16[4,64,512]{2,1,0:T(8,128)(2,1)S(1)}, u32[]{:S(2)}, u32[]{:S(2)}) collective-permute-start(bf16[4,64,512]{2,1,0:T(8,128)(2,1)S(1)} %get-tuple-element.29), channel_id=1, source_target_pairs={{0,16},{16,32},{32,48},{48,0},{1,17},{17,33},{33,49},{49,1},{2,18}... | collective-permute-start | bytes 786440 | tf_op jit(solution)/shard_map/ppermute | solution.py:554
  40.3 12.9 %collective-permute-start.4 = (bf16[4,64,512]{2,1,0:T(8,128)(2,1)S(1)}, bf16[4,64,512]{2,1,0:T(8,128)(2,1)S(1)}, u32[]{:S(2)}, u32[]{:S(2)}) collective-permute-start(bf16[4,64,512]{2,1,0:T(8,128)(2,1)S(1)} %get-tuple-element.30), channel_id=1, source_target_pairs={{0,32},{16,48},{32,0},{48,16},{1,33},{17,49},{33,1},{49,17},{2,34}... | collective-permute-start | bytes 786440 | tf_op jit(solution)/shard_map/ppermute | solution.py:554
  42.8 10.5 %collective-permute-start.5 = (bf16[4,64,512]{2,1,0:T(8,128)(2,1)S(1)}, bf16[4,64,512]{2,1,0:T(8,128)(2,1)S(1)}, u32[]{:S(2)}, u32[]{:S(2)}) collective-permute-start(bf16[4,64,512]{2,1,0:T(8,128)(2,1)S(1)} %get-tuple-element.31), channel_id=1, source_target_pairs={{0,48},{16,0},{32,16},{48,32},{1,49},{17,1},{33,17},{49,33},{2,50}... | collective-permute-start | bytes 786440 | tf_op jit(solution)/shard_map/ppermute | solution.py:554
  43.9 3.3 %collective-permute-start.8 = (bf16[8,8192]{1,0:T(8,128)(2,1)S(1)}, bf16[8,8192]{1,0:T(8,128)(2,1)S(1)}, u32[]{:S(2)}, u32[]{:S(2)}) collective-permute-start(bf16[8,8192]{1,0:T(8,128)(2,1)S(1)} %bitcast.23), channel_id=1, source_target_pairs={{0,1},{1,0},{2,3},{3,2},{4,5},{5,4},{6,7},{7,6},{8,9},{9,8},{10,11... | collective-permute-start | bytes 393224 | tf_op jit(solution)/shard_map/ppermute | solution.py:564
  46.3 1.3 collective-permute-start.9
  58.8 22.7 %all-to-all-start.2 = ((bf16[16,16,1664]{2,1,0:T(8,128)(2,1)}), bf16[16,16,1664]{2,1,0:T(8,128)(2,1)S(1)}, u32[]{:S(2)}, u32[]{:S(2)}) async-start(bf16[16,16,1664]{2,1,0:T(8,128)(2,1)} %shard_map.149), calls=%async_computation.2 | async-start | bytes 1703936 | tf_op jit(solution)/shard_map/all_to_all | solution.py:497
  66.6 12.8 %collective-permute-start.7 = (bf16[8,64,512]{2,1,0:T(8,128)(2,1)S(1)}, bf16[8,64,512]{2,1,0:T(8,128)(2,1)S(1)}, u32[]{:S(2)}, u32[]{:S(2)}) collective-permute-start(bf16[8,64,512]{2,1,0:T(8,128)(2,1)S(1)} %pad_maximum_fusion.1), channel_id=1, source_target_pairs={{0,14},{2,0},{4,2},{6,4},{8,6},{10,8},{12,10},{14,12},{1,15},{3,1}... | collective-permute-start | bytes 1572872 | tf_op jit(solution)/shard_map/ppermute | solution.py:572
  66.8 14.0 %collective-permute-start.6 = (bf16[8,64,512]{2,1,0:T(8,128)(2,1)S(1)}, bf16[8,64,512]{2,1,0:T(8,128)(2,1)S(1)}, u32[]{:S(2)}, u32[]{:S(2)}) collective-permute-start(bf16[8,64,512]{2,1,0:T(8,128)(2,1)S(1)} %pad_maximum_fusion), channel_id=1, source_target_pairs={{0,2},{2,4},{4,6},{6,8},{8,10},{10,12},{12,14},{14,0},{1,3},{3,5},... | collective-permute-start | bytes 1572872 | tf_op jit(solution)/shard_map/ppermute | solution.py:572
  87.7 4.5 %collective-permute-start.10 = (bf16[4,1344,128]{2,1,0:T(8,128)(2,1)S(1)}, bf16[4,1344,128]{2,1,0:T(8,128)(2,1)S(1)}, u32[]{:S(2)}, u32[]{:S(2)}) collective-permute-start(bf16[4,1344,128]{2,1,0:T(8,128)(2,1)S(1)} %get-tuple-element.34), channel_id=1, source_target_pairs={{0,1},{1,0},{2,3},{3,2},{4,5},{5,4},{6,7},{7,6},{8,9},{9,8},{10,11... | collective-permute-start | bytes 4128776 | tf_op jit(solution)/shard_map/ppermute | solution.py:581
  118.4 25.6 %copy-start.1 = (bf16[1024,512]{1,0:T(8,128)(2,1)S(1)}, bf16[1024,512]{1,0:T(8,128)(2,1)}, u32[]{:S(2)}) copy-start(bf16[1024,512]{1,0:T(8,128)(2,1)} %copy-done) | copy-start | bytes 3145732
  118.4 25.6 %copy-start.6 = (bf16[256,512]{1,0:T(8,128)(2,1)S(1)}, bf16[256,512]{1,0:T(8,128)(2,1)}, u32[]{:S(2)}) copy-start(bf16[256,512]{1,0:T(8,128)(2,1)} %copy-done.5) | copy-start | bytes 786436
  138.9 5.2 %collective-permute-start.11 = (bf16[4,1344,128]{2,1,0:T(8,128)(2,1)S(1)}, bf16[4,1344,128]{2,1,0:T(8,128)(2,1)S(1)}, u32[]{:S(2)}, u32[]{:S(2)}) collective-permute-start(bf16[4,1344,128]{2,1,0:T(8,128)(2,1)S(1)} %bitcast.21), channel_id=1, source_target_pairs={{0,1},{1,0},{2,3},{3,2},{4,5},{5,4},{6,7},{7,6},{8,9},{9,8},{10,11... | collective-permute-start | bytes 4128776 | tf_op jit(solution)/shard_map/ppermute | solution.py:586
  177.7 21.2 %all-to-all-start.6 = ((bf16[16,16,1152]{2,1,0:T(8,128)(2,1)}), bf16[16,16,1152]{2,1,0:T(8,128)(2,1)S(1)}, u32[]{:S(2)}, u32[]{:S(2)}) async-start(bf16[16,16,1152]{2,1,0:T(8,128)(2,1)} %all_to_all.42), calls=%async_computation.6 | async-start | bytes 1179648 | tf_op jit(solution)/shard_map/all_to_all | solution.py:497
  199.3 23.7 %copy-start.7 = (f32[1,8192]{1,0:T(1,128)S(1)}, f32[1,8192]{1,0:T(1,128)}, u32[]{:S(2)}) copy-start(f32[1,8192]{1,0:T(1,128)} %gain_ref.3) | copy-start | bytes 98308
  (6 other events, 22.7 us)

commit v6 on v5

--- a/solution.py
+++ b/solution.py
@@ -12,6 +12,7 @@
 block = 256
 vmem_bytes = 20 * 1024 * 1024
 whole_vmem_bytes = 56 * 1024 * 1024
+merge_cost_bytes = 4 * 1024 * 1024
 pipe = ("a", "b", "x")
 dp = ("z", "core")
 
@@ -113,14 +114,24 @@
 
 
 def pick_kernel(side, across, here_ref, tenant_ref, slot_ref, parts_ref, *refs):
-    lines, out_ref, turned = refs[:side], refs[side], refs[side + 1 :]
+    lines, out_ref, turned, sems = refs[:side], refs[side], refs[side + 1 : -1], refs[-1]
+    place = lax.rem(here_ref[0], across)
+    copies = [
+        pltpu.make_async_copy(
+            lines[0].at[lax.rem(place + step, across)], turned_ref.at[0], sems.at[step]
+        )
+        for step, turned_ref in enumerate(turned)
+    ]
+    for copy in copies:
+        copy.start()
     for j in range(out_ref.shape[0]):
         out_ref[j] = parts_ref[slot_ref[tenant_ref[j]]]
-    place = lax.rem(here_ref[0], across)
     for step, turned_ref in enumerate(turned):
         at = lax.rem(place + step, across)
-        for k in range(side):
+        for k in range(1, side):
             turned_ref[k] = lines[k][at]
+    for copy in copies:
+        copy.wait()
 
 
 def finish_kernel(sizes, owned_ref, gain_ref, gvd_ref, gvu_ref, god_ref, gou_ref):
@@ -141,39 +152,68 @@
     return l % (layers // 2) * 2 + l // (layers // 2)
 
 
-def gram_kernel(sizes, side, across, here_ref, *refs):
-    layers, hd, rank, tokens, cols = sizes
-    own_refs, other_refs, refs = refs[:across], refs[across : across + 2], refs[across + 2 :]
+def merge_kernel(sizes, side, across, here_ref, *refs):
+    layers, hd, rank, tokens, cols = sizes
+    own_refs, other_refs, (u_ref, v_ref) = refs[:across], refs[across:-2], refs[-2:]
     pairs = across // 2
-    q_ref, u_ref, v_ref, xs_ref, keep_ref, give_ref, x_wide, s_wide, w_wide = refs
-    rows = tokens // layers
     part = hd // 2
-    section, core = here_ref[0], lax.rem(here_ref[1], 2)
     plane = lax.rem(here_ref[1] // 2, 2)
-    line, place = section // across, lax.rem(section, across)
-    mine = pl.ds(pl.multiple_of(plane * part, part), part)
-    theirs = pl.ds(pl.multiple_of((1 - plane) * part, part), part)
+    line, place = here_ref[0] // across, lax.rem(here_ref[0], across)
     for step in range(layers):
         dx, dy = step // side, step % side
         l = lax.rem(line + side - dy, side) * across + lax.rem(place + across - dx, across)
-        slot = step % 2
-        for kind in range(2):
-            at = pl.ds(kind * part, part)
-            w_wide[slot, kind, mine, :] = own_refs[dx][dy, at, :].astype(jnp.float32)
-            w_wide[slot, kind, theirs, :] = other_refs[dx // pairs][
-                dx % pairs * side + dy, at, :
-            ].astype(jnp.float32)
+        own, other = own_refs[dx][dy], other_refs[dx // pairs][dx % pairs * side + dy]
+        mine = pl.ds(pl.multiple_of(l * hd + plane * part, part), part)
+        theirs = pl.ds(pl.multiple_of(l * hd + (1 - plane) * part, part), part)
+        v_ref[mine, :] = own[:part]
+        u_ref[mine, :] = own[part:]
+        v_ref[theirs, :] = other[:part]
+        u_ref[theirs, :] = other[part:]
+
+
+def gram_kernel(
+    sizes,
+    here_ref,
+    wo_ref,
+    wv_ref,
+    q_ref,
+    u_ref,
+    v_ref,
+    xs_ref,
+    keep_ref,
+    give_ref,
+    x_wide,
+    s_wide,
+    sems,
+):
+    layers, hd, rank, tokens, cols = sizes
+    rows = tokens // layers
+    core = lax.rem(here_ref[1], 2)
+    copies = [
+        pltpu.make_async_copy(wo_ref, u_ref, sems.at[0]),
+        pltpu.make_async_copy(wv_ref, v_ref, sems.at[1]),
+    ]
+    for copy in copies:
+        copy.start()
+    for l in range(layers):
+        both = q_ref[turned_index(l, layers), :, 2 * cols + 2 * hd :].astype(jnp.float32)
+        at = pl.ds(l * rows, rows)
+        x_wide[at, :] = both[:rows]
+        s_wide[at, :] = both[rows:]
+    for copy in copies:
+        copy.wait()
+    for l in range(layers):
         q_l = q_ref[turned_index(l, layers)]
         small = q_l[:, 2 * cols : 2 * cols + 2 * hd]
         delta_v = mm_tn(small[:, :hd], q_l[:, :cols])
         delta_u = mm_tn(small[:, hd:], q_l[:, cols : 2 * cols])
-        at = pl.ds(pl.multiple_of(l * hd, hd), hd)
-        v_ref[at, :] = (w_wide[slot, 0] + adapter_scale * delta_v).astype(jnp.bfloat16)
-        u_ref[at, :] = (w_wide[slot, 1] + adapter_scale * delta_u).astype(jnp.bfloat16)
-        both = q_l[:, 2 * cols + 2 * hd :].astype(jnp.float32)
-        at = pl.ds(pl.multiple_of(l * rows, rows), rows)
-        x_wide[at, :] = both[:rows]
-        s_wide[at, :] = both[rows:]
+        at = pl.ds(l * hd, hd)
+        v_ref[at, :] = (v_ref[at, :].astype(jnp.float32) + adapter_scale * delta_v).astype(
+            jnp.bfloat16
+        )
+        u_ref[at, :] = (u_ref[at, :].astype(jnp.float32) + adapter_scale * delta_u).astype(
+            jnp.bfloat16
+        )
     xs_ref[:tokens, :] = x_wide[...].astype(jnp.bfloat16)
     xs_ref[tokens:, :] = s_wide[...].astype(jnp.bfloat16)
     width = layers * hd
@@ -303,24 +343,6 @@
         square = square + jnp.sum(wide * (b + after), axis=1, keepdims=True)
         bp_ref[l] = after
 
-    pull = jnp.zeros((tokens, 1), jnp.float32)
-    for l in range(layers - 1, -1, -1):
-        pair = l // 2
-        p = half(k_ref[pair, 2 * tokens : 3 * tokens, :], l).astype(jnp.float32)
-        if l < layers - 1:
-            w = upto(l)
-            top = width - hd
-            p = p - pull * bp_ref[l]
-            p = p + mm_nt(d_ref[:, w:], across_row(l, w, width))
-            if w < top:
-                p = p - half(mm(ec_ref[:, w:top], k_ref[pair, base + w : base + top, :]), l)
-        inverse = inv_ref[l]
-        d_ref[:, l * hd : (l + 1) * hd] = (inverse * p).astype(jnp.bfloat16)
-        c = c_ref[:, l * hd : (l + 1) * hd].astype(jnp.float32)
-        ec_ref[:, l * hd : (l + 1) * hd] = (pull * c).astype(jnp.bfloat16)
-        correction = jnp.sum(p * a_ref[l], axis=1, keepdims=True) / features
-        pull = pull + inverse * inverse * inverse * correction
-
     below = layer_mask(block, block, hd, lambda r, c: r > c)
     upto_diag = layer_mask(block, block, hd, lambda r, c: r >= c)
     group = block // hd
@@ -335,7 +357,7 @@
         tall = jnp.concatenate(parts, axis=0)
         return jnp.where(diagonal, side_by_side([tall] * group), jnp.zeros((), jnp.bfloat16))
 
-    for start in range(0, width, block):
+    def weight_gradients(start):
         stop = start + block
         mine = pl.ds(start, block)
         c_t = c_ref[:, mine].T
@@ -345,12 +367,15 @@
         m = [jnp.where(below, mm(d_t, c_ref[:, mine]), 0.0).astype(jnp.bfloat16)]
         if start:
             m = [mm(d_t, c_ref[:, :start]).astype(jnp.bfloat16)] + m
+        yield
         y = mm(d_t, xs_ref[:tokens, :]) + mm(side_by_side(m), u_ref[:stop, :])
-
+        yield
         m = [jnp.where(upto_diag, 0.0, mm(c_t, d_ref[:, mine])).astype(jnp.bfloat16)]
         if stop < width:
             m = m + [mm(c_t, d_ref[:, stop:]).astype(jnp.bfloat16)]
+        yield
         z = mm(side_by_side([-ec_t, c_t]), xs_ref[...]) + mm(side_by_side(m), v_ref[start:, :])
+        yield
         m = [
             jnp.where(upto_diag, mm(ec_t, c_ref[:, mine]), mm(c_t, ec_ref[:, mine])).astype(
                 jnp.bfloat16
@@ -360,8 +385,9 @@
             m = [mm(ec_t, c_ref[:, :start]).astype(jnp.bfloat16)] + m
         if stop < width:
             m = m + [mm(c_t, ec_ref[:, stop:]).astype(jnp.bfloat16)]
+        yield
         z = z - mm(side_by_side(m), u_ref[...])
-
+        yield
         y = y.astype(jnp.bfloat16)
         z = z.astype(jnp.bfloat16)
         places = [turned_index(l, layers) for l in range(start // hd, stop // hd)]
@@ -380,6 +406,33 @@
             )
             out_ref[at, :, 2 * cols :] = (adapter_scale * tail).astype(jnp.bfloat16)
 
+    pull = jnp.zeros((tokens, 1), jnp.float32)
+    pending = iter(())
+    for l in range(layers - 1, -1, -1):
+        pair = l // 2
+        p = half(k_ref[pair, 2 * tokens : 3 * tokens, :], l).astype(jnp.float32)
+        if l < layers - 1:
+            w = upto(l)
+            top = width - hd
+            p = p - pull * bp_ref[l]
+            p = p + mm_nt(d_ref[:, w:], across_row(l, w, width))
+            if w < top:
+                p = p - half(mm(ec_ref[:, w:top], k_ref[pair, base + w : base + top, :]), l)
+        next(pending, None)
+        inverse = inv_ref[l]
+        d_ref[:, l * hd : (l + 1) * hd] = (inverse * p).astype(jnp.bfloat16)
+        c = c_ref[:, l * hd : (l + 1) * hd].astype(jnp.float32)
+        ec_ref[:, l * hd : (l + 1) * hd] = (pull * c).astype(jnp.bfloat16)
+        correction = jnp.sum(p * a_ref[l], axis=1, keepdims=True) / features
+        pull = pull + inverse * inverse * inverse * correction
+        next(pending, None)
+        if l * hd % block == 0:
+            for _ in pending:
+                pass
+            pending = weight_gradients(l * hd)
+    for _ in pending:
+        pass
+
 
 def params(limit=vmem_bytes):
     return pltpu.CompilerParams(vmem_limit_bytes=limit)
@@ -413,8 +466,12 @@
     return pl.pallas_call(
         functools.partial(pick_kernel, side, across),
         out_shape=(jax.ShapeDtypeStruct(parts.shape, parts.dtype),) + (turned,) * across,
-        in_specs=in_smem(len(scalars)) + in_vmem(1 + side),
+        in_specs=in_smem(len(scalars))
+        + in_vmem(1)
+        + [pl.BlockSpec(memory_space=pl.ANY)]
+        + in_vmem(side - 1),
         out_specs=tuple(in_vmem(1 + across)),
+        scratch_shapes=[pltpu.SemaphoreType.DMA((across,))],
         compiler_params=params(),
     )(*scalars, parts, *lines)
 
@@ -445,30 +502,46 @@
     )(owned, gain)
 
 
-def gram(sizes, side, here, own, other, q):
+def merge(sizes, side, here, own, other):
+    layers, hd, rank, tokens, cols = sizes
+    table = jax.ShapeDtypeStruct((layers * hd, cols), jnp.bfloat16)
+    return pl.pallas_call(
+        functools.partial(merge_kernel, sizes, side, len(own)),
+        out_shape=(table, table),
+        in_specs=in_smem(1) + in_vmem(len(own) + len(other)),
+        out_specs=tuple(in_vmem(2)),
+        compiler_params=params(),
+        cost_estimate=pl.CostEstimate(
+            flops=0, bytes_accessed=merge_cost_bytes, transcendentals=0
+        ),
+    )(here, *own, *other)
+
+
+def gram(sizes, here, w_out, w_value, q):
     layers, hd, rank, tokens, cols = sizes
     width = layers * hd
     share = jax.ShapeDtypeStruct(
         (width // (4 * hd), 3 * tokens + width - hd, 2 * hd), jnp.bfloat16
     )
+    table = jax.ShapeDtypeStruct((width, cols), jnp.bfloat16)
     return pl.pallas_call(
-        functools.partial(gram_kernel, sizes, side, len(own)),
+        functools.partial(gram_kernel, sizes),
         out_shape=(
-            jax.ShapeDtypeStruct((width, cols), jnp.bfloat16),
-            jax.ShapeDtypeStruct((width, cols), jnp.bfloat16),
+            table,
+            table,
             jax.ShapeDtypeStruct((2 * tokens, cols), jnp.bfloat16),
             share,
             share,
         ),
-        in_specs=in_smem(1) + in_vmem(len(own) + len(other) + 1),
+        in_specs=in_smem(1) + [pl.BlockSpec(memory_space=pl.ANY)] * 2 + in_vmem(1),
         out_specs=tuple(in_vmem(5)),
         scratch_shapes=[
             pltpu.VMEM((tokens, cols), jnp.float32),
             pltpu.VMEM((tokens, cols), jnp.float32),
-            pltpu.VMEM((2, 2, hd, cols), jnp.float32),
+            pltpu.SemaphoreType.DMA((2,)),
         ],
         compiler_params=params(),
-    )(here, *own, *other, q)
+    )(here, w_out, w_value, q)
 
 
 def solve(sizes, features, here, own, other, xs, u, v, q):
@@ -577,7 +650,9 @@
         for at, turn in ((0, 1), (pairs, -1))
     ]
 
-    u, v, rows_xs, kept, given = gram(sizes, side, here, turned, other, adapters)
+    u, v, rows_xs, kept, given = gram(
+        sizes, here, *merge(sizes, side, here, turned, other), adapters
+    )
     theirs = lax.ppermute(given, "core", both_cores)
     summed = (kept.astype(jnp.float32) + theirs.astype(jnp.float32)).astype(jnp.bfloat16)
     shares = swap(summed.reshape(sections // 2, -1, summed.shape[-1]), ("b", "x"))

time: 225 us -> 221 us (0.982)
    pallas_call x1, Pallas kernels: 17.6 us -> 15.2 us  [solve(): pl.pallas_call(functools.partial(solve_kernel, sizes, features), out_shap...]
    pallas_call x1 -> x2, Pallas kernels: 5.07 us -> 5.08 us  [the longest x1 4.37 us: gram(): pl.pallas_call(functools.partial(gram_kernel, sizes), out_shape=(table, t...]
where the time goes in v6:
time: 221 us
  blocking collectives  84.1 us (38%)
  waiting for transfers between devices  60 us (27%)
  starting transfers between devices  43 us (19%)
  Pallas kernels  27.5 us (12%)
  local copies, waits for them, and re-layouts  3.52 us (2%)
    all_to_all x4, blocking collectives, swap(): return lax.all_to_all(value, axis, split_axis=0, concat_axis=0, tiled=True)  84.1 us
    all_to_all x4, starting transfers between devices, swap(): return lax.all_to_all(value, axis, split_axis=0, concat_axis=0, tiled=True)  25 us
    all_to_all x4, waiting for transfers between devices, swap(): return lax.all_to_all(value, axis, split_axis=0, concat_axis=0, tiled=True)  24 us
    pallas_call x1, Pallas kernels, solve(): pl.pallas_call(functools.partial(solve_kernel, sizes, features), out_shap...  15.2 us
    ppermute x2, waiting for transfers between devices, body(): lax.ppermute(jnp.concatenate(turned[at:at + pairs], axis=0), 'z', [(i, (i...  12.4 us
    ppermute x3, waiting for transfers between devices, body(): lax.ppermute(lines[step], ('a', 'b'), [(i, (i + step) % side) for i in ra...  11 us
    ppermute x3, waiting for transfers between devices, body(): lax.ppermute(turned[step], 'x', [(i, (i + step) % across) for i in range(...  5.67 us
    ppermute x3, starting transfers between devices, body(): lax.ppermute(lines[step], ('a', 'b'), [(i, (i + step) % side) for i in ra...  4.99 us
  transfers between devices with their start and end apart: 16, of which 12 were waited for; matrix products, arithmetic and copies ran while one was open for 0% of the time, Pallas kernels for 0%

profile of v6, /device:TPU:1, one launch (start us, length us, event | category | flops | bytes accessed | tf_op | source)
XLA Modules:
  0.0 220.6 jit_solution(16655447886843887430)
XLA Ops:
  1.2 2.9 %shard_map.147 = (bf16[16,16,1152]{2,1,0:T(8,128)(2,1)}, bf16[4,64,512]{2,1,0:T(8,128)(2,1)}, bf16[4,64,512]{2,1,0:T(8,128)(2,1)}, bf16[4,64,512]{2,1,0:T(8,128)(2,1)}, bf16[4,64,512]{2,1,0:T(8,128)(2,1)}) custom-call(s32[2]{0:T(128)} %pad_add_fusion.here_ref, bf16[64,8192]{1,0:T(8,128)(2,1)} %bitcast.32, bf16[64,8192]{1,0:T(8,128)(2,1)} %bitcast.33, ...), custom_call_target="tpu_custom_call" | custom-call | tf_op jit(solution)/shard_map/pallas_call | solution.py:453
  4.2 10.0 %all-to-all-start = ((bf16[16,16,1152]{2,1,0:T(8,128)(2,1)}), bf16[16,16,1152]{2,1,0:T(8,128)(2,1)S(1)}, u32[]{:S(2)}, u32[]{:S(2)}) async-start(bf16[16,16,1152]{2,1,0:T(8,128)(2,1)} %get-tuple-element.25), calls=%async_computation | async-start | bytes 1179648 | tf_op jit(solution)/shard_map/all_to_all | solution.py:570
  15.5 2.6 %collective-permute-start.1 = (bf16[4,64,512]{2,1,0:T(8,128)(2,1)}, bf16[4,64,512]{2,1,0:T(8,128)(2,1)S(1)}, u32[]{:S(2)}, u32[]{:S(2)}) collective-permute-start(bf16[4,64,512]{2,1,0:T(8,128)(2,1)} %get-tuple-element.28), channel_id=1, source_target_pairs={{0,128},{64,192},{128,0},{192,64},{1,129},{65,193},{129,1},{193,65... | collective-permute-start | bytes 786440 | tf_op jit(solution)/shard_map/ppermute | solution.py:622
  19.2 4.3 %collective-permute-done.refs_1_ = bf16[4,64,512]{2,1,0:T(8,128)(2,1)S(1)} collective-permute-done((bf16[4,64,512]{2,1,0:T(8,128)(2,1)}, bf16[4,64,512]{2,1,0:T(8,128)(2,1)S(1)}, u32[]{:S(2)}, u32[]{:S(2)}) %collective-permute-start) | collective-permute-done | bytes 262176 | tf_op jit(solution)/shard_map/ppermute | solution.py:622
  23.5 6.7 %collective-permute-done.1.refs_2_ = bf16[4,64,512]{2,1,0:T(8,128)(2,1)S(1)} collective-permute-done((bf16[4,64,512]{2,1,0:T(8,128)(2,1)}, bf16[4,64,512]{2,1,0:T(8,128)(2,1)S(1)}, u32[]{:S(2)}, u32[]{:S(2)}) %collective-permute-start.1) | collective-permute-done | bytes 262176 | tf_op jit(solution)/shard_map/ppermute | solution.py:622
  30.2 2.6 %all-to-all-done.parts_ref = bf16[16,16,1152]{2,1,0:T(8,128)(2,1)S(1)} async-done(((bf16[16,16,1152]{2,1,0:T(8,128)(2,1)}), bf16[16,16,1152]{2,1,0:T(8,128)(2,1)S(1)}, u32[]{:S(2)}, u32[]{:S(2)}) %all-to-all-start) | async-done | bytes 589856 | tf_op jit(solution)/shard_map/all_to_all | solution.py:570
  35.7 3.8 %all-to-all-start.1 = ((bf16[16,16,1152]{2,1,0:T(8,128)(2,1)}), bf16[16,16,1152]{2,1,0:T(8,128)(2,1)S(1)}, u32[]{:S(2)}, u32[]{:S(2)}) async-start(bf16[16,16,1152]{2,1,0:T(8,128)(2,1)} %get-tuple-element.36), calls=%async_computation.1 | async-start | bytes 1179648 | tf_op jit(solution)/shard_map/all_to_all | solution.py:570
  40.6 2.5 %collective-permute-start.4 = (bf16[4,64,512]{2,1,0:T(8,128)(2,1)S(1)}, bf16[4,64,512]{2,1,0:T(8,128)(2,1)S(1)}, u32[]{:S(2)}, u32[]{:S(2)}) collective-permute-start(bf16[4,64,512]{2,1,0:T(8,128)(2,1)S(1)} %get-tuple-element.32), channel_id=1, source_target_pairs={{0,32},{16,48},{32,0},{48,16},{1,33},{17,49},{33,1},{49,17},{2,34}... | collective-permute-start | bytes 786440 | tf_op jit(solution)/shard_map/ppermute | solution.py:627
  44.2 2.3 %collective-permute-start.8 = (bf16[8,8192]{1,0:T(8,128)(2,1)S(1)}, bf16[8,8192]{1,0:T(8,128)(2,1)S(1)}, u32[]{:S(2)}, u32[]{:S(2)}) collective-permute-start(bf16[8,8192]{1,0:T(8,128)(2,1)S(1)} %bitcast.23), channel_id=1, source_target_pairs={{0,1},{1,0},{2,3},{3,2},{4,5},{5,4},{6,7},{7,6},{8,9},{9,8},{10,11... | collective-permute-start | bytes 393224 | tf_op jit(solution)/shard_map/ppermute | solution.py:637
  47.9 5.7 %collective-permute-done.4.refs_2_.refs_1_ = bf16[4,64,512]{2,1,0:T(8,128)(2,1)S(1)} collective-permute-done((bf16[4,64,512]{2,1,0:T(8,128)(2,1)S(1)}, bf16[4,64,512]{2,1,0:T(8,128)(2,1)S(1)}, u32[]{:S(2)}, u32[]{:S(2)}) %collective-permute-start.4) | collective-permute-done | bytes 262176 | tf_op jit(solution)/shard_map/ppermute | solution.py:627
  53.6 4.0 %all-to-all-done.1.parts_ref = bf16[16,16,1152]{2,1,0:T(8,128)(2,1)S(1)} async-done(((bf16[16,16,1152]{2,1,0:T(8,128)(2,1)}), bf16[16,16,1152]{2,1,0:T(8,128)(2,1)S(1)}, u32[]{:S(2)}, u32[]{:S(2)}) %all-to-all-start.1) | async-done | bytes 589856 | tf_op jit(solution)/shard_map/all_to_all | solution.py:570
  59.1 7.7 %all-to-all-start.2 = ((bf16[16,16,1664]{2,1,0:T(8,128)(2,1)}), bf16[16,16,1664]{2,1,0:T(8,128)(2,1)S(1)}, u32[]{:S(2)}, u32[]{:S(2)}) async-start(bf16[16,16,1664]{2,1,0:T(8,128)(2,1)} %shard_map.150), calls=%async_computation.2 | async-start | bytes 1703936 | tf_op jit(solution)/shard_map/all_to_all | solution.py:570
  68.6 11.1 %collective-permute-done.7.refs_5_ = bf16[8,64,512]{2,1,0:T(8,128)(2,1)S(1)} collective-permute-done((bf16[8,64,512]{2,1,0:T(8,128)(2,1)S(1)}, bf16[8,64,512]{2,1,0:T(8,128)(2,1)S(1)}, u32[]{:S(2)}, u32[]{:S(2)}) %collective-permute-start.7) | collective-permute-done | bytes 524320 | tf_op jit(solution)/shard_map/ppermute | solution.py:645
  83.9 4.4 %shard_map.151 = (bf16[1024,512]{1,0:T(8,128)(2,1)S(1)}, bf16[1024,512]{1,0:T(8,128)(2,1)S(1)}, bf16[256,512]{1,0:T(8,128)(2,1)S(1)}, bf16[4,1344,128]{2,1,0:T(8,128)(2,1)S(1)}, bf16[4,1344,128]{2,1,0:T(8,128)(2,1)S(1)}) custom-call(s32[2]{0:T(128)S(1)} %copy-done.10, bf16[1024,512]{1,0:T(8,128)(2,1)S(1)} %get-tuple-element.34.wo_ref, ...), custom_call_target="tpu_custom_call" | custom-call | tf_op jit(solution)/shard_map/pallas_call | solution.py:527
  90.1 2.8 %collective-permute-done.10 = bf16[4,1344,128]{2,1,0:T(8,128)(2,1)S(1)} collective-permute-done((bf16[4,1344,128]{2,1,0:T(8,128)(2,1)S(1)}, bf16[4,1344,128]{2,1,0:T(8,128)(2,1)S(1)}, u32[]{:S(2)}, u32[]{:S(2)}) %collective-permute-start.10) | collective-permute-done | bytes 1376288 | tf_op jit(solution)/shard_map/ppermute | solution.py:656
  93.2 24.0 %all_to_all.40 = bf16[8,672,128]{2,1,0:T(8,128)(2,1)S(1)} all-to-all(bf16[8,672,128]{2,1,0:T(8,128)(2,1)S(1)} %bitcast.27), channel_id=1, replica_groups=mesh['a'=2,'b'=2,'x'=4,'z'=8,'core'=2] {'b','x'}, dimensions={0} | all-to-all | bytes 2752512 | tf_op jit(solution)/shard_map/all_to_all | solution.py:570
  117.7 20.4 %all_to_all.41 = bf16[8,672,128]{2,1,0:T(8,128)(2,1)S(1)} all-to-all(bf16[8,672,128]{2,1,0:T(8,128)(2,1)S(1)} %broadcast_in_dim.37), channel_id=1, replica_groups=mesh['a'=2,'b'=2,'x'=4,'z'=8,'core'=2] {'b','x'}, dimensions={0} | all-to-all | bytes 2752512 | tf_op jit(solution)/shard_map/all_to_all | solution.py:570
  138.1 2.4 %collective-permute-start.11 = (bf16[4,1344,128]{2,1,0:T(8,128)(2,1)S(1)}, bf16[4,1344,128]{2,1,0:T(8,128)(2,1)S(1)}, u32[]{:S(2)}, u32[]{:S(2)}) collective-permute-start(bf16[4,1344,128]{2,1,0:T(8,128)(2,1)S(1)} %bitcast.21), channel_id=1, source_target_pairs={{0,1},{1,0},{2,3},{3,2},{4,5},{5,4},{6,7},{7,6},{8,9},{9,8},{10,11... | collective-permute-start | bytes 4128776 | tf_op jit(solution)/shard_map/ppermute | solution.py:661
  140.5 2.8 %collective-permute-done.11.other_ref = bf16[4,1344,128]{2,1,0:T(8,128)(2,1)S(1)} collective-permute-done((bf16[4,1344,128]{2,1,0:T(8,128)(2,1)S(1)}, bf16[4,1344,128]{2,1,0:T(8,128)(2,1)S(1)}, u32[]{:S(2)}, u32[]{:S(2)}) %collective-permute-start.11) | collective-permute-done | bytes 1376288 | tf_op jit(solution)/shard_map/ppermute | solution.py:661
  143.2 15.2 %shard_map.152 = bf16[16,16,1152]{2,1,0:T(8,128)(2,1)S(1)} custom-call(s32[2]{0:T(128)S(1)} %copy-done.10, bf16[4,1344,128]{2,1,0:T(8,128)(2,1)S(1)} %bitcast.22, bf16[4,1344,128]{2,1,0:T(8,128)(2,1)S(1)} %collective-permute-done.11.other_ref, bf16[256,512]{1,0:T(8,128)(2,1)S(1)} %get-tuple-element.39.xs_ref, bf16[1024,512]{1,0:T(8,128)(2,1)S(1)} %copy-done.3, ...), custom_call_target="tpu_custom_call" | custom-call | tf_op jit(solution)/shard_map/pallas_call | solution.py:550
  158.5 16.0 %all_to_all.42 = bf16[16,16,1152]{2,1,0:T(8,128)(2,1)} all-to-all(bf16[16,16,1152]{2,1,0:T(8,128)(2,1)S(1)} %shard_map.152), channel_id=1, replica_groups=mesh['a'=2,'b'=2,'x'=4,'z'=8,'core'=2] {'b','x','a'}, dimensions={0} | all-to-all | bytes 1179648 | tf_op jit(solution)/shard_map/all_to_all | solution.py:570
  174.5 3.5 %all-to-all-start.6 = ((bf16[16,16,1152]{2,1,0:T(8,128)(2,1)}), bf16[16,16,1152]{2,1,0:T(8,128)(2,1)S(1)}, u32[]{:S(2)}, u32[]{:S(2)}) async-start(bf16[16,16,1152]{2,1,0:T(8,128)(2,1)} %all_to_all.42), calls=%async_computation.6 | async-start | bytes 1179648 | tf_op jit(solution)/shard_map/all_to_all | solution.py:570
  178.2 17.4 %all-to-all-done.6 = bf16[16,16,1152]{2,1,0:T(8,128)(2,1)S(1)} async-done(((bf16[16,16,1152]{2,1,0:T(8,128)(2,1)}), bf16[16,16,1152]{2,1,0:T(8,128)(2,1)S(1)}, u32[]{:S(2)}, u32[]{:S(2)}) %all-to-all-start.6) | async-done | bytes 589856 | tf_op jit(solution)/shard_map/all_to_all | solution.py:570
  196.1 23.6 %all_to_all.43.owned_ref = bf16[16,16,1152]{2,1,0:T(8,128)(2,1)S(1)} all-to-all(bf16[16,16,1152]{2,1,0:T(8,128)(2,1)S(1)} %bitcast.31), channel_id=1, replica_groups=mesh['a'=2,'b'=2,'x'=4,'z'=8,'core'=2] {'z','core'}, dimensions={0} | all-to-all | bytes 1179648 | tf_op jit(solution)/shard_map/all_to_all | solution.py:570
  (57 shorter events, 21.1 us)
Async XLA Ops:
  1.2 31.6 %copy-start.10 = (s32[2]{0:T(128)S(1)}, s32[2]{0:T(128)}, u32[]{:S(2)}) copy-start(s32[2]{0:T(128)} %pad_add_fusion.here_ref) | copy-start | bytes 28
  1.2 31.6 %copy-start.11 = (s32[16]{0:T(128)S(1)}, s32[16]{0:T(128)}, u32[]{:S(2)}) copy-start(s32[16]{0:T(128)} %tenant_ref.3) | copy-start | bytes 196
  1.2 31.6 %copy-start.12 = (s32[16]{0:T(128)S(1)}, s32[16]{0:T(128)}, u32[]{:S(2)}) copy-start(s32[16]{0:T(128)} %slot_ref.1) | copy-start | bytes 196
  4.2 28.6 %all-to-all-start = ((bf16[16,16,1152]{2,1,0:T(8,128)(2,1)}), bf16[16,16,1152]{2,1,0:T(8,128)(2,1)S(1)}, u32[]{:S(2)}, u32[]{:S(2)}) async-start(bf16[16,16,1152]{2,1,0:T(8,128)(2,1)} %get-tuple-element.25), calls=%async_computation | async-start | bytes 1179648 | tf_op jit(solution)/shard_map/all_to_all | solution.py:570
  14.2 9.3 %collective-permute-start = (bf16[4,64,512]{2,1,0:T(8,128)(2,1)}, bf16[4,64,512]{2,1,0:T(8,128)(2,1)S(1)}, u32[]{:S(2)}, u32[]{:S(2)}) collective-permute-start(bf16[4,64,512]{2,1,0:T(8,128)(2,1)} %get-tuple-element.27), channel_id=1, source_target_pairs={{0,64},{64,128},{128,192},{192,0},{1,65},{65,129},{129,193},{193,1... | collective-permute-start | bytes 786440 | tf_op jit(solution)/shard_map/ppermute | solution.py:622
  15.5 14.7 %collective-permute-start.1 = (bf16[4,64,512]{2,1,0:T(8,128)(2,1)}, bf16[4,64,512]{2,1,0:T(8,128)(2,1)S(1)}, u32[]{:S(2)}, u32[]{:S(2)}) collective-permute-start(bf16[4,64,512]{2,1,0:T(8,128)(2,1)} %get-tuple-element.28), channel_id=1, source_target_pairs={{0,128},{64,192},{128,0},{192,64},{1,129},{65,193},{129,1},{193,65... | collective-permute-start | bytes 786440 | tf_op jit(solution)/shard_map/ppermute | solution.py:622
  18.1 12.1 %collective-permute-start.2 = (bf16[4,64,512]{2,1,0:T(8,128)(2,1)}, bf16[4,64,512]{2,1,0:T(8,128)(2,1)S(1)}, u32[]{:S(2)}, u32[]{:S(2)}) collective-permute-start(bf16[4,64,512]{2,1,0:T(8,128)(2,1)} %get-tuple-element.29), channel_id=1, source_target_pairs={{0,192},{64,0},{128,64},{192,128},{1,193},{65,1},{129,65},{193,129... | collective-permute-start | bytes 786440 | tf_op jit(solution)/shard_map/ppermute | solution.py:622
  33.8 12.8 %copy-start.9 = (bf16[1,8,8192]{2,1,0:T(8,128)(2,1)S(1)}, bf16[1,8,8192]{2,1,0:T(8,128)(2,1)}, u32[]{:S(2)}) copy-start(bf16[1,8,8192]{2,1,0:T(8,128)(2,1)} %param.13) | copy-start | bytes 393220
  33.8 23.7 %copy-start.13 = (s32[16]{0:T(128)S(1)}, s32[16]{0:T(128)}, u32[]{:S(2)}) copy-start(s32[16]{0:T(128)} %valid_ref.1) | copy-start | bytes 196
  35.7 21.9 %all-to-all-start.1 = ((bf16[16,16,1152]{2,1,0:T(8,128)(2,1)}), bf16[16,16,1152]{2,1,0:T(8,128)(2,1)S(1)}, u32[]{:S(2)}, u32[]{:S(2)}) async-start(bf16[16,16,1152]{2,1,0:T(8,128)(2,1)} %get-tuple-element.36), calls=%async_computation.1 | async-start | bytes 1179648 | tf_op jit(solution)/shard_map/all_to_all | solution.py:570
  39.4 8.5 %collective-permute-start.3 = (bf16[4,64,512]{2,1,0:T(8,128)(2,1)S(1)}, bf16[4,64,512]{2,1,0:T(8,128)(2,1)S(1)}, u32[]{:S(2)}, u32[]{:S(2)}) collective-permute-start(bf16[4,64,512]{2,1,0:T(8,128)(2,1)S(1)} %get-tuple-element.31), channel_id=1, source_target_pairs={{0,16},{16,32},{32,48},{48,0},{1,17},{17,33},{33,49},{49,1},{2,18}... | collective-permute-start | bytes 786440 | tf_op jit(solution)/shard_map/ppermute | solution.py:627
  40.6 12.9 %collective-permute-start.4 = (bf16[4,64,512]{2,1,0:T(8,128)(2,1)S(1)}, bf16[4,64,512]{2,1,0:T(8,128)(2,1)S(1)}, u32[]{:S(2)}, u32[]{:S(2)}) collective-permute-start(bf16[4,64,512]{2,1,0:T(8,128)(2,1)S(1)} %get-tuple-element.32), channel_id=1, source_target_pairs={{0,32},{16,48},{32,0},{48,16},{1,33},{17,49},{33,1},{49,17},{2,34}... | collective-permute-start | bytes 786440 | tf_op jit(solution)/shard_map/ppermute | solution.py:627
  43.1 10.5 %collective-permute-start.5 = (bf16[4,64,512]{2,1,0:T(8,128)(2,1)S(1)}, bf16[4,64,512]{2,1,0:T(8,128)(2,1)S(1)}, u32[]{:S(2)}, u32[]{:S(2)}) collective-permute-start(bf16[4,64,512]{2,1,0:T(8,128)(2,1)S(1)} %get-tuple-element.33), channel_id=1, source_target_pairs={{0,48},{16,0},{32,16},{48,32},{1,49},{17,1},{33,17},{49,33},{2,50}... | collective-permute-start | bytes 786440 | tf_op jit(solution)/shard_map/ppermute | solution.py:627
  44.2 3.3 %collective-permute-start.8 = (bf16[8,8192]{1,0:T(8,128)(2,1)S(1)}, bf16[8,8192]{1,0:T(8,128)(2,1)S(1)}, u32[]{:S(2)}, u32[]{:S(2)}) collective-permute-start(bf16[8,8192]{1,0:T(8,128)(2,1)S(1)} %bitcast.23), channel_id=1, source_target_pairs={{0,1},{1,0},{2,3},{3,2},{4,5},{5,4},{6,7},{7,6},{8,9},{9,8},{10,11... | collective-permute-start | bytes 393224 | tf_op jit(solution)/shard_map/ppermute | solution.py:637
  46.6 1.3 collective-permute-start.9
  59.1 23.6 %all-to-all-start.2 = ((bf16[16,16,1664]{2,1,0:T(8,128)(2,1)}), bf16[16,16,1664]{2,1,0:T(8,128)(2,1)S(1)}, u32[]{:S(2)}, u32[]{:S(2)}) async-start(bf16[16,16,1664]{2,1,0:T(8,128)(2,1)} %shard_map.150), calls=%async_computation.2 | async-start | bytes 1703936 | tf_op jit(solution)/shard_map/all_to_all | solution.py:570
  66.9 12.8 %collective-permute-start.7 = (bf16[8,64,512]{2,1,0:T(8,128)(2,1)S(1)}, bf16[8,64,512]{2,1,0:T(8,128)(2,1)S(1)}, u32[]{:S(2)}, u32[]{:S(2)}) collective-permute-start(bf16[8,64,512]{2,1,0:T(8,128)(2,1)S(1)} %pad_maximum_fusion.1), channel_id=1, source_target_pairs={{0,14},{2,0},{4,2},{6,4},{8,6},{10,8},{12,10},{14,12},{1,15},{3,1}... | collective-permute-start | bytes 1572872 | tf_op jit(solution)/shard_map/ppermute | solution.py:645
  67.1 14.0 %collective-permute-start.6 = (bf16[8,64,512]{2,1,0:T(8,128)(2,1)S(1)}, bf16[8,64,512]{2,1,0:T(8,128)(2,1)S(1)}, u32[]{:S(2)}, u32[]{:S(2)}) collective-permute-start(bf16[8,64,512]{2,1,0:T(8,128)(2,1)S(1)} %pad_maximum_fusion), channel_id=1, source_target_pairs={{0,2},{2,4},{4,6},{6,8},{8,10},{10,12},{12,14},{14,0},{1,3},{3,5},... | collective-permute-start | bytes 1572872 | tf_op jit(solution)/shard_map/ppermute | solution.py:645
  88.3 4.5 %collective-permute-start.10 = (bf16[4,1344,128]{2,1,0:T(8,128)(2,1)S(1)}, bf16[4,1344,128]{2,1,0:T(8,128)(2,1)S(1)}, u32[]{:S(2)}, u32[]{:S(2)}) collective-permute-start(bf16[4,1344,128]{2,1,0:T(8,128)(2,1)S(1)} %get-tuple-element.38), channel_id=1, source_target_pairs={{0,1},{1,0},{2,3},{3,2},{4,5},{5,4},{6,7},{7,6},{8,9},{9,8},{10,11... | collective-permute-start | bytes 4128776 | tf_op jit(solution)/shard_map/ppermute | solution.py:656
  117.6 25.6 %copy-start.3 = (bf16[1024,512]{1,0:T(8,128)(2,1)S(1)}, bf16[1024,512]{1,0:T(8,128)(2,1)}, u32[]{:S(2)}) copy-start(bf16[1024,512]{1,0:T(8,128)(2,1)} %copy-done.2) | copy-start | bytes 3145732
  117.7 25.6 %copy-start.5 = (bf16[1024,512]{1,0:T(8,128)(2,1)S(1)}, bf16[1024,512]{1,0:T(8,128)(2,1)}, u32[]{:S(2)}) copy-start(bf16[1024,512]{1,0:T(8,128)(2,1)} %copy-done.4) | copy-start | bytes 3145732
  138.1 5.2 %collective-permute-start.11 = (bf16[4,1344,128]{2,1,0:T(8,128)(2,1)S(1)}, bf16[4,1344,128]{2,1,0:T(8,128)(2,1)S(1)}, u32[]{:S(2)}, u32[]{:S(2)}) collective-permute-start(bf16[4,1344,128]{2,1,0:T(8,128)(2,1)S(1)} %bitcast.21), channel_id=1, source_target_pairs={{0,1},{1,0},{2,3},{3,2},{4,5},{5,4},{6,7},{7,6},{8,9},{9,8},{10,11... | collective-permute-start | bytes 4128776 | tf_op jit(solution)/shard_map/ppermute | solution.py:661
  174.5 21.2 %all-to-all-start.6 = ((bf16[16,16,1152]{2,1,0:T(8,128)(2,1)}), bf16[16,16,1152]{2,1,0:T(8,128)(2,1)S(1)}, u32[]{:S(2)}, u32[]{:S(2)}) async-start(bf16[16,16,1152]{2,1,0:T(8,128)(2,1)} %all_to_all.42), calls=%async_computation.6 | async-start | bytes 1179648 | tf_op jit(solution)/shard_map/all_to_all | solution.py:570
  196.1 23.7 %copy-start.7 = (f32[1,8192]{1,0:T(1,128)S(1)}, f32[1,8192]{1,0:T(1,128)}, u32[]{:S(2)}) copy-start(f32[1,8192]{1,0:T(1,128)} %gain_ref.3) | copy-start | bytes 98308
  (6 other events, 23.4 us)

commit v7 on v6

--- a/solution.py
+++ b/solution.py
@@ -12,7 +12,7 @@
 block = 256
 vmem_bytes = 20 * 1024 * 1024
 whole_vmem_bytes = 56 * 1024 * 1024
-merge_cost_bytes = 4 * 1024 * 1024
+merge_cost_bytes = 40 * 1024 * 1024
 pipe = ("a", "b", "x")
 dp = ("z", "core")
 
@@ -154,7 +154,7 @@
 
 def merge_kernel(sizes, side, across, here_ref, *refs):
     layers, hd, rank, tokens, cols = sizes
-    own_refs, other_refs, (u_ref, v_ref) = refs[:across], refs[across:-2], refs[-2:]
+    own_refs, other_refs, both_ref = refs[:across], refs[across:-1], refs[-1]
     pairs = across // 2
     part = hd // 2
     plane = lax.rem(here_ref[1] // 2, 2)
@@ -165,22 +165,20 @@
         own, other = own_refs[dx][dy], other_refs[dx // pairs][dx % pairs * side + dy]
         mine = pl.ds(pl.multiple_of(l * hd + plane * part, part), part)
         theirs = pl.ds(pl.multiple_of(l * hd + (1 - plane) * part, part), part)
-        v_ref[mine, :] = own[:part]
-        u_ref[mine, :] = own[part:]
-        v_ref[theirs, :] = other[:part]
-        u_ref[theirs, :] = other[part:]
+        both_ref[0, mine, :] = own[:part]
+        both_ref[1, mine, :] = own[part:]
+        both_ref[0, theirs, :] = other[:part]
+        both_ref[1, theirs, :] = other[part:]
 
 
 def gram_kernel(
     sizes,
     here_ref,
-    wo_ref,
-    wv_ref,
+    both_ref,
     q_ref,
     u_ref,
     v_ref,
     xs_ref,
-    keep_ref,
     give_ref,
     x_wide,
     s_wide,
@@ -190,8 +188,8 @@
     rows = tokens // layers
     core = lax.rem(here_ref[1], 2)
     copies = [
-        pltpu.make_async_copy(wo_ref, u_ref, sems.at[0]),
-        pltpu.make_async_copy(wv_ref, v_ref, sems.at[1]),
+        pltpu.make_async_copy(both_ref.at[0], v_ref, sems.at[0]),
+        pltpu.make_async_copy(both_ref.at[1], u_ref, sems.at[1]),
     ]
     for copy in copies:
         copy.start()
@@ -216,50 +214,63 @@
         )
     xs_ref[:tokens, :] = x_wide[...].astype(jnp.bfloat16)
     xs_ref[tokens:, :] = s_wide[...].astype(jnp.bfloat16)
+    for own_core in range(2):
+        pl.when(core == own_core)(
+            functools.partial(
+                half_products, sizes, 1 - own_core, u_ref, v_ref, xs_ref, give_ref
+            )
+        )
+
+
+def keep_kernel(sizes, here_ref, u_ref, v_ref, xs_ref, keep_ref):
+    core = lax.rem(here_ref[1], 2)
+    for own_core in range(2):
+        pl.when(core == own_core)(
+            functools.partial(half_products, sizes, own_core, u_ref, v_ref, xs_ref, keep_ref)
+        )
+
+
+def half_products(sizes, which, u_ref, v_ref, xs_ref, out_ref):
+    layers, hd, rank, tokens, cols = sizes
     width = layers * hd
     base = 3 * tokens
     below = layer_mask(block, block, hd, lambda r, c: r < c)
     lane = 2 * hd
-    half_count = width // lane // 2
-
-    def put(own_core, start, column, value):
+    count = width // block // 2
+
+    def put(start, column, value):
         value = value.astype(jnp.bfloat16)
         for at in range(0, value.shape[1], lane):
-            index = (column + at) // lane
-            out_ref = keep_ref if index // half_count == own_core else give_ref
-            out_ref[index % half_count, pl.ds(start, value.shape[0]), :] = value[:, at : at + lane]
-
-    def products(own_core):
-        for bj in range(width // block):
-            column = bj * block
-            at_col = pl.ds(column, block)
-            u_col, v_col = u_ref[at_col, :], v_ref[at_col, :]
-            x_rows, s_rows = xs_ref[:tokens, :], xs_ref[tokens:, :]
-            put(own_core, 0, column, mm_nt(x_rows, v_col))
-            x_u = mm_nt(x_rows, u_col)
-            if column + block == width:
-                wide = x_wide[...]
-                wide = wide * wide
-                folded = wide[:, :lane]
-                for at in range(lane, cols, lane):
-                    folded = folded + wide[:, at : at + lane]
-                x_u = jnp.concatenate([x_u[:, : block - hd], folded[:, :hd] + folded[:, hd:]], axis=1)
-            put(own_core, tokens, column, x_u)
-            put(own_core, 2 * tokens, column, mm_nt(s_rows, u_col))
-            for bi in range(width // block):
-                height = min(block, width - hd - bi * block)
-                rows_at = pl.ds(bi * block, height)
-                rows_u = u_ref[rows_at, :]
-                if bi < bj:
-                    part = mm_nt(rows_u, v_col)
-                elif bi > bj:
-                    part = mm_nt(rows_u, u_col)
-                else:
-                    part = jnp.where(below[:height], mm_nt(rows_u, v_col), mm_nt(rows_u, u_col))
-                put(own_core, base + bi * block, column, part)
-
-    for own_core in range(2):
-        pl.when(core == own_core)(functools.partial(products, own_core))
+            index = (column - which * count * block + at) // lane
+            out_ref[index, pl.ds(start, value.shape[0]), :] = value[:, at : at + lane]
+
+    x_rows, s_rows = xs_ref[:tokens, :], xs_ref[tokens:, :]
+    for bj in range(which * count, which * count + count):
+        column = bj * block
+        at_col = pl.ds(column, block)
+        u_col, v_col = u_ref[at_col, :], v_ref[at_col, :]
+        put(0, column, mm_nt(x_rows, v_col))
+        x_u = mm_nt(x_rows, u_col)
+        if column + block == width:
+            wide = x_rows.astype(jnp.float32)
+            wide = wide * wide
+            folded = wide[:, :lane]
+            for at in range(lane, cols, lane):
+                folded = folded + wide[:, at : at + lane]
+            x_u = jnp.concatenate([x_u[:, : block - hd], folded[:, :hd] + folded[:, hd:]], axis=1)
+        put(tokens, column, x_u)
+        put(2 * tokens, column, mm_nt(s_rows, u_col))
+        for bi in range(width // block):
+            height = min(block, width - hd - bi * block)
+            rows_at = pl.ds(bi * block, height)
+            rows_u = u_ref[rows_at, :]
+            if bi < bj:
+                part = mm_nt(rows_u, v_col)
+            elif bi > bj:
+                part = mm_nt(rows_u, u_col)
+            else:
+                part = jnp.where(below[:height], mm_nt(rows_u, v_col), mm_nt(rows_u, u_col))
+            put(base + bi * block, column, part)
 
 
 def half(pair, l):
@@ -504,12 +515,11 @@
 
 def merge(sizes, side, here, own, other):
     layers, hd, rank, tokens, cols = sizes
-    table = jax.ShapeDtypeStruct((layers * hd, cols), jnp.bfloat16)
     return pl.pallas_call(
         functools.partial(merge_kernel, sizes, side, len(own)),
-        out_shape=(table, table),
+        out_shape=jax.ShapeDtypeStruct((2, layers * hd, cols), jnp.bfloat16),
         in_specs=in_smem(1) + in_vmem(len(own) + len(other)),
-        out_specs=tuple(in_vmem(2)),
+        out_specs=in_vmem(1)[0],
         compiler_params=params(),
         cost_estimate=pl.CostEstimate(
             flops=0, bytes_accessed=merge_cost_bytes, transcendentals=0
@@ -517,7 +527,7 @@
     )(here, *own, *other)
 
 
-def gram(sizes, here, w_out, w_value, q):
+def gram(sizes, here, both, q):
     layers, hd, rank, tokens, cols = sizes
     width = layers * hd
     share = jax.ShapeDtypeStruct(
@@ -531,17 +541,27 @@
             table,
             jax.ShapeDtypeStruct((2 * tokens, cols), jnp.bfloat16),
             share,
-            share,
         ),
-        in_specs=in_smem(1) + [pl.BlockSpec(memory_space=pl.ANY)] * 2 + in_vmem(1),
-        out_specs=tuple(in_vmem(5)),
+        in_specs=in_smem(1) + [pl.BlockSpec(memory_space=pl.ANY)] + in_vmem(1),
+        out_specs=tuple(in_vmem(4)),
         scratch_shapes=[
             pltpu.VMEM((tokens, cols), jnp.float32),
             pltpu.VMEM((tokens, cols), jnp.float32),
             pltpu.SemaphoreType.DMA((2,)),
         ],
         compiler_params=params(),
-    )(here, w_out, w_value, q)
+    )(here, both, q)
+
+
+def keep(sizes, here, u, v, xs, shape):
+    return pl.pallas_call(
+        functools.partial(keep_kernel, sizes),
+        out_shape=jax.ShapeDtypeStruct(shape, jnp.bfloat16),
+        in_specs=in_smem(1) + in_vmem(3),
+        out_specs=in_vmem(1)[0],
+        compiler_params=params(),
+        cost_estimate=pl.CostEstimate(flops=1 << 31, bytes_accessed=1 << 22, transcendentals=0),
+    )(here, u, v, xs)
 
 
 def solve(sizes, features, here, own, other, xs, u, v, q):
@@ -650,10 +670,11 @@
         for at, turn in ((0, 1), (pairs, -1))
     ]
 
-    u, v, rows_xs, kept, given = gram(
-        sizes, here, *merge(sizes, side, here, turned, other), adapters
+    u, v, rows_xs, given = gram(
+        sizes, here, merge(sizes, side, here, turned, other), adapters
     )
     theirs = lax.ppermute(given, "core", both_cores)
+    kept = keep(sizes, here, u, v, rows_xs, given.shape)
     summed = (kept.astype(jnp.float32) + theirs.astype(jnp.float32)).astype(jnp.bfloat16)
     shares = swap(summed.reshape(sections // 2, -1, summed.shape[-1]), ("b", "x"))
     share = jnp.sum(shares.astype(jnp.float32), axis=0).astype(jnp.bfloat16)

time: 221 us -> 220 us (level)
  waiting for transfers between devices: 60 us -> 56 us
  transfers between devices with their start and end apart: 16 -> 16, of which waited for: 12 -> 11; matrix products, arithmetic and copies ran while one was open for 0% -> 0% of each run, Pallas kernels for 0% -> 1%
where the time goes in v7:
time: 220 us; the launch traced here: 219 us
  blocking collectives  84.6 us (38%)
  waiting for transfers between devices  56 us (25%)
  starting transfers between devices  44.7 us (20%)
  Pallas kernels  28.3 us (13%)
  local copies, waits for them, and re-layouts  3.24 us (1%)
    all_to_all x4, blocking collectives, swap(): return lax.all_to_all(value, axis, split_axis=0, concat_axis=0, tiled=True)  84.6 us
    all_to_all x4, starting transfers between devices, swap(): return lax.all_to_all(value, axis, split_axis=0, concat_axis=0, tiled=True)  25.5 us
    all_to_all x4, waiting for transfers between devices, swap(): return lax.all_to_all(value, axis, split_axis=0, concat_axis=0, tiled=True)  23.6 us
    pallas_call x1, Pallas kernels, solve(): pl.pallas_call(functools.partial(solve_kernel, sizes, features), out_shap...  15.2 us
    ppermute x2, waiting for transfers between devices, body(): lax.ppermute(jnp.concatenate(turned[at:at + pairs], axis=0), 'z', [(i, (i...  11.1 us
    ppermute x3, waiting for transfers between devices, body(): lax.ppermute(lines[step], ('a', 'b'), [(i, (i + step) % side) for i in ra...  11 us
    ppermute x3, waiting for transfers between devices, body(): lax.ppermute(turned[step], 'x', [(i, (i + step) % across) for i in range(...  5.67 us
    ppermute x3, starting transfers between devices, body(): lax.ppermute(lines[step], ('a', 'b'), [(i, (i + step) % side) for i in ra...  4.99 us
  transfers between devices with their start and end apart: 16, of which 11 were waited for; matrix products, arithmetic and copies ran while one was open for 0% of the time, Pallas kernels for 1%

profile of v7, /device:TPU:1, one launch (start us, length us, event | category | flops | bytes accessed | tf_op | source)
XLA Modules:
  0.0 219.5 jit_solution(18047204147515769644)
XLA Ops:
  1.3 2.9 %shard_map.147 = (bf16[16,16,1152]{2,1,0:T(8,128)(2,1)}, bf16[4,64,512]{2,1,0:T(8,128)(2,1)}, bf16[4,64,512]{2,1,0:T(8,128)(2,1)}, bf16[4,64,512]{2,1,0:T(8,128)(2,1)}, bf16[4,64,512]{2,1,0:T(8,128)(2,1)}) custom-call(s32[2]{0:T(128)} %pad_add_fusion.here_ref, bf16[64,8192]{1,0:T(8,128)(2,1)} %bitcast.32, bf16[64,8192]{1,0:T(8,128)(2,1)} %bitcast.33, ...), custom_call_target="tpu_custom_call" | custom-call | tf_op jit(solution)/shard_map/pallas_call | solution.py:464
  4.2 10.0 %all-to-all-start = ((bf16[16,16,1152]{2,1,0:T(8,128)(2,1)}), bf16[16,16,1152]{2,1,0:T(8,128)(2,1)S(1)}, u32[]{:S(2)}, u32[]{:S(2)}) async-start(bf16[16,16,1152]{2,1,0:T(8,128)(2,1)} %get-tuple-element.22), calls=%async_computation | async-start | bytes 1179648 | tf_op jit(solution)/shard_map/all_to_all | solution.py:590
  15.5 2.6 %collective-permute-start.1 = (bf16[4,64,512]{2,1,0:T(8,128)(2,1)}, bf16[4,64,512]{2,1,0:T(8,128)(2,1)S(1)}, u32[]{:S(2)}, u32[]{:S(2)}) collective-permute-start(bf16[4,64,512]{2,1,0:T(8,128)(2,1)} %get-tuple-element.25), channel_id=1, source_target_pairs={{0,128},{64,192},{128,0},{192,64},{1,129},{65,193},{129,1},{193,65... | collective-permute-start | bytes 786440 | tf_op jit(solution)/shard_map/ppermute | solution.py:642
  19.2 4.3 %collective-permute-done.refs_1_ = bf16[4,64,512]{2,1,0:T(8,128)(2,1)S(1)} collective-permute-done((bf16[4,64,512]{2,1,0:T(8,128)(2,1)}, bf16[4,64,512]{2,1,0:T(8,128)(2,1)S(1)}, u32[]{:S(2)}, u32[]{:S(2)}) %collective-permute-start) | collective-permute-done | bytes 262176 | tf_op jit(solution)/shard_map/ppermute | solution.py:642
  23.5 6.7 %collective-permute-done.1.refs_2_ = bf16[4,64,512]{2,1,0:T(8,128)(2,1)S(1)} collective-permute-done((bf16[4,64,512]{2,1,0:T(8,128)(2,1)}, bf16[4,64,512]{2,1,0:T(8,128)(2,1)S(1)}, u32[]{:S(2)}, u32[]{:S(2)}) %collective-permute-start.1) | collective-permute-done | bytes 262176 | tf_op jit(solution)/shard_map/ppermute | solution.py:642
  30.2 2.6 %all-to-all-done.parts_ref = bf16[16,16,1152]{2,1,0:T(8,128)(2,1)S(1)} async-done(((bf16[16,16,1152]{2,1,0:T(8,128)(2,1)}), bf16[16,16,1152]{2,1,0:T(8,128)(2,1)S(1)}, u32[]{:S(2)}, u32[]{:S(2)}) %all-to-all-start) | async-done | bytes 589856 | tf_op jit(solution)/shard_map/all_to_all | solution.py:590
  35.7 3.8 %all-to-all-start.1 = ((bf16[16,16,1152]{2,1,0:T(8,128)(2,1)}), bf16[16,16,1152]{2,1,0:T(8,128)(2,1)S(1)}, u32[]{:S(2)}, u32[]{:S(2)}) async-start(bf16[16,16,1152]{2,1,0:T(8,128)(2,1)} %get-tuple-element.31), calls=%async_computation.1 | async-start | bytes 1179648 | tf_op jit(solution)/shard_map/all_to_all | solution.py:590
  40.7 2.5 %collective-permute-start.4 = (bf16[4,64,512]{2,1,0:T(8,128)(2,1)S(1)}, bf16[4,64,512]{2,1,0:T(8,128)(2,1)S(1)}, u32[]{:S(2)}, u32[]{:S(2)}) collective-permute-start(bf16[4,64,512]{2,1,0:T(8,128)(2,1)S(1)} %get-tuple-element.29), channel_id=1, source_target_pairs={{0,32},{16,48},{32,0},{48,16},{1,33},{17,49},{33,1},{49,17},{2,34}... | collective-permute-start | bytes 786440 | tf_op jit(solution)/shard_map/ppermute | solution.py:647
  44.3 2.3 %collective-permute-start.8 = (bf16[8,8192]{1,0:T(8,128)(2,1)S(1)}, bf16[8,8192]{1,0:T(8,128)(2,1)S(1)}, u32[]{:S(2)}, u32[]{:S(2)}) collective-permute-start(bf16[8,8192]{1,0:T(8,128)(2,1)S(1)} %bitcast.23), channel_id=1, source_target_pairs={{0,1},{1,0},{2,3},{3,2},{4,5},{5,4},{6,7},{7,6},{8,9},{9,8},{10,11... | collective-permute-start | bytes 393224 | tf_op jit(solution)/shard_map/ppermute | solution.py:657
  48.0 5.7 %collective-permute-done.4.refs_2_.refs_1_ = bf16[4,64,512]{2,1,0:T(8,128)(2,1)S(1)} collective-permute-done((bf16[4,64,512]{2,1,0:T(8,128)(2,1)S(1)}, bf16[4,64,512]{2,1,0:T(8,128)(2,1)S(1)}, u32[]{:S(2)}, u32[]{:S(2)}) %collective-permute-start.4) | collective-permute-done | bytes 262176 | tf_op jit(solution)/shard_map/ppermute | solution.py:647
  53.6 4.0 %all-to-all-done.1.parts_ref = bf16[16,16,1152]{2,1,0:T(8,128)(2,1)S(1)} async-done(((bf16[16,16,1152]{2,1,0:T(8,128)(2,1)}), bf16[16,16,1152]{2,1,0:T(8,128)(2,1)S(1)}, u32[]{:S(2)}, u32[]{:S(2)}) %all-to-all-start.1) | async-done | bytes 589856 | tf_op jit(solution)/shard_map/all_to_all | solution.py:590
  59.2 7.7 %all-to-all-start.2 = ((bf16[16,16,1664]{2,1,0:T(8,128)(2,1)}), bf16[16,16,1664]{2,1,0:T(8,128)(2,1)S(1)}, u32[]{:S(2)}, u32[]{:S(2)}) async-start(bf16[16,16,1664]{2,1,0:T(8,128)(2,1)} %shard_map.150), calls=%async_computation.2 | async-start | bytes 1703936 | tf_op jit(solution)/shard_map/all_to_all | solution.py:590
  67.1 2.7 %collective-permute-start.7 = (bf16[8,64,512]{2,1,0:T(8,128)(2,1)S(1)}, bf16[8,64,512]{2,1,0:T(8,128)(2,1)S(1)}, u32[]{:S(2)}, u32[]{:S(2)}) collective-permute-start(bf16[8,64,512]{2,1,0:T(8,128)(2,1)S(1)} %pad_maximum_fusion.1), channel_id=1, source_target_pairs={{0,14},{2,0},{4,2},{6,4},{8,6},{10,8},{12,10},{14,12},{1,15},{3,1}... | collective-permute-start | bytes 1572872 | tf_op jit(solution)/shard_map/ppermute | solution.py:665
  69.8 11.1 %collective-permute-done.6.refs_4_ = bf16[8,64,512]{2,1,0:T(8,128)(2,1)S(1)} collective-permute-done((bf16[8,64,512]{2,1,0:T(8,128)(2,1)S(1)}, bf16[8,64,512]{2,1,0:T(8,128)(2,1)S(1)}, u32[]{:S(2)}, u32[]{:S(2)}) %collective-permute-start.6) | collective-permute-done | bytes 524320 | tf_op jit(solution)/shard_map/ppermute | solution.py:665
  83.6 3.0 %shard_map.151 = (bf16[1024,512]{1,0:T(8,128)(2,1)S(1)}, bf16[1024,512]{1,0:T(8,128)(2,1)S(1)}, bf16[256,512]{1,0:T(8,128)(2,1)S(1)}, bf16[4,1344,128]{2,1,0:T(8,128)(2,1)S(1)}) custom-call(s32[2]{0:T(128)S(1)} %copy-done.12, bf16[2,1024,512]{2,1,0:T(8,128)(2,1)S(1)} %shard_map.149.both_ref, bf16[16,16,1664]{2,1,0:T(8,128)(2,1)S(1)} %all-to-all-done.2.q_ref), custom_call_target="tpu_custom_call" | custom-call | tf_op jit(solution)/shard_map/pallas_call | solution.py:537
  91.4 24.0 %all_to_all.40 = bf16[8,672,128]{2,1,0:T(8,128)(2,1)S(1)} all-to-all(bf16[8,672,128]{2,1,0:T(8,128)(2,1)S(1)} %bitcast.27), channel_id=1, replica_groups=mesh['a'=2,'b'=2,'x'=4,'z'=8,'core'=2] {'b','x'}, dimensions={0} | all-to-all | bytes 2752512 | tf_op jit(solution)/shard_map/all_to_all | solution.py:590
  115.9 20.4 %all_to_all.41 = bf16[8,672,128]{2,1,0:T(8,128)(2,1)S(1)} all-to-all(bf16[8,672,128]{2,1,0:T(8,128)(2,1)S(1)} %broadcast_in_dim.37), channel_id=1, replica_groups=mesh['a'=2,'b'=2,'x'=4,'z'=8,'core'=2] {'b','x'}, dimensions={0} | all-to-all | bytes 2752512 | tf_op jit(solution)/shard_map/all_to_all | solution.py:590
  136.3 2.4 %collective-permute-start.11 = (bf16[4,1344,128]{2,1,0:T(8,128)(2,1)S(1)}, bf16[4,1344,128]{2,1,0:T(8,128)(2,1)S(1)}, u32[]{:S(2)}, u32[]{:S(2)}) collective-permute-start(bf16[4,1344,128]{2,1,0:T(8,128)(2,1)S(1)} %bitcast.21), channel_id=1, source_target_pairs={{0,1},{1,0},{2,3},{3,2},{4,5},{5,4},{6,7},{7,6},{8,9},{9,8},{10,11... | collective-permute-start | bytes 4128776 | tf_op jit(solution)/shard_map/ppermute | solution.py:682
  138.7 2.8 %collective-permute-done.11.other_ref = bf16[4,1344,128]{2,1,0:T(8,128)(2,1)S(1)} collective-permute-done((bf16[4,1344,128]{2,1,0:T(8,128)(2,1)S(1)}, bf16[4,1344,128]{2,1,0:T(8,128)(2,1)S(1)}, u32[]{:S(2)}, u32[]{:S(2)}) %collective-permute-start.11) | collective-permute-done | bytes 1376288 | tf_op jit(solution)/shard_map/ppermute | solution.py:682
  141.5 15.2 %shard_map.153 = bf16[16,16,1152]{2,1,0:T(8,128)(2,1)S(1)} custom-call(s32[2]{0:T(128)S(1)} %copy-done.12, bf16[4,1344,128]{2,1,0:T(8,128)(2,1)S(1)} %bitcast.22, bf16[4,1344,128]{2,1,0:T(8,128)(2,1)S(1)} %collective-permute-done.11.other_ref, bf16[256,512]{1,0:T(8,128)(2,1)S(1)} %get-tuple-element.34.xs_ref, bf16[1024,512]{1,0:T(8,128)(2,1)S(1)} %copy-done.5, ...), custom_call_target="tpu_custom_call" | custom-call | tf_op jit(solution)/shard_map/pallas_call | solution.py:570
  156.7 16.0 %all_to_all.42 = bf16[16,16,1152]{2,1,0:T(8,128)(2,1)} all-to-all(bf16[16,16,1152]{2,1,0:T(8,128)(2,1)S(1)} %shard_map.153), channel_id=1, replica_groups=mesh['a'=2,'b'=2,'x'=4,'z'=8,'core'=2] {'b','x','a'}, dimensions={0} | all-to-all | bytes 1179648 | tf_op jit(solution)/shard_map/all_to_all | solution.py:590
  172.7 4.1 %all-to-all-start.6 = ((bf16[16,16,1152]{2,1,0:T(8,128)(2,1)}), bf16[16,16,1152]{2,1,0:T(8,128)(2,1)S(1)}, u32[]{:S(2)}, u32[]{:S(2)}) async-start(bf16[16,16,1152]{2,1,0:T(8,128)(2,1)} %all_to_all.42), calls=%async_computation.6 | async-start | bytes 1179648 | tf_op jit(solution)/shard_map/all_to_all | solution.py:590
  177.0 17.0 %all-to-all-done.6 = bf16[16,16,1152]{2,1,0:T(8,128)(2,1)S(1)} async-done(((bf16[16,16,1152]{2,1,0:T(8,128)(2,1)}), bf16[16,16,1152]{2,1,0:T(8,128)(2,1)S(1)}, u32[]{:S(2)}, u32[]{:S(2)}) %all-to-all-start.6) | async-done | bytes 589856 | tf_op jit(solution)/shard_map/all_to_all | solution.py:590
  194.5 24.2 %all_to_all.43.owned_ref = bf16[16,16,1152]{2,1,0:T(8,128)(2,1)S(1)} all-to-all(bf16[16,16,1152]{2,1,0:T(8,128)(2,1)S(1)} %bitcast.31), channel_id=1, replica_groups=mesh['a'=2,'b'=2,'x'=4,'z'=8,'core'=2] {'z','core'}, dimensions={0} | all-to-all | bytes 1179648 | tf_op jit(solution)/shard_map/all_to_all | solution.py:590
  (62 shorter events, 20.7 us)
Async XLA Ops:
  1.3 31.6 %copy-start.12 = (s32[2]{0:T(128)S(1)}, s32[2]{0:T(128)}, u32[]{:S(2)}) copy-start(s32[2]{0:T(128)} %pad_add_fusion.here_ref) | copy-start | bytes 28
  1.3 31.6 %copy-start.13 = (s32[16]{0:T(128)S(1)}, s32[16]{0:T(128)}, u32[]{:S(2)}) copy-start(s32[16]{0:T(128)} %tenant_ref.3) | copy-start | bytes 196
  1.3 31.6 %copy-start.14 = (s32[16]{0:T(128)S(1)}, s32[16]{0:T(128)}, u32[]{:S(2)}) copy-start(s32[16]{0:T(128)} %slot_ref.1) | copy-start | bytes 196
  4.2 28.6 %all-to-all-start = ((bf16[16,16,1152]{2,1,0:T(8,128)(2,1)}), bf16[16,16,1152]{2,1,0:T(8,128)(2,1)S(1)}, u32[]{:S(2)}, u32[]{:S(2)}) async-start(bf16[16,16,1152]{2,1,0:T(8,128)(2,1)} %get-tuple-element.22), calls=%async_computation | async-start | bytes 1179648 | tf_op jit(solution)/shard_map/all_to_all | solution.py:590
  14.2 9.3 %collective-permute-start = (bf16[4,64,512]{2,1,0:T(8,128)(2,1)}, bf16[4,64,512]{2,1,0:T(8,128)(2,1)S(1)}, u32[]{:S(2)}, u32[]{:S(2)}) collective-permute-start(bf16[4,64,512]{2,1,0:T(8,128)(2,1)} %get-tuple-element.24), channel_id=1, source_target_pairs={{0,64},{64,128},{128,192},{192,0},{1,65},{65,129},{129,193},{193,1... | collective-permute-start | bytes 786440 | tf_op jit(solution)/shard_map/ppermute | solution.py:642
  15.5 14.7 %collective-permute-start.1 = (bf16[4,64,512]{2,1,0:T(8,128)(2,1)}, bf16[4,64,512]{2,1,0:T(8,128)(2,1)S(1)}, u32[]{:S(2)}, u32[]{:S(2)}) collective-permute-start(bf16[4,64,512]{2,1,0:T(8,128)(2,1)} %get-tuple-element.25), channel_id=1, source_target_pairs={{0,128},{64,192},{128,0},{192,64},{1,129},{65,193},{129,1},{193,65... | collective-permute-start | bytes 786440 | tf_op jit(solution)/shard_map/ppermute | solution.py:642
  18.1 12.1 %collective-permute-start.2 = (bf16[4,64,512]{2,1,0:T(8,128)(2,1)}, bf16[4,64,512]{2,1,0:T(8,128)(2,1)S(1)}, u32[]{:S(2)}, u32[]{:S(2)}) collective-permute-start(bf16[4,64,512]{2,1,0:T(8,128)(2,1)} %get-tuple-element.26), channel_id=1, source_target_pairs={{0,192},{64,0},{128,64},{192,128},{1,193},{65,1},{129,65},{193,129... | collective-permute-start | bytes 786440 | tf_op jit(solution)/shard_map/ppermute | solution.py:642
  33.8 23.8 %copy-start.15 = (s32[16]{0:T(128)S(1)}, s32[16]{0:T(128)}, u32[]{:S(2)}) copy-start(s32[16]{0:T(128)} %valid_ref.1) | copy-start | bytes 196
  35.7 31.2 %copy-start.2 = (bf16[4,64,512]{2,1,0:T(8,128)(2,1)}, bf16[4,64,512]{2,1,0:T(8,128)(2,1)S(1)}, u32[]{:S(2)}) copy-start(bf16[4,64,512]{2,1,0:T(8,128)(2,1)S(1)} %get-tuple-element.27.refs_0_) | copy-start | bytes 786436
  35.7 21.9 %all-to-all-start.1 = ((bf16[16,16,1152]{2,1,0:T(8,128)(2,1)}), bf16[16,16,1152]{2,1,0:T(8,128)(2,1)S(1)}, u32[]{:S(2)}, u32[]{:S(2)}) async-start(bf16[16,16,1152]{2,1,0:T(8,128)(2,1)} %get-tuple-element.31), calls=%async_computation.1 | async-start | bytes 1179648 | tf_op jit(solution)/shard_map/all_to_all | solution.py:590
  39.5 8.5 %collective-permute-start.3 = (bf16[4,64,512]{2,1,0:T(8,128)(2,1)S(1)}, bf16[4,64,512]{2,1,0:T(8,128)(2,1)S(1)}, u32[]{:S(2)}, u32[]{:S(2)}) collective-permute-start(bf16[4,64,512]{2,1,0:T(8,128)(2,1)S(1)} %get-tuple-element.28), channel_id=1, source_target_pairs={{0,16},{16,32},{32,48},{48,0},{1,17},{17,33},{33,49},{49,1},{2,18}... | collective-permute-start | bytes 786440 | tf_op jit(solution)/shard_map/ppermute | solution.py:647
  40.7 12.9 %collective-permute-start.4 = (bf16[4,64,512]{2,1,0:T(8,128)(2,1)S(1)}, bf16[4,64,512]{2,1,0:T(8,128)(2,1)S(1)}, u32[]{:S(2)}, u32[]{:S(2)}) collective-permute-start(bf16[4,64,512]{2,1,0:T(8,128)(2,1)S(1)} %get-tuple-element.29), channel_id=1, source_target_pairs={{0,32},{16,48},{32,0},{48,16},{1,33},{17,49},{33,1},{49,17},{2,34}... | collective-permute-start | bytes 786440 | tf_op jit(solution)/shard_map/ppermute | solution.py:647
  43.1 10.5 %collective-permute-start.5 = (bf16[4,64,512]{2,1,0:T(8,128)(2,1)S(1)}, bf16[4,64,512]{2,1,0:T(8,128)(2,1)S(1)}, u32[]{:S(2)}, u32[]{:S(2)}) collective-permute-start(bf16[4,64,512]{2,1,0:T(8,128)(2,1)S(1)} %get-tuple-element.30), channel_id=1, source_target_pairs={{0,48},{16,0},{32,16},{48,32},{1,49},{17,1},{33,17},{49,33},{2,50}... | collective-permute-start | bytes 786440 | tf_op jit(solution)/shard_map/ppermute | solution.py:647
  44.3 3.3 %collective-permute-start.8 = (bf16[8,8192]{1,0:T(8,128)(2,1)S(1)}, bf16[8,8192]{1,0:T(8,128)(2,1)S(1)}, u32[]{:S(2)}, u32[]{:S(2)}) collective-permute-start(bf16[8,8192]{1,0:T(8,128)(2,1)S(1)} %bitcast.23), channel_id=1, source_target_pairs={{0,1},{1,0},{2,3},{3,2},{4,5},{5,4},{6,7},{7,6},{8,9},{9,8},{10,11... | collective-permute-start | bytes 393224 | tf_op jit(solution)/shard_map/ppermute | solution.py:657
  46.6 1.3 collective-permute-start.9
  59.2 24.4 %all-to-all-start.2 = ((bf16[16,16,1664]{2,1,0:T(8,128)(2,1)}), bf16[16,16,1664]{2,1,0:T(8,128)(2,1)S(1)}, u32[]{:S(2)}, u32[]{:S(2)}) async-start(bf16[16,16,1664]{2,1,0:T(8,128)(2,1)} %shard_map.150), calls=%async_computation.2 | async-start | bytes 1703936 | tf_op jit(solution)/shard_map/all_to_all | solution.py:590
  67.0 14.0 %collective-permute-start.6 = (bf16[8,64,512]{2,1,0:T(8,128)(2,1)S(1)}, bf16[8,64,512]{2,1,0:T(8,128)(2,1)S(1)}, u32[]{:S(2)}, u32[]{:S(2)}) collective-permute-start(bf16[8,64,512]{2,1,0:T(8,128)(2,1)S(1)} %pad_maximum_fusion), channel_id=1, source_target_pairs={{0,2},{2,4},{4,6},{6,8},{8,10},{10,12},{12,14},{14,0},{1,3},{3,5},... | collective-permute-start | bytes 1572872 | tf_op jit(solution)/shard_map/ppermute | solution.py:665
  67.1 13.8 %collective-permute-start.7 = (bf16[8,64,512]{2,1,0:T(8,128)(2,1)S(1)}, bf16[8,64,512]{2,1,0:T(8,128)(2,1)S(1)}, u32[]{:S(2)}, u32[]{:S(2)}) collective-permute-start(bf16[8,64,512]{2,1,0:T(8,128)(2,1)S(1)} %pad_maximum_fusion.1), channel_id=1, source_target_pairs={{0,14},{2,0},{4,2},{6,4},{8,6},{10,8},{12,10},{14,12},{1,15},{3,1}... | collective-permute-start | bytes 1572872 | tf_op jit(solution)/shard_map/ppermute | solution.py:665
  86.6 4.5 %collective-permute-start.10 = (bf16[4,1344,128]{2,1,0:T(8,128)(2,1)S(1)}, bf16[4,1344,128]{2,1,0:T(8,128)(2,1)S(1)}, u32[]{:S(2)}, u32[]{:S(2)}) collective-permute-start(bf16[4,1344,128]{2,1,0:T(8,128)(2,1)S(1)} %get-tuple-element.35), channel_id=1, source_target_pairs={{0,1},{1,0},{2,3},{3,2},{4,5},{5,4},{6,7},{7,6},{8,9},{9,8},{10,11... | collective-permute-start | bytes 4128776 | tf_op jit(solution)/shard_map/ppermute | solution.py:676
  115.9 25.6 %copy-start.5 = (bf16[1024,512]{1,0:T(8,128)(2,1)S(1)}, bf16[1024,512]{1,0:T(8,128)(2,1)}, u32[]{:S(2)}) copy-start(bf16[1024,512]{1,0:T(8,128)(2,1)} %copy-done.4) | copy-start | bytes 3145732
  115.9 25.6 %copy-start.7 = (bf16[1024,512]{1,0:T(8,128)(2,1)S(1)}, bf16[1024,512]{1,0:T(8,128)(2,1)}, u32[]{:S(2)}) copy-start(bf16[1024,512]{1,0:T(8,128)(2,1)} %copy-done.6) | copy-start | bytes 3145732
  136.3 5.2 %collective-permute-start.11 = (bf16[4,1344,128]{2,1,0:T(8,128)(2,1)S(1)}, bf16[4,1344,128]{2,1,0:T(8,128)(2,1)S(1)}, u32[]{:S(2)}, u32[]{:S(2)}) collective-permute-start(bf16[4,1344,128]{2,1,0:T(8,128)(2,1)S(1)} %bitcast.21), channel_id=1, source_target_pairs={{0,1},{1,0},{2,3},{3,2},{4,5},{5,4},{6,7},{7,6},{8,9},{9,8},{10,11... | collective-permute-start | bytes 4128776 | tf_op jit(solution)/shard_map/ppermute | solution.py:682
  172.7 21.2 %all-to-all-start.6 = ((bf16[16,16,1152]{2,1,0:T(8,128)(2,1)}), bf16[16,16,1152]{2,1,0:T(8,128)(2,1)S(1)}, u32[]{:S(2)}, u32[]{:S(2)}) async-start(bf16[16,16,1152]{2,1,0:T(8,128)(2,1)} %all_to_all.42), calls=%async_computation.6 | async-start | bytes 1179648 | tf_op jit(solution)/shard_map/all_to_all | solution.py:590
  194.4 24.3 %copy-start.9 = (f32[1,8192]{1,0:T(1,128)S(1)}, f32[1,8192]{1,0:T(1,128)}, u32[]{:S(2)}) copy-start(f32[1,8192]{1,0:T(1,128)} %gain_ref.3) | copy-start | bytes 98308
  (8 other events, 47.3 us)

commit v8 on v7

--- a/solution.py
+++ b/solution.py
@@ -54,7 +54,7 @@
         stored_ref[k, :, cols : 2 * cols] = ou_ref[:, at]
         stored_ref[k, :, 2 * cols :] = small
     part = hd // 2
-    section, member = here_ref[0], here_ref[1]
+    section, member = (here_ref[0] // layers), lax.rem(here_ref[0], layers)
     core = lax.rem(member, 2)
     side = len(out_refs)
     across = layers // side
@@ -85,7 +85,7 @@
     out_ref = refs[-1]
     layers, hd, rank, tokens, cols = sizes
     rows = tokens // layers
-    section, member = here_ref[0], here_ref[1]
+    section, member = (here_ref[0] // layers), lax.rem(here_ref[0], layers)
     core = lax.rem(member, 2)
     position = section * rows + lax.broadcasted_iota(jnp.int32, (rows, 1), 0)
     width = 2 * cols + 2 * hd
@@ -115,7 +115,8 @@
 
 def pick_kernel(side, across, here_ref, tenant_ref, slot_ref, parts_ref, *refs):
     lines, out_ref, turned, sems = refs[:side], refs[side], refs[side + 1 : -1], refs[-1]
-    place = lax.rem(here_ref[0], across)
+    layers = side * across
+    place = lax.rem(here_ref[0] // layers, across)
     copies = [
         pltpu.make_async_copy(
             lines[0].at[lax.rem(place + step, across)], turned_ref.at[0], sems.at[step]
@@ -157,8 +158,8 @@
     own_refs, other_refs, both_ref = refs[:across], refs[across:-1], refs[-1]
     pairs = across // 2
     part = hd // 2
-    plane = lax.rem(here_ref[1] // 2, 2)
-    line, place = here_ref[0] // across, lax.rem(here_ref[0], across)
+    plane = lax.rem(lax.rem(here_ref[0], layers) // 2, 2)
+    line, place = (here_ref[0] // layers) // across, lax.rem((here_ref[0] // layers), across)
     for step in range(layers):
         dx, dy = step // side, step % side
         l = lax.rem(line + side - dy, side) * across + lax.rem(place + across - dx, across)
@@ -186,7 +187,7 @@
 ):
     layers, hd, rank, tokens, cols = sizes
     rows = tokens // layers
-    core = lax.rem(here_ref[1], 2)
+    core = lax.rem(lax.rem(here_ref[0], layers), 2)
     copies = [
         pltpu.make_async_copy(both_ref.at[0], v_ref, sems.at[0]),
         pltpu.make_async_copy(both_ref.at[1], u_ref, sems.at[1]),
@@ -223,7 +224,8 @@
 
 
 def keep_kernel(sizes, here_ref, u_ref, v_ref, xs_ref, keep_ref):
-    core = lax.rem(here_ref[1], 2)
+    layers = sizes[0]
+    core = lax.rem(lax.rem(here_ref[0], layers), 2)
     for own_core in range(2):
         pl.when(core == own_core)(
             functools.partial(half_products, sizes, own_core, u_ref, v_ref, xs_ref, keep_ref)
@@ -302,7 +304,7 @@
     width = layers * hd
     base = 3 * tokens
     half_count = own_ref.shape[0]
-    core = lax.rem(here_ref[1], 2)
+    core = lax.rem(lax.rem(here_ref[0], layers), 2)
     for index in range(half_count):
         for source, place in ((own_ref, core), (other_ref, 1 - core)):
             to = place * half_count + index
@@ -609,8 +611,7 @@
     valid_tokens,
     tenant_slot,
 ):
-    section, sections = lax.axis_index(pipe), lax.axis_size(pipe)
-    member, members = lax.axis_index(dp), lax.axis_size(dp)
+    sections, members = lax.axis_size(pipe), lax.axis_size(dp)
     rows, features = inputs.shape[1], inputs.shape[2]
     hd, rank = w_value.shape[1], value_down.shape[2]
     cols = features // sections
@@ -619,7 +620,7 @@
     side = lax.axis_size("a") * lax.axis_size("b")
     across = lax.axis_size("x")
     planes = lax.axis_size("z")
-    here = jnp.stack([section, member]).astype(jnp.int32)
+    here = lax.axis_index(pipe + dp).astype(jnp.int32)[None]
     gain = norm_gain
     both_cores = [(0, 1), (1, 0)]
 

time: 220 us -> 218 us (level)
  Pallas kernels: 28.3 us -> 25.9 us
where the time goes in v8:
time: 218 us; the launch traced here: 217 us
  blocking collectives  84.6 us (39%)
  waiting for transfers between devices  56.7 us (26%)
  starting transfers between devices  44.7 us (21%)
  Pallas kernels  25.9 us (12%)
  local copies, waits for them, and re-layouts  3.25 us (1%)
    all_to_all x4, blocking collectives, swap(): return lax.all_to_all(value, axis, split_axis=0, concat_axis=0, tiled=True)  84.6 us
    all_to_all x4, starting transfers between devices, swap(): return lax.all_to_all(value, axis, split_axis=0, concat_axis=0, tiled=True)  25.5 us
    all_to_all x4, waiting for transfers between devices, swap(): return lax.all_to_all(value, axis, split_axis=0, concat_axis=0, tiled=True)  23.6 us
    pallas_call x1, Pallas kernels, solve(): pl.pallas_call(functools.partial(solve_kernel, sizes, features), out_shap...  14.7 us
    ppermute x2, waiting for transfers between devices, body(): lax.ppermute(jnp.concatenate(turned[at:at + pairs], axis=0), 'z', [(i, (i...  11.1 us
    ppermute x3, waiting for transfers between devices, body(): lax.ppermute(lines[step], ('a', 'b'), [(i, (i + step) % side) for i in ra...  11 us
    ppermute x3, waiting for transfers between devices, body(): lax.ppermute(turned[step], 'x', [(i, (i + step) % across) for i in range(...  5.67 us
    ppermute x3, starting transfers between devices, body(): lax.ppermute(lines[step], ('a', 'b'), [(i, (i + step) % side) for i in ra...  4.99 us
  transfers between devices with their start and end apart: 16, of which 11 were waited for; matrix products, arithmetic and copies ran while one was open for 0% of the time, Pallas kernels for 1%

profile of v8, /device:TPU:1, one launch (start us, length us, event | category | flops | bytes accessed | tf_op | source)
XLA Modules:
  0.0 217.2 jit_solution(11315256536651193537)
XLA Ops:
  0.7 2.9 %shard_map.147 = (bf16[16,16,1152]{2,1,0:T(8,128)(2,1)}, bf16[4,64,512]{2,1,0:T(8,128)(2,1)}, bf16[4,64,512]{2,1,0:T(8,128)(2,1)}, bf16[4,64,512]{2,1,0:T(8,128)(2,1)}, bf16[4,64,512]{2,1,0:T(8,128)(2,1)}) custom-call(s32[1]{0:T(128)} %bitcast.here_ref, bf16[64,8192]{1,0:T(8,128)(2,1)} %bitcast.31, bf16[64,8192]{1,0:T(8,128)(2,1)} %bitcast.32, ...), custom_call_target="tpu_custom_call" | custom-call | tf_op jit(solution)/shard_map/pallas_call | solution.py:466
  3.6 10.0 %all-to-all-start = ((bf16[16,16,1152]{2,1,0:T(8,128)(2,1)}), bf16[16,16,1152]{2,1,0:T(8,128)(2,1)S(1)}, u32[]{:S(2)}, u32[]{:S(2)}) async-start(bf16[16,16,1152]{2,1,0:T(8,128)(2,1)} %get-tuple-element.22), calls=%async_computation | async-start | bytes 1179648 | tf_op jit(solution)/shard_map/all_to_all | solution.py:592
  14.9 2.6 %collective-permute-start.1 = (bf16[4,64,512]{2,1,0:T(8,128)(2,1)}, bf16[4,64,512]{2,1,0:T(8,128)(2,1)S(1)}, u32[]{:S(2)}, u32[]{:S(2)}) collective-permute-start(bf16[4,64,512]{2,1,0:T(8,128)(2,1)} %get-tuple-element.25), channel_id=1, source_target_pairs={{0,128},{64,192},{128,0},{192,64},{1,129},{65,193},{129,1},{193,65... | collective-permute-start | bytes 786440 | tf_op jit(solution)/shard_map/ppermute | solution.py:643
  18.6 4.3 %collective-permute-done.refs_1_ = bf16[4,64,512]{2,1,0:T(8,128)(2,1)S(1)} collective-permute-done((bf16[4,64,512]{2,1,0:T(8,128)(2,1)}, bf16[4,64,512]{2,1,0:T(8,128)(2,1)S(1)}, u32[]{:S(2)}, u32[]{:S(2)}) %collective-permute-start) | collective-permute-done | bytes 262176 | tf_op jit(solution)/shard_map/ppermute | solution.py:643
  22.9 6.7 %collective-permute-done.1.refs_2_ = bf16[4,64,512]{2,1,0:T(8,128)(2,1)S(1)} collective-permute-done((bf16[4,64,512]{2,1,0:T(8,128)(2,1)}, bf16[4,64,512]{2,1,0:T(8,128)(2,1)S(1)}, u32[]{:S(2)}, u32[]{:S(2)}) %collective-permute-start.1) | collective-permute-done | bytes 262176 | tf_op jit(solution)/shard_map/ppermute | solution.py:643
  29.6 2.6 %all-to-all-done.parts_ref = bf16[16,16,1152]{2,1,0:T(8,128)(2,1)S(1)} async-done(((bf16[16,16,1152]{2,1,0:T(8,128)(2,1)}), bf16[16,16,1152]{2,1,0:T(8,128)(2,1)S(1)}, u32[]{:S(2)}, u32[]{:S(2)}) %all-to-all-start) | async-done | bytes 589856 | tf_op jit(solution)/shard_map/all_to_all | solution.py:592
  35.1 3.8 %all-to-all-start.1 = ((bf16[16,16,1152]{2,1,0:T(8,128)(2,1)}), bf16[16,16,1152]{2,1,0:T(8,128)(2,1)S(1)}, u32[]{:S(2)}, u32[]{:S(2)}) async-start(bf16[16,16,1152]{2,1,0:T(8,128)(2,1)} %get-tuple-element.31), calls=%async_computation.1 | async-start | bytes 1179648 | tf_op jit(solution)/shard_map/all_to_all | solution.py:592
  40.0 2.5 %collective-permute-start.4 = (bf16[4,64,512]{2,1,0:T(8,128)(2,1)S(1)}, bf16[4,64,512]{2,1,0:T(8,128)(2,1)S(1)}, u32[]{:S(2)}, u32[]{:S(2)}) collective-permute-start(bf16[4,64,512]{2,1,0:T(8,128)(2,1)S(1)} %get-tuple-element.29), channel_id=1, source_target_pairs={{0,32},{16,48},{32,0},{48,16},{1,33},{17,49},{33,1},{49,17},{2,34}... | collective-permute-start | bytes 786440 | tf_op jit(solution)/shard_map/ppermute | solution.py:648
  43.6 2.3 %collective-permute-start.8 = (bf16[8,8192]{1,0:T(8,128)(2,1)S(1)}, bf16[8,8192]{1,0:T(8,128)(2,1)S(1)}, u32[]{:S(2)}, u32[]{:S(2)}) collective-permute-start(bf16[8,8192]{1,0:T(8,128)(2,1)S(1)} %bitcast.22), channel_id=1, source_target_pairs={{0,1},{1,0},{2,3},{3,2},{4,5},{5,4},{6,7},{7,6},{8,9},{9,8},{10,11... | collective-permute-start | bytes 393224 | tf_op jit(solution)/shard_map/ppermute | solution.py:658
  47.3 5.7 %collective-permute-done.4.refs_2_.refs_1_ = bf16[4,64,512]{2,1,0:T(8,128)(2,1)S(1)} collective-permute-done((bf16[4,64,512]{2,1,0:T(8,128)(2,1)S(1)}, bf16[4,64,512]{2,1,0:T(8,128)(2,1)S(1)}, u32[]{:S(2)}, u32[]{:S(2)}) %collective-permute-start.4) | collective-permute-done | bytes 262176 | tf_op jit(solution)/shard_map/ppermute | solution.py:648
  53.0 4.0 %all-to-all-done.1.parts_ref = bf16[16,16,1152]{2,1,0:T(8,128)(2,1)S(1)} async-done(((bf16[16,16,1152]{2,1,0:T(8,128)(2,1)}), bf16[16,16,1152]{2,1,0:T(8,128)(2,1)S(1)}, u32[]{:S(2)}, u32[]{:S(2)}) %all-to-all-start.1) | async-done | bytes 589856 | tf_op jit(solution)/shard_map/all_to_all | solution.py:592
  58.5 7.7 %all-to-all-start.2 = ((bf16[16,16,1664]{2,1,0:T(8,128)(2,1)}), bf16[16,16,1664]{2,1,0:T(8,128)(2,1)S(1)}, u32[]{:S(2)}, u32[]{:S(2)}) async-start(bf16[16,16,1664]{2,1,0:T(8,128)(2,1)} %shard_map.150), calls=%async_computation.2 | async-start | bytes 1703936 | tf_op jit(solution)/shard_map/all_to_all | solution.py:592
  66.4 2.7 %collective-permute-start.7 = (bf16[8,64,512]{2,1,0:T(8,128)(2,1)S(1)}, bf16[8,64,512]{2,1,0:T(8,128)(2,1)S(1)}, u32[]{:S(2)}, u32[]{:S(2)}) collective-permute-start(bf16[8,64,512]{2,1,0:T(8,128)(2,1)S(1)} %pad_maximum_fusion.1), channel_id=1, source_target_pairs={{0,14},{2,0},{4,2},{6,4},{8,6},{10,8},{12,10},{14,12},{1,15},{3,1}... | collective-permute-start | bytes 1572872 | tf_op jit(solution)/shard_map/ppermute | solution.py:666
  69.2 11.1 %collective-permute-done.6.refs_4_ = bf16[8,64,512]{2,1,0:T(8,128)(2,1)S(1)} collective-permute-done((bf16[8,64,512]{2,1,0:T(8,128)(2,1)S(1)}, bf16[8,64,512]{2,1,0:T(8,128)(2,1)S(1)}, u32[]{:S(2)}, u32[]{:S(2)}) %collective-permute-start.6) | collective-permute-done | bytes 524320 | tf_op jit(solution)/shard_map/ppermute | solution.py:666
  82.3 2.5 %shard_map.151 = (bf16[1024,512]{1,0:T(8,128)(2,1)S(1)}, bf16[1024,512]{1,0:T(8,128)(2,1)S(1)}, bf16[256,512]{1,0:T(8,128)(2,1)S(1)}, bf16[4,1344,128]{2,1,0:T(8,128)(2,1)S(1)}) custom-call(s32[1]{0:T(128)} %bitcast.here_ref, bf16[2,1024,512]{2,1,0:T(8,128)(2,1)S(1)} %shard_map.149.both_ref, bf16[16,16,1664]{2,1,0:T(8,128)(2,1)S(1)} %all-to-all-done.2.q_ref), custom_call_target="tpu_custom_call" | custom-call | tf_op jit(solution)/shard_map/pallas_call | solution.py:539
  89.7 24.0 %all_to_all.40 = bf16[8,672,128]{2,1,0:T(8,128)(2,1)S(1)} all-to-all(bf16[8,672,128]{2,1,0:T(8,128)(2,1)S(1)} %bitcast.26), channel_id=1, replica_groups=mesh['a'=2,'b'=2,'x'=4,'z'=8,'core'=2] {'b','x'}, dimensions={0} | all-to-all | bytes 2752512 | tf_op jit(solution)/shard_map/all_to_all | solution.py:592
  114.1 20.4 %all_to_all.41 = bf16[8,672,128]{2,1,0:T(8,128)(2,1)S(1)} all-to-all(bf16[8,672,128]{2,1,0:T(8,128)(2,1)S(1)} %broadcast_in_dim.41), channel_id=1, replica_groups=mesh['a'=2,'b'=2,'x'=4,'z'=8,'core'=2] {'b','x'}, dimensions={0} | all-to-all | bytes 2752512 | tf_op jit(solution)/shard_map/all_to_all | solution.py:592
  134.5 2.4 %collective-permute-start.11 = (bf16[4,1344,128]{2,1,0:T(8,128)(2,1)S(1)}, bf16[4,1344,128]{2,1,0:T(8,128)(2,1)S(1)}, u32[]{:S(2)}, u32[]{:S(2)}) collective-permute-start(bf16[4,1344,128]{2,1,0:T(8,128)(2,1)S(1)} %bitcast.20), channel_id=1, source_target_pairs={{0,1},{1,0},{2,3},{3,2},{4,5},{5,4},{6,7},{7,6},{8,9},{9,8},{10,11... | collective-permute-start | bytes 4128776 | tf_op jit(solution)/shard_map/ppermute | solution.py:683
  136.9 2.8 %collective-permute-done.11.other_ref = bf16[4,1344,128]{2,1,0:T(8,128)(2,1)S(1)} collective-permute-done((bf16[4,1344,128]{2,1,0:T(8,128)(2,1)S(1)}, bf16[4,1344,128]{2,1,0:T(8,128)(2,1)S(1)}, u32[]{:S(2)}, u32[]{:S(2)}) %collective-permute-start.11) | collective-permute-done | bytes 1376288 | tf_op jit(solution)/shard_map/ppermute | solution.py:683
  139.7 14.7 %shard_map.153 = bf16[16,16,1152]{2,1,0:T(8,128)(2,1)S(1)} custom-call(s32[1]{0:T(128)} %bitcast.here_ref, bf16[4,1344,128]{2,1,0:T(8,128)(2,1)S(1)} %bitcast.21, bf16[4,1344,128]{2,1,0:T(8,128)(2,1)S(1)} %collective-permute-done.11.other_ref, bf16[256,512]{1,0:T(8,128)(2,1)S(1)} %get-tuple-element.34.xs_ref, bf16[1024,512]{1,0:T(8,128)(2,1)S(1)} %copy-done.5, ...), custom_call_target="tpu_custom_call" | custom-call | tf_op jit(solution)/shard_map/pallas_call | solution.py:572
  154.4 16.0 %all_to_all.42 = bf16[16,16,1152]{2,1,0:T(8,128)(2,1)} all-to-all(bf16[16,16,1152]{2,1,0:T(8,128)(2,1)S(1)} %shard_map.153), channel_id=1, replica_groups=mesh['a'=2,'b'=2,'x'=4,'z'=8,'core'=2] {'b','x','a'}, dimensions={0} | all-to-all | bytes 1179648 | tf_op jit(solution)/shard_map/all_to_all | solution.py:592
  170.4 4.1 %all-to-all-start.6 = ((bf16[16,16,1152]{2,1,0:T(8,128)(2,1)}), bf16[16,16,1152]{2,1,0:T(8,128)(2,1)S(1)}, u32[]{:S(2)}, u32[]{:S(2)}) async-start(bf16[16,16,1152]{2,1,0:T(8,128)(2,1)} %all_to_all.42), calls=%async_computation.6 | async-start | bytes 1179648 | tf_op jit(solution)/shard_map/all_to_all | solution.py:592
  174.7 17.0 %all-to-all-done.6 = bf16[16,16,1152]{2,1,0:T(8,128)(2,1)S(1)} async-done(((bf16[16,16,1152]{2,1,0:T(8,128)(2,1)}), bf16[16,16,1152]{2,1,0:T(8,128)(2,1)S(1)}, u32[]{:S(2)}, u32[]{:S(2)}) %all-to-all-start.6) | async-done | bytes 589856 | tf_op jit(solution)/shard_map/all_to_all | solution.py:592
  192.2 24.2 %all_to_all.43.owned_ref = bf16[16,16,1152]{2,1,0:T(8,128)(2,1)S(1)} all-to-all(bf16[16,16,1152]{2,1,0:T(8,128)(2,1)S(1)} %bitcast.30), channel_id=1, replica_groups=mesh['a'=2,'b'=2,'x'=4,'z'=8,'core'=2] {'z','core'}, dimensions={0} | all-to-all | bytes 1179648 | tf_op jit(solution)/shard_map/all_to_all | solution.py:592
  (59 shorter events, 19.5 us)
Async XLA Ops:
  0.6 31.6 %copy-start.12 = (s32[16]{0:T(128)S(1)}, s32[16]{0:T(128)}, u32[]{:S(2)}) copy-start(s32[16]{0:T(128)} %tenant_ref.3) | copy-start | bytes 196
  0.7 31.6 %copy-start.13 = (s32[16]{0:T(128)S(1)}, s32[16]{0:T(128)}, u32[]{:S(2)}) copy-start(s32[16]{0:T(128)} %slot_ref.1) | copy-start | bytes 196
  3.6 28.6 %all-to-all-start = ((bf16[16,16,1152]{2,1,0:T(8,128)(2,1)}), bf16[16,16,1152]{2,1,0:T(8,128)(2,1)S(1)}, u32[]{:S(2)}, u32[]{:S(2)}) async-start(bf16[16,16,1152]{2,1,0:T(8,128)(2,1)} %get-tuple-element.22), calls=%async_computation | async-start | bytes 1179648 | tf_op jit(solution)/shard_map/all_to_all | solution.py:592
  13.6 9.3 %collective-permute-start = (bf16[4,64,512]{2,1,0:T(8,128)(2,1)}, bf16[4,64,512]{2,1,0:T(8,128)(2,1)S(1)}, u32[]{:S(2)}, u32[]{:S(2)}) collective-permute-start(bf16[4,64,512]{2,1,0:T(8,128)(2,1)} %get-tuple-element.24), channel_id=1, source_target_pairs={{0,64},{64,128},{128,192},{192,0},{1,65},{65,129},{129,193},{193,1... | collective-permute-start | bytes 786440 | tf_op jit(solution)/shard_map/ppermute | solution.py:643
  14.9 14.7 %collective-permute-start.1 = (bf16[4,64,512]{2,1,0:T(8,128)(2,1)}, bf16[4,64,512]{2,1,0:T(8,128)(2,1)S(1)}, u32[]{:S(2)}, u32[]{:S(2)}) collective-permute-start(bf16[4,64,512]{2,1,0:T(8,128)(2,1)} %get-tuple-element.25), channel_id=1, source_target_pairs={{0,128},{64,192},{128,0},{192,64},{1,129},{65,193},{129,1},{193,65... | collective-permute-start | bytes 786440 | tf_op jit(solution)/shard_map/ppermute | solution.py:643
  17.5 12.1 %collective-permute-start.2 = (bf16[4,64,512]{2,1,0:T(8,128)(2,1)}, bf16[4,64,512]{2,1,0:T(8,128)(2,1)S(1)}, u32[]{:S(2)}, u32[]{:S(2)}) collective-permute-start(bf16[4,64,512]{2,1,0:T(8,128)(2,1)} %get-tuple-element.26), channel_id=1, source_target_pairs={{0,192},{64,0},{128,64},{192,128},{1,193},{65,1},{129,65},{193,129... | collective-permute-start | bytes 786440 | tf_op jit(solution)/shard_map/ppermute | solution.py:643
  33.2 23.7 %copy-start.14 = (s32[16]{0:T(128)S(1)}, s32[16]{0:T(128)}, u32[]{:S(2)}) copy-start(s32[16]{0:T(128)} %valid_ref.1) | copy-start | bytes 196
  35.0 31.2 %copy-start.2 = (bf16[4,64,512]{2,1,0:T(8,128)(2,1)}, bf16[4,64,512]{2,1,0:T(8,128)(2,1)S(1)}, u32[]{:S(2)}) copy-start(bf16[4,64,512]{2,1,0:T(8,128)(2,1)S(1)} %get-tuple-element.27.refs_0_) | copy-start | bytes 786436
  35.1 21.9 %all-to-all-start.1 = ((bf16[16,16,1152]{2,1,0:T(8,128)(2,1)}), bf16[16,16,1152]{2,1,0:T(8,128)(2,1)S(1)}, u32[]{:S(2)}, u32[]{:S(2)}) async-start(bf16[16,16,1152]{2,1,0:T(8,128)(2,1)} %get-tuple-element.31), calls=%async_computation.1 | async-start | bytes 1179648 | tf_op jit(solution)/shard_map/all_to_all | solution.py:592
  38.8 8.5 %collective-permute-start.3 = (bf16[4,64,512]{2,1,0:T(8,128)(2,1)S(1)}, bf16[4,64,512]{2,1,0:T(8,128)(2,1)S(1)}, u32[]{:S(2)}, u32[]{:S(2)}) collective-permute-start(bf16[4,64,512]{2,1,0:T(8,128)(2,1)S(1)} %get-tuple-element.28), channel_id=1, source_target_pairs={{0,16},{16,32},{32,48},{48,0},{1,17},{17,33},{33,49},{49,1},{2,18}... | collective-permute-start | bytes 786440 | tf_op jit(solution)/shard_map/ppermute | solution.py:648
  40.0 12.9 %collective-permute-start.4 = (bf16[4,64,512]{2,1,0:T(8,128)(2,1)S(1)}, bf16[4,64,512]{2,1,0:T(8,128)(2,1)S(1)}, u32[]{:S(2)}, u32[]{:S(2)}) collective-permute-start(bf16[4,64,512]{2,1,0:T(8,128)(2,1)S(1)} %get-tuple-element.29), channel_id=1, source_target_pairs={{0,32},{16,48},{32,0},{48,16},{1,33},{17,49},{33,1},{49,17},{2,34}... | collective-permute-start | bytes 786440 | tf_op jit(solution)/shard_map/ppermute | solution.py:648
  42.5 10.5 %collective-permute-start.5 = (bf16[4,64,512]{2,1,0:T(8,128)(2,1)S(1)}, bf16[4,64,512]{2,1,0:T(8,128)(2,1)S(1)}, u32[]{:S(2)}, u32[]{:S(2)}) collective-permute-start(bf16[4,64,512]{2,1,0:T(8,128)(2,1)S(1)} %get-tuple-element.30), channel_id=1, source_target_pairs={{0,48},{16,0},{32,16},{48,32},{1,49},{17,1},{33,17},{49,33},{2,50}... | collective-permute-start | bytes 786440 | tf_op jit(solution)/shard_map/ppermute | solution.py:648
  43.6 3.3 %collective-permute-start.8 = (bf16[8,8192]{1,0:T(8,128)(2,1)S(1)}, bf16[8,8192]{1,0:T(8,128)(2,1)S(1)}, u32[]{:S(2)}, u32[]{:S(2)}) collective-permute-start(bf16[8,8192]{1,0:T(8,128)(2,1)S(1)} %bitcast.22), channel_id=1, source_target_pairs={{0,1},{1,0},{2,3},{3,2},{4,5},{5,4},{6,7},{7,6},{8,9},{9,8},{10,11... | collective-permute-start | bytes 393224 | tf_op jit(solution)/shard_map/ppermute | solution.py:658
  45.9 1.3 collective-permute-start.9
  53.0 13.4 %copy-start = (bf16[4,64,512]{2,1,0:T(8,128)(2,1)}, bf16[4,64,512]{2,1,0:T(8,128)(2,1)S(1)}, u32[]{:S(2)}) copy-start(bf16[4,64,512]{2,1,0:T(8,128)(2,1)S(1)} %collective-permute-done.5.refs_3_.refs_2_) | copy-start | bytes 786436
  58.5 23.8 %all-to-all-start.2 = ((bf16[16,16,1664]{2,1,0:T(8,128)(2,1)}), bf16[16,16,1664]{2,1,0:T(8,128)(2,1)S(1)}, u32[]{:S(2)}, u32[]{:S(2)}) async-start(bf16[16,16,1664]{2,1,0:T(8,128)(2,1)} %shard_map.150), calls=%async_computation.2 | async-start | bytes 1703936 | tf_op jit(solution)/shard_map/all_to_all | solution.py:592
  66.3 14.0 %collective-permute-start.6 = (bf16[8,64,512]{2,1,0:T(8,128)(2,1)S(1)}, bf16[8,64,512]{2,1,0:T(8,128)(2,1)S(1)}, u32[]{:S(2)}, u32[]{:S(2)}) collective-permute-start(bf16[8,64,512]{2,1,0:T(8,128)(2,1)S(1)} %pad_maximum_fusion), channel_id=1, source_target_pairs={{0,2},{2,4},{4,6},{6,8},{8,10},{10,12},{12,14},{14,0},{1,3},{3,5},... | collective-permute-start | bytes 1572872 | tf_op jit(solution)/shard_map/ppermute | solution.py:666
  66.4 13.8 %collective-permute-start.7 = (bf16[8,64,512]{2,1,0:T(8,128)(2,1)S(1)}, bf16[8,64,512]{2,1,0:T(8,128)(2,1)S(1)}, u32[]{:S(2)}, u32[]{:S(2)}) collective-permute-start(bf16[8,64,512]{2,1,0:T(8,128)(2,1)S(1)} %pad_maximum_fusion.1), channel_id=1, source_target_pairs={{0,14},{2,0},{4,2},{6,4},{8,6},{10,8},{12,10},{14,12},{1,15},{3,1}... | collective-permute-start | bytes 1572872 | tf_op jit(solution)/shard_map/ppermute | solution.py:666
  84.8 4.5 %collective-permute-start.10 = (bf16[4,1344,128]{2,1,0:T(8,128)(2,1)S(1)}, bf16[4,1344,128]{2,1,0:T(8,128)(2,1)S(1)}, u32[]{:S(2)}, u32[]{:S(2)}) collective-permute-start(bf16[4,1344,128]{2,1,0:T(8,128)(2,1)S(1)} %get-tuple-element.35), channel_id=1, source_target_pairs={{0,1},{1,0},{2,3},{3,2},{4,5},{5,4},{6,7},{7,6},{8,9},{9,8},{10,11... | collective-permute-start | bytes 4128776 | tf_op jit(solution)/shard_map/ppermute | solution.py:677
  114.1 25.6 %copy-start.5 = (bf16[1024,512]{1,0:T(8,128)(2,1)S(1)}, bf16[1024,512]{1,0:T(8,128)(2,1)}, u32[]{:S(2)}) copy-start(bf16[1024,512]{1,0:T(8,128)(2,1)} %copy-done.4) | copy-start | bytes 3145732
  114.1 25.6 %copy-start.7 = (bf16[1024,512]{1,0:T(8,128)(2,1)S(1)}, bf16[1024,512]{1,0:T(8,128)(2,1)}, u32[]{:S(2)}) copy-start(bf16[1024,512]{1,0:T(8,128)(2,1)} %copy-done.6) | copy-start | bytes 3145732
  134.5 5.2 %collective-permute-start.11 = (bf16[4,1344,128]{2,1,0:T(8,128)(2,1)S(1)}, bf16[4,1344,128]{2,1,0:T(8,128)(2,1)S(1)}, u32[]{:S(2)}, u32[]{:S(2)}) collective-permute-start(bf16[4,1344,128]{2,1,0:T(8,128)(2,1)S(1)} %bitcast.20), channel_id=1, source_target_pairs={{0,1},{1,0},{2,3},{3,2},{4,5},{5,4},{6,7},{7,6},{8,9},{9,8},{10,11... | collective-permute-start | bytes 4128776 | tf_op jit(solution)/shard_map/ppermute | solution.py:683
  170.4 21.3 %all-to-all-start.6 = ((bf16[16,16,1152]{2,1,0:T(8,128)(2,1)}), bf16[16,16,1152]{2,1,0:T(8,128)(2,1)S(1)}, u32[]{:S(2)}, u32[]{:S(2)}) async-start(bf16[16,16,1152]{2,1,0:T(8,128)(2,1)} %all_to_all.42), calls=%async_computation.6 | async-start | bytes 1179648 | tf_op jit(solution)/shard_map/all_to_all | solution.py:592
  192.1 24.3 %copy-start.9 = (f32[1,8192]{1,0:T(1,128)S(1)}, f32[1,8192]{1,0:T(1,128)}, u32[]{:S(2)}) copy-start(f32[1,8192]{1,0:T(1,128)} %gain_ref.3) | copy-start | bytes 98308
  (7 other events, 32.3 us)

commit v9 on v8

--- a/solution.py
+++ b/solution.py
@@ -10,7 +10,8 @@
 adapter_scale = 2.0
 norm_eps = 1e-05
 block = 256
-vmem_bytes = 20 * 1024 * 1024
+vmem_bytes = 12 * 1024 * 1024
+solve_vmem_bytes = 20 * 1024 * 1024
 whole_vmem_bytes = 56 * 1024 * 1024
 merge_cost_bytes = 40 * 1024 * 1024
 pipe = ("a", "b", "x")
@@ -584,7 +585,7 @@
             pltpu.VMEM((2 * own.shape[0],) + own.shape[1:], jnp.bfloat16),
             pltpu.SemaphoreType.DMA((2 * own.shape[0],)),
         ],
-        compiler_params=params(),
+        compiler_params=params(solve_vmem_bytes),
     )(here, own, other, xs, u, v, q)
 
 

time: 218 us -> 218 us (level)
  no operation moved by 1% of the time
where the time goes in v9:
time: 218 us; the launch traced here: 217 us
  blocking collectives  84.6 us (39%)
  waiting for transfers between devices  56.8 us (26%)
  starting transfers between devices  44.7 us (21%)
  Pallas kernels  25.9 us (12%)
  local copies, waits for them, and re-layouts  3.25 us (1%)
    all_to_all x4, blocking collectives, swap(): return lax.all_to_all(value, axis, split_axis=0, concat_axis=0, tiled=True)  84.6 us
    all_to_all x4, starting transfers between devices, swap(): return lax.all_to_all(value, axis, split_axis=0, concat_axis=0, tiled=True)  25.5 us
    all_to_all x4, waiting for transfers between devices, swap(): return lax.all_to_all(value, axis, split_axis=0, concat_axis=0, tiled=True)  23.6 us
    pallas_call x1, Pallas kernels, solve(): pl.pallas_call(functools.partial(solve_kernel, sizes, features), out_shap...  14.7 us
    ppermute x2, waiting for transfers between devices, body(): lax.ppermute(jnp.concatenate(turned[at:at + pairs], axis=0), 'z', [(i, (i...  11.1 us
    ppermute x3, waiting for transfers between devices, body(): lax.ppermute(lines[step], ('a', 'b'), [(i, (i + step) % side) for i in ra...  11 us
    ppermute x3, waiting for transfers between devices, body(): lax.ppermute(turned[step], 'x', [(i, (i + step) % across) for i in range(...  5.67 us
    ppermute x3, starting transfers between devices, body(): lax.ppermute(lines[step], ('a', 'b'), [(i, (i + step) % side) for i in ra...  4.99 us
  transfers between devices with their start and end apart: 16, of which 11 were waited for; matrix products, arithmetic and copies ran while one was open for 0% of the time, Pallas kernels for 1%

profile of v9, /device:TPU:1, one launch (start us, length us, event | category | flops | bytes accessed | tf_op | source)
XLA Modules:
  0.0 217.2 jit_solution(14080038730704007223)
XLA Ops:
  0.7 2.9 %shard_map.147 = (bf16[16,16,1152]{2,1,0:T(8,128)(2,1)}, bf16[4,64,512]{2,1,0:T(8,128)(2,1)}, bf16[4,64,512]{2,1,0:T(8,128)(2,1)}, bf16[4,64,512]{2,1,0:T(8,128)(2,1)}, bf16[4,64,512]{2,1,0:T(8,128)(2,1)}) custom-call(s32[1]{0:T(128)} %bitcast.here_ref, bf16[64,8192]{1,0:T(8,128)(2,1)} %bitcast.31, bf16[64,8192]{1,0:T(8,128)(2,1)} %bitcast.32, ...), custom_call_target="tpu_custom_call" | custom-call | tf_op jit(solution)/shard_map/pallas_call | solution.py:467
  3.6 10.0 %all-to-all-start = ((bf16[16,16,1152]{2,1,0:T(8,128)(2,1)}), bf16[16,16,1152]{2,1,0:T(8,128)(2,1)S(1)}, u32[]{:S(2)}, u32[]{:S(2)}) async-start(bf16[16,16,1152]{2,1,0:T(8,128)(2,1)} %get-tuple-element.22), calls=%async_computation | async-start | bytes 1179648 | tf_op jit(solution)/shard_map/all_to_all | solution.py:593
  14.9 2.6 %collective-permute-start.1 = (bf16[4,64,512]{2,1,0:T(8,128)(2,1)}, bf16[4,64,512]{2,1,0:T(8,128)(2,1)S(1)}, u32[]{:S(2)}, u32[]{:S(2)}) collective-permute-start(bf16[4,64,512]{2,1,0:T(8,128)(2,1)} %get-tuple-element.25), channel_id=1, source_target_pairs={{0,128},{64,192},{128,0},{192,64},{1,129},{65,193},{129,1},{193,65... | collective-permute-start | bytes 786440 | tf_op jit(solution)/shard_map/ppermute | solution.py:644
  18.6 4.3 %collective-permute-done.refs_1_ = bf16[4,64,512]{2,1,0:T(8,128)(2,1)S(1)} collective-permute-done((bf16[4,64,512]{2,1,0:T(8,128)(2,1)}, bf16[4,64,512]{2,1,0:T(8,128)(2,1)S(1)}, u32[]{:S(2)}, u32[]{:S(2)}) %collective-permute-start) | collective-permute-done | bytes 262176 | tf_op jit(solution)/shard_map/ppermute | solution.py:644
  22.9 6.7 %collective-permute-done.1.refs_2_ = bf16[4,64,512]{2,1,0:T(8,128)(2,1)S(1)} collective-permute-done((bf16[4,64,512]{2,1,0:T(8,128)(2,1)}, bf16[4,64,512]{2,1,0:T(8,128)(2,1)S(1)}, u32[]{:S(2)}, u32[]{:S(2)}) %collective-permute-start.1) | collective-permute-done | bytes 262176 | tf_op jit(solution)/shard_map/ppermute | solution.py:644
  29.6 2.6 %all-to-all-done.parts_ref = bf16[16,16,1152]{2,1,0:T(8,128)(2,1)S(1)} async-done(((bf16[16,16,1152]{2,1,0:T(8,128)(2,1)}), bf16[16,16,1152]{2,1,0:T(8,128)(2,1)S(1)}, u32[]{:S(2)}, u32[]{:S(2)}) %all-to-all-start) | async-done | bytes 589856 | tf_op jit(solution)/shard_map/all_to_all | solution.py:593
  35.1 3.8 %all-to-all-start.1 = ((bf16[16,16,1152]{2,1,0:T(8,128)(2,1)}), bf16[16,16,1152]{2,1,0:T(8,128)(2,1)S(1)}, u32[]{:S(2)}, u32[]{:S(2)}) async-start(bf16[16,16,1152]{2,1,0:T(8,128)(2,1)} %get-tuple-element.31), calls=%async_computation.1 | async-start | bytes 1179648 | tf_op jit(solution)/shard_map/all_to_all | solution.py:593
  40.0 2.5 %collective-permute-start.4 = (bf16[4,64,512]{2,1,0:T(8,128)(2,1)S(1)}, bf16[4,64,512]{2,1,0:T(8,128)(2,1)S(1)}, u32[]{:S(2)}, u32[]{:S(2)}) collective-permute-start(bf16[4,64,512]{2,1,0:T(8,128)(2,1)S(1)} %get-tuple-element.29), channel_id=1, source_target_pairs={{0,32},{16,48},{32,0},{48,16},{1,33},{17,49},{33,1},{49,17},{2,34}... | collective-permute-start | bytes 786440 | tf_op jit(solution)/shard_map/ppermute | solution.py:649
  43.6 2.3 %collective-permute-start.8 = (bf16[8,8192]{1,0:T(8,128)(2,1)S(1)}, bf16[8,8192]{1,0:T(8,128)(2,1)S(1)}, u32[]{:S(2)}, u32[]{:S(2)}) collective-permute-start(bf16[8,8192]{1,0:T(8,128)(2,1)S(1)} %bitcast.22), channel_id=1, source_target_pairs={{0,1},{1,0},{2,3},{3,2},{4,5},{5,4},{6,7},{7,6},{8,9},{9,8},{10,11... | collective-permute-start | bytes 393224 | tf_op jit(solution)/shard_map/ppermute | solution.py:659
  47.3 5.7 %collective-permute-done.4.refs_2_.refs_1_ = bf16[4,64,512]{2,1,0:T(8,128)(2,1)S(1)} collective-permute-done((bf16[4,64,512]{2,1,0:T(8,128)(2,1)S(1)}, bf16[4,64,512]{2,1,0:T(8,128)(2,1)S(1)}, u32[]{:S(2)}, u32[]{:S(2)}) %collective-permute-start.4) | collective-permute-done | bytes 262176 | tf_op jit(solution)/shard_map/ppermute | solution.py:649
  53.0 4.0 %all-to-all-done.1.parts_ref = bf16[16,16,1152]{2,1,0:T(8,128)(2,1)S(1)} async-done(((bf16[16,16,1152]{2,1,0:T(8,128)(2,1)}), bf16[16,16,1152]{2,1,0:T(8,128)(2,1)S(1)}, u32[]{:S(2)}, u32[]{:S(2)}) %all-to-all-start.1) | async-done | bytes 589856 | tf_op jit(solution)/shard_map/all_to_all | solution.py:593
  58.5 7.7 %all-to-all-start.2 = ((bf16[16,16,1664]{2,1,0:T(8,128)(2,1)}), bf16[16,16,1664]{2,1,0:T(8,128)(2,1)S(1)}, u32[]{:S(2)}, u32[]{:S(2)}) async-start(bf16[16,16,1664]{2,1,0:T(8,128)(2,1)} %shard_map.150), calls=%async_computation.2 | async-start | bytes 1703936 | tf_op jit(solution)/shard_map/all_to_all | solution.py:593
  66.4 2.7 %collective-permute-start.7 = (bf16[8,64,512]{2,1,0:T(8,128)(2,1)S(1)}, bf16[8,64,512]{2,1,0:T(8,128)(2,1)S(1)}, u32[]{:S(2)}, u32[]{:S(2)}) collective-permute-start(bf16[8,64,512]{2,1,0:T(8,128)(2,1)S(1)} %pad_maximum_fusion.1), channel_id=1, source_target_pairs={{0,14},{2,0},{4,2},{6,4},{8,6},{10,8},{12,10},{14,12},{1,15},{3,1}... | collective-permute-start | bytes 1572872 | tf_op jit(solution)/shard_map/ppermute | solution.py:667
  69.2 11.1 %collective-permute-done.6.refs_4_ = bf16[8,64,512]{2,1,0:T(8,128)(2,1)S(1)} collective-permute-done((bf16[8,64,512]{2,1,0:T(8,128)(2,1)S(1)}, bf16[8,64,512]{2,1,0:T(8,128)(2,1)S(1)}, u32[]{:S(2)}, u32[]{:S(2)}) %collective-permute-start.6) | collective-permute-done | bytes 524320 | tf_op jit(solution)/shard_map/ppermute | solution.py:667
  82.3 2.5 %shard_map.151 = (bf16[1024,512]{1,0:T(8,128)(2,1)S(1)}, bf16[1024,512]{1,0:T(8,128)(2,1)S(1)}, bf16[256,512]{1,0:T(8,128)(2,1)S(1)}, bf16[4,1344,128]{2,1,0:T(8,128)(2,1)S(1)}) custom-call(s32[1]{0:T(128)} %bitcast.here_ref, bf16[2,1024,512]{2,1,0:T(8,128)(2,1)S(1)} %shard_map.149.both_ref, bf16[16,16,1664]{2,1,0:T(8,128)(2,1)S(1)} %all-to-all-done.2.q_ref), custom_call_target="tpu_custom_call" | custom-call | tf_op jit(solution)/shard_map/pallas_call | solution.py:540
  89.7 24.0 %all_to_all.40 = bf16[8,672,128]{2,1,0:T(8,128)(2,1)S(1)} all-to-all(bf16[8,672,128]{2,1,0:T(8,128)(2,1)S(1)} %bitcast.26), channel_id=1, replica_groups=mesh['a'=2,'b'=2,'x'=4,'z'=8,'core'=2] {'b','x'}, dimensions={0} | all-to-all | bytes 2752512 | tf_op jit(solution)/shard_map/all_to_all | solution.py:593
  114.1 20.4 %all_to_all.41 = bf16[8,672,128]{2,1,0:T(8,128)(2,1)S(1)} all-to-all(bf16[8,672,128]{2,1,0:T(8,128)(2,1)S(1)} %broadcast_in_dim.41), channel_id=1, replica_groups=mesh['a'=2,'b'=2,'x'=4,'z'=8,'core'=2] {'b','x'}, dimensions={0} | all-to-all | bytes 2752512 | tf_op jit(solution)/shard_map/all_to_all | solution.py:593
  134.5 2.4 %collective-permute-start.11 = (bf16[4,1344,128]{2,1,0:T(8,128)(2,1)S(1)}, bf16[4,1344,128]{2,1,0:T(8,128)(2,1)S(1)}, u32[]{:S(2)}, u32[]{:S(2)}) collective-permute-start(bf16[4,1344,128]{2,1,0:T(8,128)(2,1)S(1)} %bitcast.20), channel_id=1, source_target_pairs={{0,1},{1,0},{2,3},{3,2},{4,5},{5,4},{6,7},{7,6},{8,9},{9,8},{10,11... | collective-permute-start | bytes 4128776 | tf_op jit(solution)/shard_map/ppermute | solution.py:684
  137.0 2.8 %collective-permute-done.11.other_ref = bf16[4,1344,128]{2,1,0:T(8,128)(2,1)S(1)} collective-permute-done((bf16[4,1344,128]{2,1,0:T(8,128)(2,1)S(1)}, bf16[4,1344,128]{2,1,0:T(8,128)(2,1)S(1)}, u32[]{:S(2)}, u32[]{:S(2)}) %collective-permute-start.11) | collective-permute-done | bytes 1376288 | tf_op jit(solution)/shard_map/ppermute | solution.py:684
  139.7 14.7 %shard_map.153 = bf16[16,16,1152]{2,1,0:T(8,128)(2,1)S(1)} custom-call(s32[1]{0:T(128)} %bitcast.here_ref, bf16[4,1344,128]{2,1,0:T(8,128)(2,1)S(1)} %bitcast.21, bf16[4,1344,128]{2,1,0:T(8,128)(2,1)S(1)} %collective-permute-done.11.other_ref, bf16[256,512]{1,0:T(8,128)(2,1)S(1)} %get-tuple-element.34.xs_ref, bf16[1024,512]{1,0:T(8,128)(2,1)S(1)} %copy-done.5, ...), custom_call_target="tpu_custom_call" | custom-call | tf_op jit(solution)/shard_map/pallas_call | solution.py:573
  154.4 16.0 %all_to_all.42 = bf16[16,16,1152]{2,1,0:T(8,128)(2,1)} all-to-all(bf16[16,16,1152]{2,1,0:T(8,128)(2,1)S(1)} %shard_map.153), channel_id=1, replica_groups=mesh['a'=2,'b'=2,'x'=4,'z'=8,'core'=2] {'b','x','a'}, dimensions={0} | all-to-all | bytes 1179648 | tf_op jit(solution)/shard_map/all_to_all | solution.py:593
  170.4 4.1 %all-to-all-start.6 = ((bf16[16,16,1152]{2,1,0:T(8,128)(2,1)}), bf16[16,16,1152]{2,1,0:T(8,128)(2,1)S(1)}, u32[]{:S(2)}, u32[]{:S(2)}) async-start(bf16[16,16,1152]{2,1,0:T(8,128)(2,1)} %all_to_all.42), calls=%async_computation.6 | async-start | bytes 1179648 | tf_op jit(solution)/shard_map/all_to_all | solution.py:593
  174.7 17.0 %all-to-all-done.6 = bf16[16,16,1152]{2,1,0:T(8,128)(2,1)S(1)} async-done(((bf16[16,16,1152]{2,1,0:T(8,128)(2,1)}), bf16[16,16,1152]{2,1,0:T(8,128)(2,1)S(1)}, u32[]{:S(2)}, u32[]{:S(2)}) %all-to-all-start.6) | async-done | bytes 589856 | tf_op jit(solution)/shard_map/all_to_all | solution.py:593
  192.2 24.2 %all_to_all.43.owned_ref = bf16[16,16,1152]{2,1,0:T(8,128)(2,1)S(1)} all-to-all(bf16[16,16,1152]{2,1,0:T(8,128)(2,1)S(1)} %bitcast.30), channel_id=1, replica_groups=mesh['a'=2,'b'=2,'x'=4,'z'=8,'core'=2] {'z','core'}, dimensions={0} | all-to-all | bytes 1179648 | tf_op jit(solution)/shard_map/all_to_all | solution.py:593
  (59 shorter events, 19.5 us)
Async XLA Ops:
  0.6 31.6 %copy-start.12 = (s32[16]{0:T(128)S(1)}, s32[16]{0:T(128)}, u32[]{:S(2)}) copy-start(s32[16]{0:T(128)} %tenant_ref.3) | copy-start | bytes 196
  0.7 31.6 %copy-start.13 = (s32[16]{0:T(128)S(1)}, s32[16]{0:T(128)}, u32[]{:S(2)}) copy-start(s32[16]{0:T(128)} %slot_ref.1) | copy-start | bytes 196
  3.6 28.6 %all-to-all-start = ((bf16[16,16,1152]{2,1,0:T(8,128)(2,1)}), bf16[16,16,1152]{2,1,0:T(8,128)(2,1)S(1)}, u32[]{:S(2)}, u32[]{:S(2)}) async-start(bf16[16,16,1152]{2,1,0:T(8,128)(2,1)} %get-tuple-element.22), calls=%async_computation | async-start | bytes 1179648 | tf_op jit(solution)/shard_map/all_to_all | solution.py:593
  13.6 9.3 %collective-permute-start = (bf16[4,64,512]{2,1,0:T(8,128)(2,1)}, bf16[4,64,512]{2,1,0:T(8,128)(2,1)S(1)}, u32[]{:S(2)}, u32[]{:S(2)}) collective-permute-start(bf16[4,64,512]{2,1,0:T(8,128)(2,1)} %get-tuple-element.24), channel_id=1, source_target_pairs={{0,64},{64,128},{128,192},{192,0},{1,65},{65,129},{129,193},{193,1... | collective-permute-start | bytes 786440 | tf_op jit(solution)/shard_map/ppermute | solution.py:644
  14.9 14.7 %collective-permute-start.1 = (bf16[4,64,512]{2,1,0:T(8,128)(2,1)}, bf16[4,64,512]{2,1,0:T(8,128)(2,1)S(1)}, u32[]{:S(2)}, u32[]{:S(2)}) collective-permute-start(bf16[4,64,512]{2,1,0:T(8,128)(2,1)} %get-tuple-element.25), channel_id=1, source_target_pairs={{0,128},{64,192},{128,0},{192,64},{1,129},{65,193},{129,1},{193,65... | collective-permute-start | bytes 786440 | tf_op jit(solution)/shard_map/ppermute | solution.py:644
  17.5 12.1 %collective-permute-start.2 = (bf16[4,64,512]{2,1,0:T(8,128)(2,1)}, bf16[4,64,512]{2,1,0:T(8,128)(2,1)S(1)}, u32[]{:S(2)}, u32[]{:S(2)}) collective-permute-start(bf16[4,64,512]{2,1,0:T(8,128)(2,1)} %get-tuple-element.26), channel_id=1, source_target_pairs={{0,192},{64,0},{128,64},{192,128},{1,193},{65,1},{129,65},{193,129... | collective-permute-start | bytes 786440 | tf_op jit(solution)/shard_map/ppermute | solution.py:644
  33.2 23.7 %copy-start.14 = (s32[16]{0:T(128)S(1)}, s32[16]{0:T(128)}, u32[]{:S(2)}) copy-start(s32[16]{0:T(128)} %valid_ref.1) | copy-start | bytes 196
  35.0 31.2 %copy-start.2 = (bf16[4,64,512]{2,1,0:T(8,128)(2,1)}, bf16[4,64,512]{2,1,0:T(8,128)(2,1)S(1)}, u32[]{:S(2)}) copy-start(bf16[4,64,512]{2,1,0:T(8,128)(2,1)S(1)} %get-tuple-element.27.refs_0_) | copy-start | bytes 786436
  35.1 21.9 %all-to-all-start.1 = ((bf16[16,16,1152]{2,1,0:T(8,128)(2,1)}), bf16[16,16,1152]{2,1,0:T(8,128)(2,1)S(1)}, u32[]{:S(2)}, u32[]{:S(2)}) async-start(bf16[16,16,1152]{2,1,0:T(8,128)(2,1)} %get-tuple-element.31), calls=%async_computation.1 | async-start | bytes 1179648 | tf_op jit(solution)/shard_map/all_to_all | solution.py:593
  38.8 8.5 %collective-permute-start.3 = (bf16[4,64,512]{2,1,0:T(8,128)(2,1)S(1)}, bf16[4,64,512]{2,1,0:T(8,128)(2,1)S(1)}, u32[]{:S(2)}, u32[]{:S(2)}) collective-permute-start(bf16[4,64,512]{2,1,0:T(8,128)(2,1)S(1)} %get-tuple-element.28), channel_id=1, source_target_pairs={{0,16},{16,32},{32,48},{48,0},{1,17},{17,33},{33,49},{49,1},{2,18}... | collective-permute-start | bytes 786440 | tf_op jit(solution)/shard_map/ppermute | solution.py:649
  40.0 12.9 %collective-permute-start.4 = (bf16[4,64,512]{2,1,0:T(8,128)(2,1)S(1)}, bf16[4,64,512]{2,1,0:T(8,128)(2,1)S(1)}, u32[]{:S(2)}, u32[]{:S(2)}) collective-permute-start(bf16[4,64,512]{2,1,0:T(8,128)(2,1)S(1)} %get-tuple-element.29), channel_id=1, source_target_pairs={{0,32},{16,48},{32,0},{48,16},{1,33},{17,49},{33,1},{49,17},{2,34}... | collective-permute-start | bytes 786440 | tf_op jit(solution)/shard_map/ppermute | solution.py:649
  42.5 10.5 %collective-permute-start.5 = (bf16[4,64,512]{2,1,0:T(8,128)(2,1)S(1)}, bf16[4,64,512]{2,1,0:T(8,128)(2,1)S(1)}, u32[]{:S(2)}, u32[]{:S(2)}) collective-permute-start(bf16[4,64,512]{2,1,0:T(8,128)(2,1)S(1)} %get-tuple-element.30), channel_id=1, source_target_pairs={{0,48},{16,0},{32,16},{48,32},{1,49},{17,1},{33,17},{49,33},{2,50}... | collective-permute-start | bytes 786440 | tf_op jit(solution)/shard_map/ppermute | solution.py:649
  43.6 3.3 %collective-permute-start.8 = (bf16[8,8192]{1,0:T(8,128)(2,1)S(1)}, bf16[8,8192]{1,0:T(8,128)(2,1)S(1)}, u32[]{:S(2)}, u32[]{:S(2)}) collective-permute-start(bf16[8,8192]{1,0:T(8,128)(2,1)S(1)} %bitcast.22), channel_id=1, source_target_pairs={{0,1},{1,0},{2,3},{3,2},{4,5},{5,4},{6,7},{7,6},{8,9},{9,8},{10,11... | collective-permute-start | bytes 393224 | tf_op jit(solution)/shard_map/ppermute | solution.py:659
  45.9 1.3 collective-permute-start.9
  53.0 13.4 %copy-start = (bf16[4,64,512]{2,1,0:T(8,128)(2,1)}, bf16[4,64,512]{2,1,0:T(8,128)(2,1)S(1)}, u32[]{:S(2)}) copy-start(bf16[4,64,512]{2,1,0:T(8,128)(2,1)S(1)} %collective-permute-done.5.refs_3_.refs_2_) | copy-start | bytes 786436
  58.5 23.8 %all-to-all-start.2 = ((bf16[16,16,1664]{2,1,0:T(8,128)(2,1)}), bf16[16,16,1664]{2,1,0:T(8,128)(2,1)S(1)}, u32[]{:S(2)}, u32[]{:S(2)}) async-start(bf16[16,16,1664]{2,1,0:T(8,128)(2,1)} %shard_map.150), calls=%async_computation.2 | async-start | bytes 1703936 | tf_op jit(solution)/shard_map/all_to_all | solution.py:593
  66.3 14.0 %collective-permute-start.6 = (bf16[8,64,512]{2,1,0:T(8,128)(2,1)S(1)}, bf16[8,64,512]{2,1,0:T(8,128)(2,1)S(1)}, u32[]{:S(2)}, u32[]{:S(2)}) collective-permute-start(bf16[8,64,512]{2,1,0:T(8,128)(2,1)S(1)} %pad_maximum_fusion), channel_id=1, source_target_pairs={{0,2},{2,4},{4,6},{6,8},{8,10},{10,12},{12,14},{14,0},{1,3},{3,5},... | collective-permute-start | bytes 1572872 | tf_op jit(solution)/shard_map/ppermute | solution.py:667
  66.4 13.8 %collective-permute-start.7 = (bf16[8,64,512]{2,1,0:T(8,128)(2,1)S(1)}, bf16[8,64,512]{2,1,0:T(8,128)(2,1)S(1)}, u32[]{:S(2)}, u32[]{:S(2)}) collective-permute-start(bf16[8,64,512]{2,1,0:T(8,128)(2,1)S(1)} %pad_maximum_fusion.1), channel_id=1, source_target_pairs={{0,14},{2,0},{4,2},{6,4},{8,6},{10,8},{12,10},{14,12},{1,15},{3,1}... | collective-permute-start | bytes 1572872 | tf_op jit(solution)/shard_map/ppermute | solution.py:667
  84.8 4.5 %collective-permute-start.10 = (bf16[4,1344,128]{2,1,0:T(8,128)(2,1)S(1)}, bf16[4,1344,128]{2,1,0:T(8,128)(2,1)S(1)}, u32[]{:S(2)}, u32[]{:S(2)}) collective-permute-start(bf16[4,1344,128]{2,1,0:T(8,128)(2,1)S(1)} %get-tuple-element.35), channel_id=1, source_target_pairs={{0,1},{1,0},{2,3},{3,2},{4,5},{5,4},{6,7},{7,6},{8,9},{9,8},{10,11... | collective-permute-start | bytes 4128776 | tf_op jit(solution)/shard_map/ppermute | solution.py:678
  114.1 25.6 %copy-start.5 = (bf16[1024,512]{1,0:T(8,128)(2,1)S(1)}, bf16[1024,512]{1,0:T(8,128)(2,1)}, u32[]{:S(2)}) copy-start(bf16[1024,512]{1,0:T(8,128)(2,1)} %copy-done.4) | copy-start | bytes 3145732
  114.1 25.6 %copy-start.7 = (bf16[1024,512]{1,0:T(8,128)(2,1)S(1)}, bf16[1024,512]{1,0:T(8,128)(2,1)}, u32[]{:S(2)}) copy-start(bf16[1024,512]{1,0:T(8,128)(2,1)} %copy-done.6) | copy-start | bytes 3145732
  134.5 5.2 %collective-permute-start.11 = (bf16[4,1344,128]{2,1,0:T(8,128)(2,1)S(1)}, bf16[4,1344,128]{2,1,0:T(8,128)(2,1)S(1)}, u32[]{:S(2)}, u32[]{:S(2)}) collective-permute-start(bf16[4,1344,128]{2,1,0:T(8,128)(2,1)S(1)} %bitcast.20), channel_id=1, source_target_pairs={{0,1},{1,0},{2,3},{3,2},{4,5},{5,4},{6,7},{7,6},{8,9},{9,8},{10,11... | collective-permute-start | bytes 4128776 | tf_op jit(solution)/shard_map/ppermute | solution.py:684
  170.4 21.3 %all-to-all-start.6 = ((bf16[16,16,1152]{2,1,0:T(8,128)(2,1)}), bf16[16,16,1152]{2,1,0:T(8,128)(2,1)S(1)}, u32[]{:S(2)}, u32[]{:S(2)}) async-start(bf16[16,16,1152]{2,1,0:T(8,128)(2,1)} %all_to_all.42), calls=%async_computation.6 | async-start | bytes 1179648 | tf_op jit(solution)/shard_map/all_to_all | solution.py:593
  192.1 24.2 %copy-start.9 = (f32[1,8192]{1,0:T(1,128)S(1)}, f32[1,8192]{1,0:T(1,128)}, u32[]{:S(2)}) copy-start(f32[1,8192]{1,0:T(1,128)} %gain_ref.3) | copy-start | bytes 98308
  (7 other events, 32.4 us)
